TPU v7x, 256 devices: a whole 4x4x8 slice. The times are simulated.
256 devices in a mesh: grp: 2 (over core), row: 16 (over x_lo, z), col: 8 (over y, x_hi).
Axes of the slice: x: 4 (x_hi: 2, x_lo: 2; x = x_hi * 2 + x_lo), y: 4, z: 8, core: 2. Of those that a mesh axis runs over, the one named last changes fastest.
Arguments:
- occ_orbitals: float32 [32, 128, 128, 128], P(('grp', 'col'), 'row'), may hold values from -12 to 12
- vir_orbitals: float32 [256, 128, 128, 128], P(('grp', 'col'), 'row'), may hold values from -12 to 12
- xc_kernel: float32 [128, 128, 128], P('row'), may hold values from -8 to 0
- pairs: int32 [256, 2], P(('grp', 'col')), may hold values from 0 to 255, as said below
- batch_slot: int32 [16], replicated, may hold values from 0 to 15
Outputs:
- coupling: float32 [256, 16], P(('grp', 'col'))
Inputs may be any that keep to these rules, and one draw needn't show every extreme that they name: `pairs`: column 0 is an occupied orbital below 32 and column 1 a virtual orbital; the virtual orbitals of rows b * 16 to (b + 1) * 16 - 1 lie in b * 16 to (b + 1) * 16 - 1; no pair appears twice.
All inputs are finite; a program needn't handle non-finite values.
Results may differ from a plain program's by a relative error of at most 0.00005.
Values sent between devices are 32-bit elements; how exact they have to be, the bound alone decides.
No kernel may reach another device: no remote copies, remote signals or barrier semaphores. Data moves between devices by JAX's collectives and lax.ppermute only.
A program may use at most 128 MiB of HBM per device.

v0:
```python
import jax
import jax.numpy as jnp
from jax import lax
from jax.sharding import PartitionSpec as P

COULOMB = 0.4


def cas_table(length):
    indices = jnp.arange(length, dtype=jnp.int32)
    products = indices[:, None] * indices[None, :] % length
    angles = products.astype(jnp.float32) * (2.0 * jnp.pi / length)
    return jnp.cos(angles) + jnp.sin(angles)


def signed_square(frequency, length):
    signed = ((frequency + length // 2) % length - length // 2).astype(jnp.float32)
    return signed * signed


def hartree(density):
    planes, length, depth = density.shape
    cas_rows = cas_table(length)
    highest = lax.Precision.HIGHEST
    grid_field = jnp.dot(density, cas_rows, precision=highest)
    grid_field = jnp.einsum("xyz,yv->xvz", grid_field, cas_rows, precision=highest)
    columns = lax.all_to_all(grid_field, "row", split_axis=1, concat_axis=0, tiled=True)
    columns = jnp.einsum("xyz,xu->uyz", columns, cas_rows, precision=highest)
    y_width = columns.shape[1]
    frequency = jnp.arange(length, dtype=jnp.int32)
    local_y = lax.axis_index("row") * y_width + jnp.arange(y_width, dtype=jnp.int32)
    squared_sum = (
        signed_square(frequency, length)[:, None, None]
        + signed_square(local_y, length)[None, :, None]
        + signed_square(frequency, length)[None, None, :]
    )
    kernel = jnp.where(squared_sum > 0, COULOMB / jnp.maximum(squared_sum, 1.0), 0.0)
    columns = jnp.einsum("xyz,xu->uyz", columns * kernel, cas_rows, precision=highest)
    grid_field = lax.all_to_all(columns, "row", split_axis=0, concat_axis=1, tiled=True)
    grid_field = jnp.einsum("xyz,yv->xvz", grid_field, cas_rows, precision=highest)
    grid_field = jnp.dot(grid_field, cas_rows, precision=highest)
    return grid_field * (1.0 / float(length) ** 3)


def contract(left_rows, right_rows):
    return lax.dot_general(
        left_rows,
        right_rows,
        (((1,), (1,)), ((), ())),
        precision=lax.Precision.HIGHEST,
        preferred_element_type=jnp.float32,
    )


def on_device(occ_orbitals, vir_orbitals, xc_kernel, pairs, batch_slot):
    planes, size_y, size_z = xc_kernel.shape
    cell_count = planes * size_y * size_z
    scale = 1.0 / float(cell_count * lax.axis_size("row"))
    block_index = lax.axis_index(("grp", "col"))
    occ_flat = occ_orbitals.reshape(occ_orbitals.shape[0], cell_count)
    vir_flat = vir_orbitals.reshape(vir_orbitals.shape[0], cell_count)
    occ_index = pairs[:, 0]
    vir_index = pairs[:, 1] - block_index * vir_flat.shape[0]
    every_occ = lax.all_gather(occ_flat, ("grp", "col"), axis=0, tiled=True)
    densities = jnp.take(every_occ, occ_index, axis=0) * jnp.take(vir_flat, vir_index, axis=0)
    own_slot = jnp.take(batch_slot, block_index)
    own_density = lax.dynamic_index_in_dim(densities, own_slot, 0, keepdims=False).reshape(
        planes, size_y, size_z
    )
    potential = hartree(own_density) + xc_kernel * own_density
    partial_value = contract(
        lax.all_gather(potential.reshape(1, cell_count), ("grp", "col"), axis=0, tiled=True),
        densities,
    )
    partial_value = partial_value.T * scale
    return lax.psum(partial_value, "row")


def solution(mesh):
    return jax.shard_map(
        on_device,
        mesh=mesh,
        in_specs=(
            P(("grp", "col"), "row", None, None),
            P(("grp", "col"), "row", None, None),
            P("row", None, None),
            P(("grp", "col"), None),
            P(),
        ),
        out_specs=P(("grp", "col"), None),
        check_vma=False,
    )
```

profile of v0, /device:TPU:2, one launch (start us, length us, event | category | flops | bytes accessed | tf_op | source)
XLA Modules:
  0.0 377.7 jit_solution(15667185891987496810)
XLA Ops:
  6.5 0.0 all-gather.5.cloned.1.call-start
  6.5 3.0 reshape.174
  9.5 0.0 all-gather.5.cloned.1.call-update
  9.5 1.3 dynamic-slice.2
  11.4 0.0 copy-start.2
  11.4 8.2 %copy.53 = f32[2,8,1024,128]{3,1,2,0:T(8,128)S(1)} copy(f32[2,8,1024,128]{3,2,1,0:T(8,128)} %bitcast.60) | data formatting | bytes 16777216
  19.7 0.0 copy-done.2
  19.7 3.8 %fusion.61 = (f32[16,65536]{1,0:T(8,128)}, f32[16,65536]{1,0:T(8,128)}) fusion(f32[16,131072]{1,0:T(8,128)S(1)} %bitcast.59), kind=kLoop, calls=%fused_computation.90 | loop fusion | bytes 16777216 | tf_op jit(solution)/shard_map/jit(_take)/gather | solution.py:65
  23.5 8.0 %gather_fusion.3 = f32[16,65536]{1,0:T(8,128)} fusion(f32[16,65536]{1,0:T(8,128)} %get-tuple-element.21, s32[1024]{0:T(1024)S(1)} %pad_clamp_fusion), kind=kCustom, calls=%fused_computation.3 | custom fusion | bytes 8388672 | tf_op jit(solution)/shard_map/jit(_take)/gather | solution.py:65
  31.5 7.8 %gather_fusion.2 = f32[16,65536]{1,0:T(8,128)} fusion(f32[16,65536]{1,0:T(8,128)} %get-tuple-element.20, s32[1024]{0:T(1024)S(1)} %pad_clamp_fusion), kind=kCustom, calls=%fused_computation.2 | custom fusion | bytes 8388672 | tf_op jit(solution)/shard_map/jit(_take)/gather | solution.py:65
  39.4 87.1 %all-gather.5.cloned.1.call-done = f32[16,2,131072]{2,1,0:T(2,128)} async-done(((f32[1,2,131072]{2,1,0:T(2,128)}), f32[16,2,131072]{2,1,0:T(2,128)}) %all-gather.5.cloned.1.call-update) | async-done | bytes 16777232 | tf_op jit(solution)/shard_map/all_gather | solution.py:64
  126.5 16.7 %reshape.175 = f32[32,131072]{1,0:T(8,128)} reshape(f32[16,2,131072]{2,1,0:T(2,128)} %all-gather.5.cloned.1.call-done) | data formatting | bytes 33554432
  143.1 11.6 %fusion.60 = (f32[32,65536]{1,0:T(8,128)}, f32[32,65536]{1,0:T(8,128)}) fusion(f32[32,131072]{1,0:T(8,128)} %reshape.175), kind=kLoop, calls=%fused_computation.89 | loop fusion | bytes 33554432 | tf_op jit(solution)/shard_map/jit(_take)/gather | solution.py:65
  154.7 8.8 %gather_fusion.1 = f32[16,65536]{1,0:T(8,128)} fusion(f32[32,65536]{1,0:T(8,128)} %get-tuple-element.19, s32[1024]{0:T(1024)S(1)} %pad_clamp_fusion.1), kind=kCustom, calls=%fused_computation.1 | custom fusion | bytes 8388672 | tf_op jit(solution)/shard_map/jit(_take)/gather | solution.py:65
  163.5 8.8 %gather_fusion = f32[16,65536]{1,0:T(8,128)} fusion(f32[32,65536]{1,0:T(8,128)} %get-tuple-element.18, s32[1024]{0:T(1024)S(1)} %pad_clamp_fusion.1), kind=kCustom, calls=%fused_computation | custom fusion | bytes 8388672 | tf_op jit(solution)/shard_map/jit(_take)/gather | solution.py:65
  172.3 16.0 %fusion = f32[16,131072]{1,0:T(8,128)S(1)} fusion(f32[16,65536]{1,0:T(8,128)} %gather_fusion.1, f32[16,65536]{1,0:T(8,128)} %gather_fusion, f32[16,65536]{1,0:T(8,128)} %gather_fusion.3, f32[16,65536]{1,0:T(8,128)} %gather_fusion.2, pred[16]{0:T(512)(128)(4,1)S(1)} %get-tuple-element.16, pred[16]{0:T(512)(128)(4,1)S(1)} %get-tuple-element.22), kind=kLoop, calls=%fused_computation.6 | loop fusion | flops 10485760 | bytes 25165856 | tf_op jit(solution)/shard_map/mul | solution.py:65
  188.3 0.0 copy-start
  188.3 3.2 copy-done
  191.5 0.0 copy-start.1
  191.5 0.4 constant_dynamic-slice_fusion
  191.8 0.8 fusion.17
  192.7 0.9 convolution_bitcast_fusion.1
  193.6 1.1 copy.20
  194.7 8.5 %all-to-all-start = ((f32[8,128,128]{2,0,1:T(8,128)}), f32[8,128,128]{2,0,1:T(8,128)S(1)}, u32[]{:S(2)}, u32[]{:S(2)}) async-start(f32[8,128,128]{2,0,1:T(8,128)} %copy.20), calls=%async_computation | async-start | bytes 1048576 | tf_op jit(solution)/shard_map/all_to_all | solution.py:27
  203.2 0.0 all-gather.7.cloned.1.call-start
  203.3 0.1 broadcast_add_fusion
  203.4 14.8 %all-to-all-done = f32[8,128,128]{2,0,1:T(8,128)S(1)} async-done(((f32[8,128,128]{2,0,1:T(8,128)}), f32[8,128,128]{2,0,1:T(8,128)S(1)}, u32[]{:S(2)}, u32[]{:S(2)}) %all-to-all-start) | async-done | bytes 524320 | tf_op jit(solution)/shard_map/all_to_all | solution.py:27
  218.1 0.1 copy.22
  218.2 0.9 convolution_multiply_fusion.1
  219.2 0.9 fusion.21
  220.1 0.3 copy.26
  220.4 20.3 %all_to_all.36 = f32[128,8,128]{2,1,0:T(8,128)S(1)} all-to-all(f32[128,8,128]{2,1,0:T(8,128)S(1)} %copy.26), channel_id=1, replica_groups=mesh['grp'=2,'row'=16,'col'=8] {'row'}, dimensions={0} | all-to-all | bytes 1048576 | tf_op jit(solution)/shard_map/all_to_all | solution.py:39
  240.7 0.9 convolution_bitcast_fusion
  241.6 0.0 copy-done.1
  241.6 1.6 fusion.4
  243.2 0.0 all-gather.7.cloned.1.call-update
  243.2 73.7 %all-gather.7.cloned.1.call-done = f32[16,1,131072]{2,1,0:T(1,128)} async-done(((f32[1,1,131072]{2,1,0:T(1,128)}), f32[16,1,131072]{2,1,0:T(1,128)}) %all-gather.7.cloned.1.call-update) | async-done | bytes 8388624 | tf_op jit(solution)/shard_map/all_gather | solution.py:72
  316.9 17.9 %fusion.5 = f32[16,16]{1,0:T(8,128)S(1)} fusion(f32[16,131072]{1,0:T(8,128)} %copy-done, f32[16,1,131072]{2,1,0:T(1,128)} %all-gather.7.cloned.1.call-done), kind=kOutput, calls=%fused_computation.16 | convolution fusion | flops 402653440 | bytes 16778240 | tf_op jit(solution)/shard_map/dot_general | solution.py:46
  334.7 35.9 %psum.7 = f32[16,16]{1,0:T(8,128)} all-reduce(f32[16,16]{1,0:T(8,128)S(1)} %fusion.5), channel_id=1, replica_groups=mesh['grp'=2,'row'=16,'col'=8] {'row'}, use_global_device_ids=true, to_apply=%region_0.1 | all-reduce | flops 256 | bytes 2048 | tf_op jit(solution)/shard_map/psum | solution.py:76
  (6 shorter events, 0.1 us)
Async XLA Ops:
  6.5 119.9 %all-gather.5.cloned.1.call-start = ((), (), s32[]{:S(2)}) async-start(), calls=%async_computation.2 | async-start | bytes 17825792 | tf_op jit(solution)/shard_map/all_gather | solution.py:64
  11.4 8.3 %copy-start.2 = (s32[16,2]{0,1:T(2,128)S(1)}, s32[16,2]{0,1:T(2,128)}, u32[]{:S(2)}) copy-start(s32[16,2]{0,1:T(2,128)} %param.8) | copy-start | bytes 388
  188.3 3.2 copy-start
  191.5 50.1 %copy-start.1 = (f32[8,128,128]{2,1,0:T(8,128)S(1)}, f32[8,128,128]{2,1,0:T(8,128)}, u32[]{:S(2)}) copy-start(f32[8,128,128]{2,1,0:T(8,128)} %param.7) | copy-start | bytes 1572868
  194.7 23.4 %all-to-all-start = ((f32[8,128,128]{2,0,1:T(8,128)}), f32[8,128,128]{2,0,1:T(8,128)S(1)}, u32[]{:S(2)}, u32[]{:S(2)}) async-start(f32[8,128,128]{2,0,1:T(8,128)} %copy.20), calls=%async_computation | async-start | bytes 1048576 | tf_op jit(solution)/shard_map/all_to_all | solution.py:27
  203.2 113.7 %all-gather.7.cloned.1.call-start = ((), (), s32[]{:S(2)}) async-start(), calls=%async_computation.3 | async-start | bytes 8912896 | tf_op jit(solution)/shard_map/all_gather | solution.py:72
Sparse Core Ops, SparseCore 0:
  10.1 116.2 all-gather.4
  243.4 73.4 all-gather.6
where the time goes:
time: 382 us; the launch traced here: 378 us
  waiting for transfers between devices  176 us (46%)
  local copies, waits for them, and re-layouts  83 us (22%)
  blocking collectives  56.2 us (15%)
  matrix products  23.9 us (6%)
  other arithmetic  16.1 us (4%)
  between operations  14.4 us (4%)
  starting transfers between devices  8.53 us (2%)
    all_gather x1, waiting for transfers between devices, on_device(): every_occ = lax.all_gather(occ_flat, ('grp', 'col'), axis=0, tiled=True)  87.1 us
    all_gather x1, waiting for transfers between devices, on_device(): lax.all_gather(potential.reshape(1, cell_count), ('grp', 'col'), axis=0,...  73.7 us
    psum x1, blocking collectives, on_device(): return lax.psum(partial_value, 'row')  35.9 us
    unnamed x9, local copies, waits for them, and re-layouts  31.1 us
    gather x3, local copies, waits for them, and re-layouts, on_device(): jnp.take(every_occ, occ_index, axis=0)  29.2 us
    all_to_all x1, blocking collectives, hartree(): lax.all_to_all(columns, 'row', split_axis=0, concat_axis=1, tiled=True)  20.3 us
    gather x3, local copies, waits for them, and re-layouts, on_device(): jnp.take(vir_flat, vir_index, axis=0)  19.6 us
    dot_general x1, matrix products, contract(): lax.dot_general(left_rows, right_rows, (((1,), (1,)), ((), ())), precisio...  17.9 us
  transfers between devices with their start and end apart: 3, of which 3 were waited for; matrix products, arithmetic and copies ran while one was open for 8% of the time, Pallas kernels for 0%

commit v1 on v0

v1 whole, which is shorter than its diff:
```python
import jax
import jax.numpy as jnp
from jax import lax
from jax.experimental import pallas as pl
from jax.experimental.pallas import tpu as pltpu
from jax.sharding import PartitionSpec as P

COULOMB = 0.4
LANES = 128
BLOCK_AXES = ("grp", "col")
VMEM_BYTES = 48 * 1024 * 1024


def cas_table(length):
    indices = jnp.arange(length, dtype=jnp.int32)
    products = indices[:, None] * indices[None, :] % length
    angles = products.astype(jnp.float32) * (2.0 * jnp.pi / length)
    return jnp.cos(angles) + jnp.sin(angles)


def signed_square(frequency, length):
    signed = ((frequency + length // 2) % length - length // 2).astype(jnp.float32)
    return signed * signed


def hartree(density):
    planes, length, depth = density.shape
    cas_rows = cas_table(length)
    highest = lax.Precision.HIGHEST
    grid_field = jnp.dot(density, cas_rows, precision=highest)
    grid_field = jnp.einsum("xyz,yv->xvz", grid_field, cas_rows, precision=highest)
    columns = lax.all_to_all(grid_field, "row", split_axis=1, concat_axis=0, tiled=True)
    columns = jnp.einsum("xyz,xu->uyz", columns, cas_rows, precision=highest)
    y_width = columns.shape[1]
    frequency = jnp.arange(length, dtype=jnp.int32)
    local_y = lax.axis_index("row") * y_width + jnp.arange(y_width, dtype=jnp.int32)
    squared_sum = (
        signed_square(frequency, length)[:, None, None]
        + signed_square(local_y, length)[None, :, None]
        + signed_square(frequency, length)[None, None, :]
    )
    kernel = jnp.where(squared_sum > 0, COULOMB / jnp.maximum(squared_sum, 1.0), 0.0)
    columns = jnp.einsum("xyz,xu->uyz", columns * kernel, cas_rows, precision=highest)
    grid_field = lax.all_to_all(columns, "row", split_axis=0, concat_axis=1, tiled=True)
    grid_field = jnp.einsum("xyz,yv->xvz", grid_field, cas_rows, precision=highest)
    grid_field = jnp.dot(grid_field, cas_rows, precision=highest)
    return grid_field * (1.0 / float(length) ** 3)


RING_Y, RING_X = 4, 2


def shift_col(value, dy, dx):
    pairs = [
        (y * RING_X + x, (y + dy) % RING_Y * RING_X + (x + dx) % RING_X)
        for y in range(RING_Y)
        for x in range(RING_X)
    ]
    return lax.ppermute(value, "col", pairs)


OFFSETS = ((0, 0), (1, 0), (3, 0), (0, 1), (2, 0), (1, 1), (3, 1), (2, 1))


def spread(piece):
    half = piece.shape[0] // 2
    from_below = shift_col(piece, 1, 0)
    from_above = shift_col(piece, -1, 0)
    from_side = shift_col(piece, 0, 1)
    far_low = shift_col(from_below[:half], 1, 0)
    far_high = shift_col(from_above[half:], -1, 0)
    side_below = shift_col(from_side, 1, 0)
    side_above = shift_col(from_side, -1, 0)
    far = jnp.concatenate([far_low, far_high], axis=0)
    side_far = shift_col(far, 0, 1)
    return [piece, from_below, from_above, from_side, far, side_below, side_above, side_far]


def swap_core(value):
    return lax.ppermute(value, "grp", [(0, 1), (1, 0)])


def pick_kernel(index_ref, held_ref, out_ref):
    rows = out_ref.shape[1]
    for block in range(out_ref.shape[0]):
        index = index_ref[block]
        start = pl.multiple_of(index % 2 * rows, rows)
        out_ref[block] = held_ref[index // 2, pl.ds(start, rows), :]


def pick(held, index, rows):
    return pl.pallas_call(
        pick_kernel,
        out_shape=jax.ShapeDtypeStruct((index.shape[0], rows, LANES), jnp.float32),
        in_specs=[
            pl.BlockSpec(memory_space=pltpu.SMEM),
            pl.BlockSpec(memory_space=pltpu.VMEM),
        ],
        out_specs=pl.BlockSpec(memory_space=pltpu.VMEM),
        compiler_params=pltpu.CompilerParams(vmem_limit_bytes=VMEM_BYTES),
        name="pick_occ",
    )(index, held)


def density_kernel(occ_ref, vir_index_ref, place_ref, *refs):
    pieces, vir_ref, out_ref = refs[:8], refs[8], refs[9]
    index = occ_ref[pl.program_id(0)]
    rows = pieces[0].shape[1] // 2
    start = pl.multiple_of(index % 2 * rows, rows)
    for number, piece in enumerate(pieces):
        cells = pl.ds(pl.multiple_of(place_ref[number] * rows, rows), rows)
        out_ref[0, cells, :] = piece[index // 2, pl.ds(start, rows), :] * vir_ref[0, 0, cells, :]


def form_densities(occ_index, vir_index, place, pieces, vir):
    number = occ_index.shape[0]
    rows = vir.shape[2]
    whole = pl.BlockSpec(memory_space=pltpu.VMEM)
    return pl.pallas_call(
        density_kernel,
        grid_spec=pltpu.PrefetchScalarGridSpec(
            num_scalar_prefetch=3,
            grid=(number,),
            in_specs=[whole] * 8
            + [pl.BlockSpec((1, 1, rows, LANES), lambda p, occ, vir, place: (vir[p], place[8], 0, 0))],
            out_specs=pl.BlockSpec((1, rows, LANES), lambda p, occ, vir, place: (p, 0, 0)),
        ),
        out_shape=jax.ShapeDtypeStruct((number, rows, LANES), jnp.float32),
        compiler_params=pltpu.CompilerParams(vmem_limit_bytes=VMEM_BYTES),
        cost_estimate=pl.CostEstimate(
            flops=number * rows * LANES, bytes_accessed=16 * 1024 * 1024, transcendentals=0
        ),
        name="form_densities",
    )(occ_index, vir_index, place, *pieces, vir)


PAIR_GROUP = 4


def contract_kernel(own_ref, mate_ref, *refs):
    fields, out_ref, total = refs[:4], refs[4], refs[5]
    step = pl.program_id(0)
    rows = own_ref.shape[1]
    per_half = own_ref.shape[0]

    @pl.when(step == 0)
    def _():
        total[...] = jnp.zeros_like(total)

    for half, densities in enumerate((own_ref, mate_ref)):

        @pl.loop(0, per_half // PAIR_GROUP)
        def _(group):
            first = group * PAIR_GROUP
            sums = [None] * (PAIR_GROUP * 8)
            for tile in range(rows // 8):
                cells = pl.ds(tile * 8, 8)
                left = [densities[first + k, cells, :] for k in range(PAIR_GROUP)]
                right = [field[j, cells, :] for field in fields for j in range(2)]
                for k in range(PAIR_GROUP):
                    for b in range(8):
                        term = left[k] * right[b]
                        slot = k * 8 + b
                        sums[slot] = term if sums[slot] is None else sums[slot] + term
            base = (half * per_half + first) * 8
            for slot, value in enumerate(sums):
                total[base + slot] += value

    @pl.when(step == pl.num_programs(0) - 1)
    def _():
        lanes = jnp.sum(total[...], axis=1)
        out_ref[...] = lax.dot_general(
            jnp.ones((8, LANES), jnp.float32),
            lanes,
            (((1,), (1,)), ((), ())),
            precision=lax.Precision.HIGHEST,
            preferred_element_type=jnp.float32,
        )


def contract(own, mate, fields):
    pairs, rows, _ = own.shape
    tile = 64
    return pl.pallas_call(
        contract_kernel,
        grid=(rows // tile,),
        in_specs=[pl.BlockSpec((pairs, tile, LANES), lambda i: (0, i, 0))] * 2
        + [pl.BlockSpec((2, tile, LANES), lambda i: (0, i, 0))] * 4,
        out_specs=pl.BlockSpec((8, 2 * pairs * 8), lambda i: (0, 0)),
        out_shape=jax.ShapeDtypeStruct((8, 2 * pairs * 8), jnp.float32),
        scratch_shapes=[pltpu.VMEM((2 * pairs * 8, 8, LANES), jnp.float32)],
        compiler_params=pltpu.CompilerParams(vmem_limit_bytes=VMEM_BYTES),
        cost_estimate=pl.CostEstimate(
            flops=2 * 16 * pairs * rows * LANES, bytes_accessed=12 * 1024 * 1024, transcendentals=0
        ),
        name="contract",
    )(own, mate, *fields)


def on_device(occ_orbitals, vir_orbitals, xc_kernel, pairs, batch_slot):
    planes, size_y, size_z = xc_kernel.shape
    cell_count = planes * size_y * size_z
    row_count = lax.axis_size("row")
    scale = 1.0 / float(cell_count * row_count)
    grp = lax.axis_index("grp")
    col = lax.axis_index("col")
    blocks = lax.axis_size(BLOCK_AXES)
    block_index = grp * lax.axis_size("col") + col
    occ_local, vir_local = occ_orbitals.shape[0], vir_orbitals.shape[0]
    chunk_rows = cell_count // blocks // LANES
    half_rows = cell_count // 2 // LANES

    mate_pairs = swap_core(pairs)
    vir_halves = vir_orbitals.reshape(vir_local, 2, half_rows, LANES)
    mate_vir = swap_core(lax.dynamic_index_in_dim(vir_halves, 1 - grp, 1, keepdims=True))

    own_slot = jnp.take(batch_slot, block_index)
    own_pair = lax.dynamic_index_in_dim(pairs, own_slot, 0, keepdims=False)
    wanted = own_pair[0].astype(jnp.float32)
    chunks = occ_orbitals.reshape(occ_local, blocks, chunk_rows, LANES)
    chunks = chunks.transpose(1, 0, 2, 3).reshape(blocks, occ_local * chunk_rows, LANES)
    note = jnp.full((blocks, 8, LANES), wanted, jnp.float32)
    held = lax.all_to_all(
        jnp.concatenate([chunks, note], axis=1), BLOCK_AXES, 0, 0, tiled=True
    )
    wanted_all = held[:, occ_local * chunk_rows, 0].astype(jnp.int32)
    picked = pick(held, wanted_all, chunk_rows)
    own_occ = lax.all_to_all(picked, BLOCK_AXES, 0, 0, tiled=True)
    own_vir = lax.dynamic_index_in_dim(
        vir_orbitals, own_pair[1] - block_index * vir_local, 0, keepdims=False
    )
    sigma = own_occ.reshape(planes, size_y, size_z) * own_vir

    occ_pieces = spread(held[:, : occ_local * chunk_rows])

    potential = hartree(sigma) + xc_kernel * sigma
    halves = potential.reshape(2, half_rows, LANES)
    kept = lax.dynamic_index_in_dim(halves, grp, 0, keepdims=True)
    moved = swap_core(lax.dynamic_index_in_dim(halves, 1 - grp, 0, keepdims=True))
    fields = spread(jnp.concatenate([kept, moved], axis=0))

    own_y, own_x = col // RING_X, col % RING_X
    places = [
        (own_y + RING_Y - dy) % RING_Y * RING_X + (own_x + RING_X - dx) % RING_X
        for dy, dx in OFFSETS
    ]
    place = jnp.stack(places).astype(jnp.int32)
    zero = jnp.zeros((1,), jnp.int32)
    mate_block = (1 - grp) * lax.axis_size("col") + col
    own = form_densities(
        pairs[:, 0],
        pairs[:, 1] - block_index * vir_local,
        jnp.concatenate([place, zero + grp]),
        occ_pieces,
        vir_halves,
    )
    mate = form_densities(
        mate_pairs[:, 0],
        mate_pairs[:, 1] - mate_block * vir_local,
        jnp.concatenate([place, zero]),
        occ_pieces,
        mate_vir,
    )
    near = contract(own, mate, fields[:4])
    far = contract(own, mate, fields[4:])

    pair_count = pairs.shape[0]
    sums = jnp.stack([near[0], far[0]]).reshape(2, 2, pair_count * 8)
    sums = sums.transpose(1, 0, 2)
    sums = jnp.where(grp == 0, sums, sums[::-1])
    sent = jnp.broadcast_to(sums[:, None], (2, row_count, 2, pair_count * 8))
    got = lax.all_to_all(
        sent.reshape(2 * row_count, 2, pair_count * 8), ("grp", "row"), 0, 0, tiled=True
    )
    got = jnp.sum(got.reshape(2, row_count, 2, pair_count, 4, 2), axis=1)
    got = got[0] + got[1][..., ::-1]
    got = got.transpose(1, 3, 0, 2).reshape(pair_count, 2, 8)
    chosen = place[:, None] == jnp.arange(8, dtype=jnp.int32)[None, :]
    ordered = jnp.sum(jnp.where(chosen, got[:, :, :, None], 0.0), axis=2)
    return ordered.reshape(pair_count, blocks) * scale


def solution(mesh):
    return jax.shard_map(
        on_device,
        mesh=mesh,
        in_specs=(
            P(BLOCK_AXES, "row", None, None),
            P(BLOCK_AXES, "row", None, None),
            P("row", None, None),
            P(BLOCK_AXES, None),
            P(),
        ),
        out_specs=P(BLOCK_AXES, None),
        check_vma=False,
    )
```

time: 382 us -> 273 us (0.71)
  local copies, waits for them, and re-layouts: 83 us -> 17.6 us
  waiting for transfers between devices: 176 us -> 117 us
  starting transfers between devices: 8.53 us -> 54.1 us
  Pallas kernels: 0 us -> 44.3 us
  blocking collectives: 56.2 us -> 24.8 us
  matrix products: 23.9 us -> 7.52 us
  other arithmetic: 16.1 us -> 1.86 us
  between operations: 14.4 us -> 2.14 us
    all_gather x2 -> x0, waiting for transfers between devices: 161 us -> none  [the longest x1 87.1 us: on_device(): every_occ = lax.all_gather(occ_flat, ('grp', 'col'), axis=0, tiled=True)]
    ppermute x0 -> x19, waiting for transfers between devices: none -> 82.8 us  [the longest x16 82 us: shift_col(): return lax.ppermute(value, 'col', pairs)]
    gather x6 -> x0, local copies, waits for them, and re-layouts: 48.8 us -> none  [the longest x3 29.2 us: on_device(): jnp.take(every_occ, occ_index, axis=0)]
    pallas_call x0 -> x5, Pallas kernels: none -> 44.3 us  [the longest x2 25.1 us: form_densities(): pl.pallas_call(density_kernel, grid_spec=pltpu.PrefetchScalarGridSpec(num...]
    psum x1 -> x0, blocking collectives: 35.9 us -> none  [on_device(): return lax.psum(partial_value, 'row')]
    unnamed x9 -> x21, local copies, waits for them, and re-layouts: 31.1 us -> 2.73 us
    ppermute x0 -> x19, starting transfers between devices: none -> 26.4 us  [the longest x16 26.3 us: shift_col(): return lax.ppermute(value, 'col', pairs)]
    all_to_all x0 -> x3, waiting for transfers between devices: none -> 25.9 us  [the longest x1 11.1 us: on_device(): own_occ = lax.all_to_all(picked, BLOCK_AXES, 0, 0, tiled=True)]
  transfers between devices with their start and end apart: 3 -> 23, of which waited for: 3 -> 11; matrix products, arithmetic and copies ran while one was open for 8% -> 6% of each run, Pallas kernels for 0% -> 13%
where the time goes in v1:
time: 273 us; the launch traced here: 270 us
  waiting for transfers between devices  117 us (43%)
  starting transfers between devices  54.1 us (20%)
  Pallas kernels  44.3 us (16%)
  blocking collectives  24.8 us (9%)
  local copies, waits for them, and re-layouts  17.6 us (6%)
  matrix products  7.52 us (3%)
    ppermute x16, waiting for transfers between devices, shift_col(): return lax.ppermute(value, 'col', pairs)  82 us
    ppermute x16, starting transfers between devices, shift_col(): return lax.ppermute(value, 'col', pairs)  26.3 us
    pallas_call x2, Pallas kernels, form_densities(): pl.pallas_call(density_kernel, grid_spec=pltpu.PrefetchScalarGridSpec(num...  25.1 us
    all_to_all x1, blocking collectives, on_device(): lax.all_to_all(jnp.concatenate([chunks, note], axis=1), BLOCK_AXES, 0, 0,...  24.8 us
    pallas_call x2, Pallas kernels, contract(): pl.pallas_call(contract_kernel, grid=(rows // tile,), in_specs=[pl.BlockS...  17.7 us
    all_to_all x1, waiting for transfers between devices, on_device(): own_occ = lax.all_to_all(picked, BLOCK_AXES, 0, 0, tiled=True)  11.1 us
    all_to_all x1, starting transfers between devices, hartree(): lax.all_to_all(grid_field, 'row', split_axis=1, concat_axis=0, tiled=True)  9.94 us
    all_to_all x1, waiting for transfers between devices, hartree(): lax.all_to_all(grid_field, 'row', split_axis=1, concat_axis=0, tiled=True)  8.67 us
  transfers between devices with their start and end apart: 23, of which 11 were waited for; matrix products, arithmetic and copies ran while one was open for 6% of the time, Pallas kernels for 13%

profile of v1, /device:TPU:2, one launch (start us, length us, event | category | flops | bytes accessed | tf_op | source)
XLA Modules:
  0.0 269.8 jit_solution(6069127537374774784)
XLA Ops:
  0.0 1.3 dynamic-slice.2
  2.0 0.8 constant_dynamic-slice_fusion.3
  2.7 0.5 fusion.55
  3.8 1.3 copy.79
  5.2 24.8 %all_to_all.51.held_ref = f32[16,136,128]{2,1,0:T(8,128)S(1)} all-to-all(f32[16,136,128]{2,1,0:T(8,128)S(1)} %concatenate.21), channel_id=1, replica_groups=mesh['grp'=2,'row'=16,'col'=8] {'grp','col'}, dimensions={0} | all-to-all | bytes 2228224 | tf_op jit(solution)/shard_map/all_to_all | solution.py:223
  30.1 0.4 fusion.20.index_ref
  30.4 1.5 pick_occ.1
  31.9 3.6 %all-to-all-start.1 = ((f32[16,64,128]{2,1,0:T(8,128)}), f32[16,64,128]{2,1,0:T(8,128)S(1)}, u32[]{:S(2)}, u32[]{:S(2)}) async-start(f32[16,64,128]{2,1,0:T(8,128)} %pick_occ.1), calls=%async_computation.1 | async-start | bytes 1048576 | tf_op jit(solution)/shard_map/all_to_all | solution.py:228
  36.0 11.1 %all-to-all-done.1 = f32[16,64,128]{2,1,0:T(8,128)S(1)} async-done(((f32[16,64,128]{2,1,0:T(8,128)}), f32[16,64,128]{2,1,0:T(8,128)S(1)}, u32[]{:S(2)}, u32[]{:S(2)}) %all-to-all-start.1) | async-done | bytes 524320 | tf_op jit(solution)/shard_map/all_to_all | solution.py:228
  47.1 1.1 bitcast_multiply_fusion
  48.2 0.8 fusion.10
  49.1 0.9 convolution_bitcast_fusion.1
  50.0 1.1 copy.81
  51.1 9.9 %all-to-all-start.2 = ((f32[8,128,128]{2,0,1:T(8,128)}), f32[8,128,128]{2,0,1:T(8,128)S(1)}, u32[]{:S(2)}, u32[]{:S(2)}) async-start(f32[8,128,128]{2,0,1:T(8,128)} %copy.81), calls=%async_computation.2 | async-start | bytes 1048576 | tf_op jit(solution)/shard_map/all_to_all | solution.py:32
  61.0 4.6 %constant_dynamic-slice_fusion.2 = f32[16,1,512,128]{3,2,1,0:T(8,128)} fusion(f32[16,2,512,128]{3,2,1,0:T(8,128)} %bitcast.83, s32[]{:T(128)S(6)} %select_n.152), kind=kLoop, calls=%fused_computation.61 | loop fusion | bytes 8388612 | tf_op jit(solution)/shard_map/jit(dynamic_index_in_dim)/dynamic_slice | solution.py:215
  65.7 8.7 %all-to-all-done.2 = f32[8,128,128]{2,0,1:T(8,128)S(1)} async-done(((f32[8,128,128]{2,0,1:T(8,128)}), f32[8,128,128]{2,0,1:T(8,128)S(1)}, u32[]{:S(2)}, u32[]{:S(2)}) %all-to-all-start.2) | async-done | bytes 524320 | tf_op jit(solution)/shard_map/all_to_all | solution.py:32
  74.4 0.1 copy.83
  74.5 0.9 convolution_multiply_fusion.1
  75.4 0.9 fusion.14
  76.4 1.1 copy.87
  77.4 6.0 %all-to-all-start.3 = ((f32[128,8,128]{2,1,0:T(8,128)}), f32[128,8,128]{2,1,0:T(8,128)}, u32[]{:S(2)}, u32[]{:S(2)}) async-start(f32[128,8,128]{2,1,0:T(8,128)} %copy.87), calls=%async_computation.3 | async-start | bytes 1048576 | tf_op jit(solution)/shard_map/all_to_all | solution.py:44
  83.4 0.1 slice.71.refs_0_
  83.5 0.7 collective-permute-start
  84.2 2.6 collective-permute-start.1
  86.8 2.3 collective-permute-start.2
  89.1 7.6 %all-to-all-done.3 = f32[128,8,128]{2,1,0:T(8,128)} async-done(((f32[128,8,128]{2,1,0:T(8,128)}), f32[128,8,128]{2,1,0:T(8,128)}, u32[]{:S(2)}, u32[]{:S(2)}) %all-to-all-start.3) | async-done | bytes 524320 | tf_op jit(solution)/shard_map/all_to_all | solution.py:44
  96.8 1.9 convolution_bitcast_fusion
  98.7 2.1 fusion
  100.8 0.1 collective-permute-start.10
  100.9 7.0 %collective-permute-done.refs_1_ = f32[16,128,128]{2,1,0:T(8,128)S(1)} collective-permute-done((f32[16,128,128]{2,1,0:T(8,128)S(1)}, f32[16,128,128]{2,1,0:T(8,128)S(1)}, u32[]{:S(2)}, u32[]{:S(2)}) %collective-permute-start) | collective-permute-done | bytes 1048608 | tf_op jit(solution)/shard_map/ppermute | solution.py:59
  108.0 0.3 collective-permute-start.3
  108.3 0.8 collective-permute-done.8
  109.1 3.2 %collective-permute-start.12 = (f32[2,512,128]{2,1,0:T(8,128)S(1)}, f32[2,512,128]{2,1,0:T(8,128)S(1)}, u32[]{:S(2)}, u32[]{:S(2)}) collective-permute-start(f32[2,512,128]{2,1,0:T(8,128)S(1)} %pad_maximum_fusion.refs_0_), channel_id=1, source_target_pairs={{0,6},{1,7},{2,0},{3,1},{4,2},{5,3},{6,4},{7,5},{8,14},{9,15},{10,... | collective-permute-start | bytes 1572872 | tf_op jit(solution)/shard_map/ppermute | solution.py:59
  112.4 3.3 %collective-permute-done.2.refs_3_ = f32[16,128,128]{2,1,0:T(8,128)} collective-permute-done((f32[16,128,128]{2,1,0:T(8,128)S(1)}, f32[16,128,128]{2,1,0:T(8,128)}, u32[]{:S(2)}, u32[]{:S(2)}) %collective-permute-start.2) | collective-permute-done | bytes 1048608 | tf_op jit(solution)/shard_map/ppermute | solution.py:59
  115.7 1.0 collective-permute-start.4
  116.7 7.5 %collective-permute-done.3 = f32[8,128,128]{2,1,0:T(8,128)S(1)} collective-permute-done((f32[8,128,128]{2,1,0:T(8,128)S(1)}, f32[8,128,128]{2,1,0:T(8,128)S(1)}, u32[]{:S(2)}, u32[]{:S(2)}) %collective-permute-start.3) | collective-permute-done | bytes 524320 | tf_op jit(solution)/shard_map/ppermute | solution.py:59
  124.2 11.2 %collective-permute-done.11.refs_1_ = f32[2,512,128]{2,1,0:T(8,128)S(1)} collective-permute-done((f32[2,512,128]{2,1,0:T(8,128)S(1)}, f32[2,512,128]{2,1,0:T(8,128)S(1)}, u32[]{:S(2)}, u32[]{:S(2)}) %collective-permute-start.11) | collective-permute-done | bytes 524320 | tf_op jit(solution)/shard_map/ppermute | solution.py:59
  135.4 0.2 collective-permute-start.6
  135.7 1.9 collective-permute-start.14
  137.6 1.5 collective-permute-start.15
  139.1 0.8 constant_dynamic-update-slice_fusion.1
  140.0 0.9 constant_dynamic-update-slice_fusion.refs_4_
  140.8 22.3 %collective-permute-done.14 = f32[1,512,128]{2,1,0:T(8,128)S(1)} collective-permute-done((f32[1,512,128]{2,1,0:T(8,128)S(1)}, f32[1,512,128]{2,1,0:T(8,128)S(1)}, u32[]{:S(2)}, u32[]{:S(2)}) %collective-permute-start.14) | collective-permute-done | bytes 262176 | tf_op jit(solution)/shard_map/ppermute | solution.py:59
  163.1 3.5 %collective-permute-start.7 = (f32[16,128,128]{2,1,0:T(8,128)}, f32[16,128,128]{2,1,0:T(8,128)}, u32[]{:S(2)}, u32[]{:S(2)}) collective-permute-start(f32[16,128,128]{2,1,0:T(8,128)} %constant_dynamic-update-slice_fusion.refs_4_), channel_id=1, source_target_pairs={{0,1},{1,0},{2,3},{3,2},{4,5},{5,4},{6,7},{7,6},{8,9},{9,8},{10,11... | collective-permute-start | bytes 3145736 | tf_op jit(solution)/shard_map/ppermute | solution.py:59
  166.7 2.5 collective-permute-start.13
  169.2 0.7 constant_dynamic-update-slice_fusion.3
  169.9 0.7 constant_dynamic-update-slice_fusion.2.refs_0_
  170.7 30.6 %collective-permute-done.13.refs_3_ = f32[2,512,128]{2,1,0:T(8,128)} collective-permute-done((f32[2,512,128]{2,1,0:T(8,128)S(1)}, f32[2,512,128]{2,1,0:T(8,128)}, u32[]{:S(2)}, u32[]{:S(2)}) %collective-permute-start.13) | collective-permute-done | bytes 524320 | tf_op jit(solution)/shard_map/ppermute | solution.py:59
  201.3 1.0 copy-done.7
  202.3 3.2 %collective-permute-start.17 = (f32[2,512,128]{2,1,0:T(8,128)}, f32[2,512,128]{2,1,0:T(8,128)}, u32[]{:S(2)}, u32[]{:S(2)}) collective-permute-start(f32[2,512,128]{2,1,0:T(8,128)} %collective-permute-done.13.refs_3_), channel_id=1, source_target_pairs={{0,6},{1,7},{2,0},{3,1},{4,2},{5,3},{6,4},{7,5},{8,14},{9,15},{10,... | collective-permute-start | bytes 1572872 | tf_op jit(solution)/shard_map/ppermute | solution.py:59
  205.5 3.2 %collective-permute-start.18 = (f32[2,512,128]{2,1,0:T(8,128)}, f32[2,512,128]{2,1,0:T(8,128)}, u32[]{:S(2)}, u32[]{:S(2)}) collective-permute-start(f32[2,512,128]{2,1,0:T(8,128)} %constant_dynamic-update-slice_fusion.2.refs_0_), channel_id=1, source_target_pairs={{0,1},{1,0},{2,3},{3,2},{4,5},{5,4},{6,7},{7,6},{8,9},{9,8},{10,11... | collective-permute-start | bytes 1572872 | tf_op jit(solution)/shard_map/ppermute | solution.py:59
  209.0 12.5 %form_densities.2.own_ref = f32[16,512,128]{2,1,0:T(8,128)} custom-call(s32[16]{0:T(128)S(1)} %get-tuple-element.25.occ_ref, s32[16]{0:T(128)S(1)} %get-tuple-element.24.vir_index_ref, s32[9]{0:T(128)S(1)} %concatenate.20.place_ref, f32[16,128,128]{2,1,0:T(8,128)S(1)} %slice.71.refs_0_, f32[16,128,128]{2,1,0:T(8,128)S(1)} %collective-permute-done.refs_1_, ...), custom_call_target="tpu_custom_call" | custom-call | flops 1048576 | bytes 16777216 | tf_op jit(solution)/shard_map/form_densities/pallas_call | solution.py:119
  221.6 12.6 %form_densities.3.mate_ref = f32[16,512,128]{2,1,0:T(8,128)} custom-call(s32[16]{0:T(128)S(1)} %get-tuple-element.23.occ_ref, s32[16]{0:T(128)S(1)} %get-tuple-element.22.vir_index_ref, s32[9]{0:T(128)S(1)} %concatenate.23.place_ref, f32[16,128,128]{2,1,0:T(8,128)S(1)} %slice.71.refs_0_, f32[16,128,128]{2,1,0:T(8,128)S(1)} %collective-permute-done.refs_1_, ...), custom_call_target="tpu_custom_call" | custom-call | flops 1048576 | bytes 16777216 | tf_op jit(solution)/shard_map/form_densities/pallas_call | solution.py:119
  234.2 8.8 %contract.2 = f32[8,256]{1,0:T(8,128)S(1)} custom-call(f32[16,512,128]{2,1,0:T(8,128)} %form_densities.2.own_ref, f32[16,512,128]{2,1,0:T(8,128)} %form_densities.3.mate_ref, f32[2,512,128]{2,1,0:T(8,128)S(1)} %copy-done.1, f32[2,512,128]{2,1,0:T(8,128)S(1)} %copy-done.3, f32[2,512,128]{2,1,0:T(8,128)S(1)} %copy-done.5, ...), custom_call_target="tpu_custom_call" | custom-call | flops 33554432 | bytes 12582912 | tf_op jit(solution)/shard_map/contract/pallas_call | solution.py:184
  243.1 8.9 %contract.3 = f32[8,256]{1,0:T(8,128)S(1)} custom-call(f32[16,512,128]{2,1,0:T(8,128)} %form_densities.2.own_ref, f32[16,512,128]{2,1,0:T(8,128)} %form_densities.3.mate_ref, f32[2,512,128]{2,1,0:T(8,128)} %constant_dynamic-update-slice_fusion.2.refs_0_, f32[2,512,128]{2,1,0:T(8,128)} %collective-permute-done.16.refs_1_, ...), custom_call_target="tpu_custom_call" | custom-call | flops 33554432 | bytes 12582912 | tf_op jit(solution)/shard_map/contract/pallas_call | solution.py:184
  252.1 0.6 copy.90
  252.7 8.3 %all-to-all-start.4 = ((f32[32,2,128]{2,1,0:T(2,128)}), f32[32,2,128]{2,1,0:T(2,128)S(1)}, u32[]{:S(2)}, u32[]{:S(2)}) async-start(f32[32,2,128]{2,1,0:T(2,128)} %copy.90), calls=%async_computation.4 | async-start | bytes 65536 | tf_op jit(solution)/shard_map/all_to_all | solution.py:272
  261.1 7.2 %all-to-all-done.4 = f32[32,2,128]{2,1,0:T(2,128)S(1)} async-done(((f32[32,2,128]{2,1,0:T(2,128)}), f32[32,2,128]{2,1,0:T(2,128)S(1)}, u32[]{:S(2)}, u32[]{:S(2)}) %all-to-all-start.4) | async-done | bytes 32800 | tf_op jit(solution)/shard_map/all_to_all | solution.py:272
  268.3 0.1 copy.105
  268.4 0.2 fusion.54
  268.6 0.2 copy.93
  268.8 0.2 copy.92
  269.0 0.1 select_reduce_fusion
  269.1 0.7 copy.95
  (61 shorter events, 0.9 us)
Async XLA Ops:
  31.9 15.2 %all-to-all-start.1 = ((f32[16,64,128]{2,1,0:T(8,128)}), f32[16,64,128]{2,1,0:T(8,128)S(1)}, u32[]{:S(2)}, u32[]{:S(2)}) async-start(f32[16,64,128]{2,1,0:T(8,128)} %pick_occ.1), calls=%async_computation.1 | async-start | bytes 1048576 | tf_op jit(solution)/shard_map/all_to_all | solution.py:228
  48.2 17.4 %copy-start.6 = (f32[8,128,128]{2,1,0:T(8,128)}, f32[8,128,128]{2,1,0:T(8,128)S(1)}, u32[]{:S(2)}) copy-start(f32[8,128,128]{2,1,0:T(8,128)S(1)} %bitcast_multiply_fusion) | copy-start | bytes 1572868
  51.1 23.3 %all-to-all-start.2 = ((f32[8,128,128]{2,0,1:T(8,128)}), f32[8,128,128]{2,0,1:T(8,128)S(1)}, u32[]{:S(2)}, u32[]{:S(2)}) async-start(f32[8,128,128]{2,0,1:T(8,128)} %copy.81), calls=%async_computation.2 | async-start | bytes 1048576 | tf_op jit(solution)/shard_map/all_to_all | solution.py:32
  65.6 155.9 %collective-permute-start.9 = (f32[16,1,512,128]{3,2,1,0:T(8,128)}, f32[16,1,512,128]{3,2,1,0:T(8,128)}, u32[]{:S(2)}, u32[]{:S(2)}) collective-permute-start(f32[16,1,512,128]{3,2,1,0:T(8,128)} %constant_dynamic-slice_fusion.2), channel_id=1, source_target_pairs={{0,128},{128,0},{1,129},{129,1},{2,130},{130,2},{3,131},{131,3},{4... | collective-permute-start | bytes 12582920 | tf_op jit(solution)/shard_map/ppermute | solution.py:80
  76.3 31.6 %copy-start.8 = (s32[16,2]{0,1:T(2,128)S(1)}, s32[16,2]{0,1:T(2,128)}, u32[]{:S(2)}) copy-start(s32[16,2]{0,1:T(2,128)} %param.8) | copy-start | bytes 388
  77.4 19.3 %all-to-all-start.3 = ((f32[128,8,128]{2,1,0:T(8,128)}), f32[128,8,128]{2,1,0:T(8,128)}, u32[]{:S(2)}, u32[]{:S(2)}) async-start(f32[128,8,128]{2,1,0:T(8,128)} %copy.87), calls=%async_computation.3 | async-start | bytes 1048576 | tf_op jit(solution)/shard_map/all_to_all | solution.py:44
  83.5 24.4 %collective-permute-start = (f32[16,128,128]{2,1,0:T(8,128)S(1)}, f32[16,128,128]{2,1,0:T(8,128)S(1)}, u32[]{:S(2)}, u32[]{:S(2)}) collective-permute-start(f32[16,128,128]{2,1,0:T(8,128)S(1)} %slice.71.refs_0_), channel_id=1, source_target_pairs={{0,2},{1,3},{2,4},{3,5},{4,6},{5,7},{6,0},{7,1},{8,10},{9,11},{10,... | collective-permute-start | bytes 3145736 | tf_op jit(solution)/shard_map/ppermute | solution.py:59
  84.2 24.8 %collective-permute-start.1 = (f32[16,128,128]{2,1,0:T(8,128)S(1)}, f32[16,128,128]{2,1,0:T(8,128)S(1)}, u32[]{:S(2)}, u32[]{:S(2)}) collective-permute-start(f32[16,128,128]{2,1,0:T(8,128)S(1)} %slice.71.refs_0_), channel_id=1, source_target_pairs={{0,6},{1,7},{2,0},{3,1},{4,2},{5,3},{6,4},{7,5},{8,14},{9,15},{10,... | collective-permute-start | bytes 3145736 | tf_op jit(solution)/shard_map/ppermute | solution.py:59
  86.8 28.9 %collective-permute-start.2 = (f32[16,128,128]{2,1,0:T(8,128)S(1)}, f32[16,128,128]{2,1,0:T(8,128)}, u32[]{:S(2)}, u32[]{:S(2)}) collective-permute-start(f32[16,128,128]{2,1,0:T(8,128)S(1)} %slice.71.refs_0_), channel_id=1, source_target_pairs={{0,1},{1,0},{2,3},{3,2},{4,5},{5,4},{6,7},{7,6},{8,9},{9,8},{10,11... | collective-permute-start | bytes 3145736 | tf_op jit(solution)/shard_map/ppermute | solution.py:59
  100.8 7.2 %collective-permute-start.10 = (f32[1,512,128]{2,1,0:T(8,128)S(1)}, f32[1,512,128]{2,1,0:T(8,128)S(1)}, u32[]{:S(2)}, u32[]{:S(2)}) collective-permute-start(f32[1,512,128]{2,1,0:T(8,128)S(1)} %get-tuple-element.17), channel_id=1, source_target_pairs={{0,128},{128,0},{1,129},{129,1},{2,130},{130,2},{3,131},{131,3},{4... | collective-permute-start | bytes 786440 | tf_op jit(solution)/shard_map/ppermute | solution.py:80
  107.9 1.1 collective-permute-start.8
  108.0 16.2 %collective-permute-start.3 = (f32[8,128,128]{2,1,0:T(8,128)S(1)}, f32[8,128,128]{2,1,0:T(8,128)S(1)}, u32[]{:S(2)}, u32[]{:S(2)}) collective-permute-start(f32[8,128,128]{2,1,0:T(8,128)S(1)} %slice.72), channel_id=1, source_target_pairs={{0,2},{1,3},{2,4},{3,5},{4,6},{5,7},{6,0},{7,1},{8,10},{9,11},{10,... | collective-permute-start | bytes 1572872 | tf_op jit(solution)/shard_map/ppermute | solution.py:59
  108.3 58.3 %copy-start = (f32[2,512,128]{2,1,0:T(8,128)}, f32[2,512,128]{2,1,0:T(8,128)S(1)}, u32[]{:S(2)}) copy-start(f32[2,512,128]{2,1,0:T(8,128)S(1)} %pad_maximum_fusion.refs_0_) | copy-start | bytes 1572868
  109.1 26.3 %collective-permute-start.11 = (f32[2,512,128]{2,1,0:T(8,128)S(1)}, f32[2,512,128]{2,1,0:T(8,128)S(1)}, u32[]{:S(2)}, u32[]{:S(2)}) collective-permute-start(f32[2,512,128]{2,1,0:T(8,128)S(1)} %pad_maximum_fusion.refs_0_), channel_id=1, source_target_pairs={{0,2},{1,3},{2,4},{3,5},{4,6},{5,7},{6,0},{7,1},{8,10},{9,11},{10,... | collective-permute-start | bytes 1572872 | tf_op jit(solution)/shard_map/ppermute | solution.py:59
  109.1 26.6 %collective-permute-start.12 = (f32[2,512,128]{2,1,0:T(8,128)S(1)}, f32[2,512,128]{2,1,0:T(8,128)S(1)}, u32[]{:S(2)}, u32[]{:S(2)}) collective-permute-start(f32[2,512,128]{2,1,0:T(8,128)S(1)} %pad_maximum_fusion.refs_0_), channel_id=1, source_target_pairs={{0,6},{1,7},{2,0},{3,1},{4,2},{5,3},{6,4},{7,5},{8,14},{9,15},{10,... | collective-permute-start | bytes 1572872 | tf_op jit(solution)/shard_map/ppermute | solution.py:59
  115.7 21.9 %collective-permute-start.4 = (f32[8,128,128]{2,1,0:T(8,128)S(1)}, f32[8,128,128]{2,1,0:T(8,128)S(1)}, u32[]{:S(2)}, u32[]{:S(2)}) collective-permute-start(f32[8,128,128]{2,1,0:T(8,128)S(1)} %slice.73), channel_id=1, source_target_pairs={{0,6},{1,7},{2,0},{3,1},{4,2},{5,3},{6,4},{7,5},{8,14},{9,15},{10,... | collective-permute-start | bytes 1572872 | tf_op jit(solution)/shard_map/ppermute | solution.py:59
  124.2 77.1 %collective-permute-start.5 = (f32[16,128,128]{2,1,0:T(8,128)}, f32[16,128,128]{2,1,0:T(8,128)S(1)}, u32[]{:S(2)}, u32[]{:S(2)}) collective-permute-start(f32[16,128,128]{2,1,0:T(8,128)} %collective-permute-done.2.refs_3_), channel_id=1, source_target_pairs={{0,2},{1,3},{2,4},{3,5},{4,6},{5,7},{6,0},{7,1},{8,10},{9,11},{10,... | collective-permute-start | bytes 3145736 | tf_op jit(solution)/shard_map/ppermute | solution.py:59
  135.4 65.8 %copy-start.2 = (f32[2,512,128]{2,1,0:T(8,128)}, f32[2,512,128]{2,1,0:T(8,128)S(1)}, u32[]{:S(2)}) copy-start(f32[2,512,128]{2,1,0:T(8,128)S(1)} %collective-permute-done.11.refs_1_) | copy-start | bytes 1572868
  135.4 70.1 %collective-permute-start.6 = (f32[16,128,128]{2,1,0:T(8,128)}, f32[16,128,128]{2,1,0:T(8,128)}, u32[]{:S(2)}, u32[]{:S(2)}) collective-permute-start(f32[16,128,128]{2,1,0:T(8,128)} %collective-permute-done.2.refs_3_), channel_id=1, source_target_pairs={{0,6},{1,7},{2,0},{3,1},{4,2},{5,3},{6,4},{7,5},{8,14},{9,15},{10,... | collective-permute-start | bytes 3145736 | tf_op jit(solution)/shard_map/ppermute | solution.py:59
  135.7 65.6 %copy-start.4 = (f32[2,512,128]{2,1,0:T(8,128)}, f32[2,512,128]{2,1,0:T(8,128)S(1)}, u32[]{:S(2)}) copy-start(f32[2,512,128]{2,1,0:T(8,128)S(1)} %collective-permute-done.12.refs_2_) | copy-start | bytes 1572868
  135.7 27.4 %collective-permute-start.14 = (f32[1,512,128]{2,1,0:T(8,128)S(1)}, f32[1,512,128]{2,1,0:T(8,128)S(1)}, u32[]{:S(2)}, u32[]{:S(2)}) collective-permute-start(f32[1,512,128]{2,1,0:T(8,128)S(1)} %slice.76), channel_id=1, source_target_pairs={{0,2},{1,3},{2,4},{3,5},{4,6},{5,7},{6,0},{7,1},{8,10},{9,11},{10,... | collective-permute-start | bytes 786440 | tf_op jit(solution)/shard_map/ppermute | solution.py:59
  137.6 29.1 %collective-permute-start.15 = (f32[1,512,128]{2,1,0:T(8,128)S(1)}, f32[1,512,128]{2,1,0:T(8,128)S(1)}, u32[]{:S(2)}, u32[]{:S(2)}) collective-permute-start(f32[1,512,128]{2,1,0:T(8,128)S(1)} %slice.77), channel_id=1, source_target_pairs={{0,6},{1,7},{2,0},{3,1},{4,2},{5,3},{6,4},{7,5},{8,14},{9,15},{10,... | collective-permute-start | bytes 786440 | tf_op jit(solution)/shard_map/ppermute | solution.py:59
  163.1 45.9 %collective-permute-start.7 = (f32[16,128,128]{2,1,0:T(8,128)}, f32[16,128,128]{2,1,0:T(8,128)}, u32[]{:S(2)}, u32[]{:S(2)}) collective-permute-start(f32[16,128,128]{2,1,0:T(8,128)} %constant_dynamic-update-slice_fusion.refs_4_), channel_id=1, source_target_pairs={{0,1},{1,0},{2,3},{3,2},{4,5},{5,4},{6,7},{7,6},{8,9},{9,8},{10,11... | collective-permute-start | bytes 3145736 | tf_op jit(solution)/shard_map/ppermute | solution.py:59
  166.7 34.6 %collective-permute-start.13 = (f32[2,512,128]{2,1,0:T(8,128)S(1)}, f32[2,512,128]{2,1,0:T(8,128)}, u32[]{:S(2)}, u32[]{:S(2)}) collective-permute-start(f32[2,512,128]{2,1,0:T(8,128)S(1)} %pad_maximum_fusion.refs_0_), channel_id=1, source_target_pairs={{0,1},{1,0},{2,3},{3,2},{4,5},{5,4},{6,7},{7,6},{8,9},{9,8},{10,11... | collective-permute-start | bytes 1572872 | tf_op jit(solution)/shard_map/ppermute | solution.py:59
  201.3 41.8 %collective-permute-start.16 = (f32[2,512,128]{2,1,0:T(8,128)}, f32[2,512,128]{2,1,0:T(8,128)}, u32[]{:S(2)}, u32[]{:S(2)}) collective-permute-start(f32[2,512,128]{2,1,0:T(8,128)} %collective-permute-done.13.refs_3_), channel_id=1, source_target_pairs={{0,2},{1,3},{2,4},{3,5},{4,6},{5,7},{6,0},{7,1},{8,10},{9,11},{10,... | collective-permute-start | bytes 1572872 | tf_op jit(solution)/shard_map/ppermute | solution.py:59
  201.3 1.0 copy-start.7
  202.3 40.8 %collective-permute-start.17 = (f32[2,512,128]{2,1,0:T(8,128)}, f32[2,512,128]{2,1,0:T(8,128)}, u32[]{:S(2)}, u32[]{:S(2)}) collective-permute-start(f32[2,512,128]{2,1,0:T(8,128)} %collective-permute-done.13.refs_3_), channel_id=1, source_target_pairs={{0,6},{1,7},{2,0},{3,1},{4,2},{5,3},{6,4},{7,5},{8,14},{9,15},{10,... | collective-permute-start | bytes 1572872 | tf_op jit(solution)/shard_map/ppermute | solution.py:59
  205.5 37.6 %collective-permute-start.18 = (f32[2,512,128]{2,1,0:T(8,128)}, f32[2,512,128]{2,1,0:T(8,128)}, u32[]{:S(2)}, u32[]{:S(2)}) collective-permute-start(f32[2,512,128]{2,1,0:T(8,128)} %constant_dynamic-update-slice_fusion.2.refs_0_), channel_id=1, source_target_pairs={{0,1},{1,0},{2,3},{3,2},{4,5},{5,4},{6,7},{7,6},{8,9},{9,8},{10,11... | collective-permute-start | bytes 1572872 | tf_op jit(solution)/shard_map/ppermute | solution.py:59
  221.6 12.6 %copy-start.1 = (f32[2,512,128]{2,1,0:T(8,128)S(1)}, f32[2,512,128]{2,1,0:T(8,128)}, u32[]{:S(2)}) copy-start(f32[2,512,128]{2,1,0:T(8,128)} %copy-done) | copy-start | bytes 1572868
  221.6 12.6 %copy-start.3 = (f32[2,512,128]{2,1,0:T(8,128)S(1)}, f32[2,512,128]{2,1,0:T(8,128)}, u32[]{:S(2)}) copy-start(f32[2,512,128]{2,1,0:T(8,128)} %copy-done.2) | copy-start | bytes 1572868
  221.6 12.6 %copy-start.5 = (f32[2,512,128]{2,1,0:T(8,128)S(1)}, f32[2,512,128]{2,1,0:T(8,128)}, u32[]{:S(2)}) copy-start(f32[2,512,128]{2,1,0:T(8,128)} %copy-done.4) | copy-start | bytes 1572868
  252.7 15.5 %all-to-all-start.4 = ((f32[32,2,128]{2,1,0:T(2,128)}), f32[32,2,128]{2,1,0:T(2,128)S(1)}, u32[]{:S(2)}, u32[]{:S(2)}) async-start(f32[32,2,128]{2,1,0:T(2,128)} %copy.90), calls=%async_computation.4 | async-start | bytes 65536 | tf_op jit(solution)/shard_map/all_to_all | solution.py:272

commit v2 on v1

--- a/solution.py
+++ b/solution.py
@@ -102,71 +102,32 @@
     )(index, held)
 
 
-def density_kernel(occ_ref, vir_index_ref, place_ref, *refs):
-    pieces, vir_ref, out_ref = refs[:8], refs[8], refs[9]
-    index = occ_ref[pl.program_id(0)]
-    rows = pieces[0].shape[1] // 2
-    start = pl.multiple_of(index % 2 * rows, rows)
-    for number, piece in enumerate(pieces):
-        cells = pl.ds(pl.multiple_of(place_ref[number] * rows, rows), rows)
-        out_ref[0, cells, :] = piece[index // 2, pl.ds(start, rows), :] * vir_ref[0, 0, cells, :]
-
-
-def form_densities(occ_index, vir_index, place, pieces, vir):
-    number = occ_index.shape[0]
-    rows = vir.shape[2]
-    whole = pl.BlockSpec(memory_space=pltpu.VMEM)
-    return pl.pallas_call(
-        density_kernel,
-        grid_spec=pltpu.PrefetchScalarGridSpec(
-            num_scalar_prefetch=3,
-            grid=(number,),
-            in_specs=[whole] * 8
-            + [pl.BlockSpec((1, 1, rows, LANES), lambda p, occ, vir, place: (vir[p], place[8], 0, 0))],
-            out_specs=pl.BlockSpec((1, rows, LANES), lambda p, occ, vir, place: (p, 0, 0)),
-        ),
-        out_shape=jax.ShapeDtypeStruct((number, rows, LANES), jnp.float32),
-        compiler_params=pltpu.CompilerParams(vmem_limit_bytes=VMEM_BYTES),
-        cost_estimate=pl.CostEstimate(
-            flops=number * rows * LANES, bytes_accessed=16 * 1024 * 1024, transcendentals=0
-        ),
-        name="form_densities",
-    )(occ_index, vir_index, place, *pieces, vir)
-
-
 PAIR_GROUP = 4
 
 
-def contract_kernel(own_ref, mate_ref, *refs):
-    fields, out_ref, total = refs[:4], refs[4], refs[5]
-    step = pl.program_id(0)
-    rows = own_ref.shape[1]
-    per_half = own_ref.shape[0]
-
-    @pl.when(step == 0)
+def add_products(total, first, densities, fields, rows):
+    sums = [None] * (PAIR_GROUP * 8)
+    for tile in range(rows // 8):
+        cells = pl.ds(tile * 8, 8)
+        right = [field[j, cells, :] for field in fields for j in range(2)]
+        for k in range(PAIR_GROUP):
+            left = densities(k, cells)
+            for b in range(8):
+                term = left * right[b]
+                slot = k * 8 + b
+                sums[slot] = term if sums[slot] is None else sums[slot] + term
+    for slot, value in enumerate(sums):
+        total[first * 8 + slot] += value
+
+
+def start_total(total):
+    @pl.when(pl.program_id(0) == 0)
     def _():
         total[...] = jnp.zeros_like(total)
 
-    for half, densities in enumerate((own_ref, mate_ref)):
-
-        @pl.loop(0, per_half // PAIR_GROUP)
-        def _(group):
-            first = group * PAIR_GROUP
-            sums = [None] * (PAIR_GROUP * 8)
-            for tile in range(rows // 8):
-                cells = pl.ds(tile * 8, 8)
-                left = [densities[first + k, cells, :] for k in range(PAIR_GROUP)]
-                right = [field[j, cells, :] for field in fields for j in range(2)]
-                for k in range(PAIR_GROUP):
-                    for b in range(8):
-                        term = left[k] * right[b]
-                        slot = k * 8 + b
-                        sums[slot] = term if sums[slot] is None else sums[slot] + term
-            base = (half * per_half + first) * 8
-            for slot, value in enumerate(sums):
-                total[base + slot] += value
-
-    @pl.when(step == pl.num_programs(0) - 1)
+
+def finish_total(total, out_ref):
+    @pl.when(pl.program_id(0) == pl.num_programs(0) - 1)
     def _():
         lanes = jnp.sum(total[...], axis=1)
         out_ref[...] = lax.dot_general(
@@ -178,23 +139,99 @@
         )
 
 
-def contract(own, mate, fields):
-    pairs, rows, _ = own.shape
-    tile = 64
+def form_kernel(occ_index, vir_index, half, occ_ref, own_vir, mate_vir, *refs):
+    fields, density_ref, out_ref, total = refs[:4], refs[4], refs[5], refs[6]
+    rows = occ_ref.shape[2]
+    per_block = own_vir.shape[0]
+    start_total(total)
+    for block, vir_ref in enumerate((own_vir.at[:, 0], mate_vir.at[:, 0])):
+
+        @pl.loop(0, per_block // PAIR_GROUP)
+        def _(group):
+            first = block * per_block + group * PAIR_GROUP
+            occ = [occ_index[first + k] for k in range(PAIR_GROUP)]
+            vir = [vir_index[first + k] for k in range(PAIR_GROUP)]
+
+            def density(k, cells):
+                value = occ_ref[occ[k], 0, cells, :] * vir_ref[vir[k], cells, :]
+                density_ref[first + k, cells, :] = value
+                return value
+
+            add_products(total, first, density, fields, rows)
+
+    finish_total(total, out_ref)
+
+
+def contract_kernel(density_ref, *refs):
+    fields, out_ref, total = refs[:4], refs[4], refs[5]
+    start_total(total)
+
+    @pl.loop(0, density_ref.shape[0] // PAIR_GROUP)
+    def _(group):
+        first = group * PAIR_GROUP
+        add_products(
+            total,
+            first,
+            lambda k, cells: density_ref[first + k, cells, :],
+            fields,
+            density_ref.shape[1],
+        )
+
+    finish_total(total, out_ref)
+
+
+TILE = 128
+
+
+def form_and_contract(occ_index, vir_index, half, occ, own_vir, mate_vir, fields):
+    pairs = occ_index.shape[0]
+    orbitals, _, rows, _ = occ.shape
+    per_block = own_vir.shape[0]
+    return pl.pallas_call(
+        form_kernel,
+        grid_spec=pltpu.PrefetchScalarGridSpec(
+            num_scalar_prefetch=3,
+            grid=(rows // TILE,),
+            in_specs=[
+                pl.BlockSpec((orbitals, 1, TILE, LANES), lambda i, o, v, half: (0, half[0], i, 0)),
+                pl.BlockSpec((per_block, 1, TILE, LANES), lambda i, o, v, half: (0, half[0], i, 0)),
+                pl.BlockSpec((per_block, 1, TILE, LANES), lambda i, o, v, half: (0, 0, i, 0)),
+            ]
+            + [pl.BlockSpec((2, TILE, LANES), lambda i, o, v, half: (0, i, 0))] * 4,
+            out_specs=[
+                pl.BlockSpec((pairs, TILE, LANES), lambda i, o, v, half: (0, i, 0)),
+                pl.BlockSpec((8, pairs * 8), lambda i, o, v, half: (0, 0)),
+            ],
+            scratch_shapes=[pltpu.VMEM((pairs * 8, 8, LANES), jnp.float32)],
+        ),
+        out_shape=[
+            jax.ShapeDtypeStruct((pairs, rows, LANES), jnp.float32),
+            jax.ShapeDtypeStruct((8, pairs * 8), jnp.float32),
+        ],
+        compiler_params=pltpu.CompilerParams(vmem_limit_bytes=VMEM_BYTES),
+        cost_estimate=pl.CostEstimate(
+            flops=17 * pairs * rows * LANES, bytes_accessed=26 * 1024 * 1024, transcendentals=0
+        ),
+        name="form_and_contract",
+    )(occ_index, vir_index, half, occ, own_vir, mate_vir, *fields)
+
+
+def contract(densities, fields):
+    pairs, rows, _ = densities.shape
     return pl.pallas_call(
         contract_kernel,
-        grid=(rows // tile,),
-        in_specs=[pl.BlockSpec((pairs, tile, LANES), lambda i: (0, i, 0))] * 2
-        + [pl.BlockSpec((2, tile, LANES), lambda i: (0, i, 0))] * 4,
-        out_specs=pl.BlockSpec((8, 2 * pairs * 8), lambda i: (0, 0)),
-        out_shape=jax.ShapeDtypeStruct((8, 2 * pairs * 8), jnp.float32),
-        scratch_shapes=[pltpu.VMEM((2 * pairs * 8, 8, LANES), jnp.float32)],
+        grid=(rows // TILE,),
+        in_specs=[pl.BlockSpec((pairs, TILE, LANES), lambda i: (0, i, 0))]
+        + [pl.BlockSpec((2, TILE, LANES), lambda i: (0, i, 0))] * 4,
+        out_specs=pl.BlockSpec((8, pairs * 8), lambda i: (0, 0)),
+        out_shape=jax.ShapeDtypeStruct((8, pairs * 8), jnp.float32),
+        scratch_shapes=[pltpu.VMEM((pairs * 8, 8, LANES), jnp.float32)],
         compiler_params=pltpu.CompilerParams(vmem_limit_bytes=VMEM_BYTES),
         cost_estimate=pl.CostEstimate(
-            flops=2 * 16 * pairs * rows * LANES, bytes_accessed=12 * 1024 * 1024, transcendentals=0
+            flops=16 * pairs * rows * LANES, bytes_accessed=10 * 1024 * 1024, transcendentals=0
         ),
         name="contract",
-    )(own, mate, *fields)
+    )(densities, *fields)
 
 
 def on_device(occ_orbitals, vir_orbitals, xc_kernel, pairs, batch_slot):
@@ -210,6 +247,8 @@
     chunk_rows = cell_count // blocks // LANES
     half_rows = cell_count // 2 // LANES
 
+    every_occ = lax.all_gather(occ_orbitals, BLOCK_AXES, axis=0, tiled=True)
+    every_occ = every_occ.reshape(every_occ.shape[0], 2, half_rows, LANES)
     mate_pairs = swap_core(pairs)
     vir_halves = vir_orbitals.reshape(vir_local, 2, half_rows, LANES)
     mate_vir = swap_core(lax.dynamic_index_in_dim(vir_halves, 1 - grp, 1, keepdims=True))
@@ -231,8 +270,6 @@
     )
     sigma = own_occ.reshape(planes, size_y, size_z) * own_vir
 
-    occ_pieces = spread(held[:, : occ_local * chunk_rows])
-
     potential = hartree(sigma) + xc_kernel * sigma
     halves = potential.reshape(2, half_rows, LANES)
     kept = lax.dynamic_index_in_dim(halves, grp, 0, keepdims=True)
@@ -245,24 +282,19 @@
         for dy, dx in OFFSETS
     ]
     place = jnp.stack(places).astype(jnp.int32)
-    zero = jnp.zeros((1,), jnp.int32)
     mate_block = (1 - grp) * lax.axis_size("col") + col
-    own = form_densities(
-        pairs[:, 0],
-        pairs[:, 1] - block_index * vir_local,
-        jnp.concatenate([place, zero + grp]),
-        occ_pieces,
+    densities, near = form_and_contract(
+        jnp.concatenate([pairs[:, 0], mate_pairs[:, 0]]),
+        jnp.concatenate(
+            [pairs[:, 1] - block_index * vir_local, mate_pairs[:, 1] - mate_block * vir_local]
+        ),
+        jnp.full((1,), grp, jnp.int32),
+        every_occ,
         vir_halves,
-    )
-    mate = form_densities(
-        mate_pairs[:, 0],
-        mate_pairs[:, 1] - mate_block * vir_local,
-        jnp.concatenate([place, zero]),
-        occ_pieces,
         mate_vir,
-    )
-    near = contract(own, mate, fields[:4])
-    far = contract(own, mate, fields[4:])
+        fields[:4],
+    )
+    far = contract(densities, fields[4:])
 
     pair_count = pairs.shape[0]
     sums = jnp.stack([near[0], far[0]]).reshape(2, 2, pair_count * 8)

time: 273 us -> 219 us (0.80)
  waiting for transfers between devices: 117 us -> 76.5 us
  Pallas kernels: 44.3 us -> 21.7 us
  between operations: 2.14 us -> 15.5 us
  blocking collectives: 24.8 us -> 30.7 us
  starting transfers between devices: 54.1 us -> 50.3 us
  local copies, waits for them, and re-layouts: 17.6 us -> 14.7 us
    ppermute x16 -> x8, waiting for transfers between devices: 82 us -> 17 us  [shift_col(): return lax.ppermute(value, 'col', pairs)]
    pallas_call x4 -> x2, Pallas kernels: 42.8 us -> 20.2 us  [the longest x1 12.6 us: form_and_contract(): pl.pallas_call(form_kernel, grid_spec=pltpu.PrefetchScalarGridSpec(num_sc...]
    all_gather x0 -> x1, waiting for transfers between devices: none -> 16.1 us  [on_device(): every_occ = lax.all_gather(occ_orbitals, BLOCK_AXES, axis=0, tiled=True)]
    ppermute x16 -> x8, starting transfers between devices: 26.3 us -> 20.4 us  [shift_col(): return lax.ppermute(value, 'col', pairs)]
    all_to_all x1, blocking collectives: 24.8 us -> 30.7 us  [on_device(): lax.all_to_all(jnp.concatenate([chunks, note], axis=1), BLOCK_AXES, 0, 0,...]
    all_to_all x1, waiting for transfers between devices: 7.64 us -> 13.3 us  [hartree(): lax.all_to_all(columns, 'row', split_axis=0, concat_axis=1, tiled=True)]
  transfers between devices with their start and end apart: 23 -> 16, of which waited for: 11 -> 8; matrix products, arithmetic and copies ran while one was open for 6% -> 9% of each run, Pallas kernels for 13% -> 7%
where the time goes in v2:
time: 219 us; the launch traced here: 217 us
  waiting for transfers between devices  76.5 us (35%)
  starting transfers between devices  50.3 us (23%)
  blocking collectives  30.7 us (14%)
  Pallas kernels  21.7 us (10%)
  between operations  15.5 us (7%)
  local copies, waits for them, and re-layouts  14.7 us (7%)
  matrix products  5.28 us (2%)
    all_to_all x1, blocking collectives, on_device(): lax.all_to_all(jnp.concatenate([chunks, note], axis=1), BLOCK_AXES, 0, 0,...  30.7 us
    ppermute x8, starting transfers between devices, shift_col(): return lax.ppermute(value, 'col', pairs)  20.4 us
    ppermute x8, waiting for transfers between devices, shift_col(): return lax.ppermute(value, 'col', pairs)  17 us
    all_gather x1, waiting for transfers between devices, on_device(): every_occ = lax.all_gather(occ_orbitals, BLOCK_AXES, axis=0, tiled=True)  16.1 us
    all_to_all x1, waiting for transfers between devices, hartree(): lax.all_to_all(columns, 'row', split_axis=0, concat_axis=1, tiled=True)  13.3 us
    pallas_call x1, Pallas kernels, form_and_contract(): pl.pallas_call(form_kernel, grid_spec=pltpu.PrefetchScalarGridSpec(num_sc...  12.6 us
    all_to_all x1, waiting for transfers between devices, on_device(): own_occ = lax.all_to_all(picked, BLOCK_AXES, 0, 0, tiled=True)  11.5 us
    all_to_all x1, starting transfers between devices, hartree(): lax.all_to_all(grid_field, 'row', split_axis=1, concat_axis=0, tiled=True)  11.4 us
  transfers between devices with their start and end apart: 16, of which 8 were waited for; matrix products, arithmetic and copies ran while one was open for 9% of the time, Pallas kernels for 7%

profile of v2, /device:TPU:2, one launch (start us, length us, event | category | flops | bytes accessed | tf_op | source)
XLA Modules:
  0.0 216.5 jit_solution(17204764316327256875)
XLA Ops:
  6.5 0.7 all-gather.2.cloned.1.call-update
  7.3 1.3 dynamic-slice.2
  9.2 1.3 copy.79
  10.5 0.8 constant_dynamic-slice_fusion.2
  11.2 0.5 fusion.55
  12.4 0.1 concatenate.17
  12.5 30.7 %all_to_all.51.held_ref = f32[16,136,128]{2,1,0:T(8,128)S(1)} all-to-all(f32[16,136,128]{2,1,0:T(8,128)S(1)} %concatenate.17), channel_id=1, replica_groups=mesh['grp'=2,'row'=16,'col'=8] {'grp','col'}, dimensions={0} | all-to-all | bytes 2228224 | tf_op jit(solution)/shard_map/all_to_all | solution.py:262
  43.1 0.4 fusion.20.index_ref
  43.5 1.5 pick_occ.1
  45.0 3.6 %all-to-all-start.1 = ((f32[16,64,128]{2,1,0:T(8,128)}), f32[16,64,128]{2,1,0:T(8,128)S(1)}, u32[]{:S(2)}, u32[]{:S(2)}) async-start(f32[16,64,128]{2,1,0:T(8,128)} %pick_occ.1), calls=%async_computation.1 | async-start | bytes 1048576 | tf_op jit(solution)/shard_map/all_to_all | solution.py:267
  49.1 11.5 %all-to-all-done.1 = f32[16,64,128]{2,1,0:T(8,128)S(1)} async-done(((f32[16,64,128]{2,1,0:T(8,128)}), f32[16,64,128]{2,1,0:T(8,128)S(1)}, u32[]{:S(2)}, u32[]{:S(2)}) %all-to-all-start.1) | async-done | bytes 524320 | tf_op jit(solution)/shard_map/all_to_all | solution.py:267
  60.6 1.1 bitcast_multiply_fusion
  61.7 0.8 fusion.10
  62.5 0.9 convolution_bitcast_fusion.1
  63.4 1.1 copy.81
  64.6 11.4 %all-to-all-start.2 = ((f32[8,128,128]{2,0,1:T(8,128)}), f32[8,128,128]{2,0,1:T(8,128)S(1)}, u32[]{:S(2)}, u32[]{:S(2)}) async-start(f32[8,128,128]{2,0,1:T(8,128)} %copy.81), calls=%async_computation.2 | async-start | bytes 1048576 | tf_op jit(solution)/shard_map/all_to_all | solution.py:32
  76.0 4.5 %constant_dynamic-slice_fusion.3 = f32[16,1,512,128]{3,2,1,0:T(8,128)} fusion(f32[16,2,512,128]{3,2,1,0:T(8,128)} %bitcast.84, s32[]{:T(128)S(6)} %select_n.149), kind=kLoop, calls=%fused_computation.60 | loop fusion | bytes 8388612 | tf_op jit(solution)/shard_map/jit(dynamic_index_in_dim)/dynamic_slice | solution.py:254
  80.5 0.0 collective-permute-start.1
  80.5 0.1 broadcast_add_fusion
  80.6 9.2 %all-to-all-done.2 = f32[8,128,128]{2,0,1:T(8,128)S(1)} async-done(((f32[8,128,128]{2,0,1:T(8,128)}), f32[8,128,128]{2,0,1:T(8,128)S(1)}, u32[]{:S(2)}, u32[]{:S(2)}) %all-to-all-start.2) | async-done | bytes 524320 | tf_op jit(solution)/shard_map/all_to_all | solution.py:32
  89.8 0.1 copy.83
  89.9 0.9 convolution_multiply_fusion.1
  90.8 0.9 fusion.14
  91.7 0.0 copy-start.1
  91.7 1.1 copy.87
  92.9 5.9 %all-to-all-start.3 = ((f32[128,8,128]{2,1,0:T(8,128)}), f32[128,8,128]{2,1,0:T(8,128)S(1)}, u32[]{:S(2)}, u32[]{:S(2)}) async-start(f32[128,8,128]{2,1,0:T(8,128)} %copy.87), calls=%async_computation.3 | async-start | bytes 1048576 | tf_op jit(solution)/shard_map/all_to_all | solution.py:44
  98.8 13.3 %all-to-all-done.3 = f32[128,8,128]{2,1,0:T(8,128)S(1)} async-done(((f32[128,8,128]{2,1,0:T(8,128)}), f32[128,8,128]{2,1,0:T(8,128)S(1)}, u32[]{:S(2)}, u32[]{:S(2)}) %all-to-all-start.3) | async-done | bytes 524320 | tf_op jit(solution)/shard_map/all_to_all | solution.py:44
  112.1 0.9 convolution_bitcast_fusion
  113.0 0.9 fusion
  114.0 0.1 collective-permute-start.2
  114.1 1.5 collective-permute-done.2
  115.6 0.6 collective-permute-start.3
  116.3 2.7 %collective-permute-start.4 = (f32[2,512,128]{2,1,0:T(8,128)S(1)}, f32[2,512,128]{2,1,0:T(8,128)S(1)}, u32[]{:S(2)}, u32[]{:S(2)}) collective-permute-start(f32[2,512,128]{2,1,0:T(8,128)S(1)} %pad_maximum_fusion.refs_0_), channel_id=1, source_target_pairs={{0,6},{1,7},{2,0},{3,1},{4,2},{5,3},{6,4},{7,5},{8,14},{9,15},{10,... | collective-permute-start | bytes 1572872 | tf_op jit(solution)/shard_map/ppermute | solution.py:59
  118.9 3.4 %collective-permute-start.5 = (f32[2,512,128]{2,1,0:T(8,128)S(1)}, f32[2,512,128]{2,1,0:T(8,128)S(1)}, u32[]{:S(2)}, u32[]{:S(2)}) collective-permute-start(f32[2,512,128]{2,1,0:T(8,128)S(1)} %pad_maximum_fusion.refs_0_), channel_id=1, source_target_pairs={{0,1},{1,0},{2,3},{3,2},{4,5},{5,4},{6,7},{7,6},{8,9},{9,8},{10,11... | collective-permute-start | bytes 1572872 | tf_op jit(solution)/shard_map/ppermute | solution.py:59
  122.3 11.4 %collective-permute-done.3.refs_1_ = f32[2,512,128]{2,1,0:T(8,128)S(1)} collective-permute-done((f32[2,512,128]{2,1,0:T(8,128)S(1)}, f32[2,512,128]{2,1,0:T(8,128)S(1)}, u32[]{:S(2)}, u32[]{:S(2)}) %collective-permute-start.3) | collective-permute-done | bytes 524320 | tf_op jit(solution)/shard_map/ppermute | solution.py:59
  133.7 0.3 collective-permute-start.6
  134.0 0.0 collective-permute-done.4.refs_2_
  134.0 0.7 slice.61
  134.7 3.2 %collective-permute-start.7 = (f32[1,512,128]{2,1,0:T(8,128)}, f32[1,512,128]{2,1,0:T(8,128)}, u32[]{:S(2)}, u32[]{:S(2)}) collective-permute-start(f32[1,512,128]{2,1,0:T(8,128)} %slice.61), channel_id=1, source_target_pairs={{0,6},{1,7},{2,0},{3,1},{4,2},{5,3},{6,4},{7,5},{8,14},{9,15},{10,... | collective-permute-start | bytes 786440 | tf_op jit(solution)/shard_map/ppermute | solution.py:59
  137.9 5.6 %collective-permute-done.5.refs_3_ = f32[2,512,128]{2,1,0:T(8,128)S(1)} collective-permute-done((f32[2,512,128]{2,1,0:T(8,128)S(1)}, f32[2,512,128]{2,1,0:T(8,128)S(1)}, u32[]{:S(2)}, u32[]{:S(2)}) %collective-permute-start.5) | collective-permute-done | bytes 524320 | tf_op jit(solution)/shard_map/ppermute | solution.py:59
  143.5 1.1 collective-permute-start.8
  144.7 2.1 collective-permute-start.9
  146.8 0.0 collective-permute-done.7
  146.8 1.0 constant_dynamic-update-slice_fusion.refs_0_
  147.8 7.0 %collective-permute-start.10 = (f32[2,512,128]{2,1,0:T(8,128)S(1)}, f32[2,512,128]{2,1,0:T(8,128)}, u32[]{:S(2)}, u32[]{:S(2)}) collective-permute-start(f32[2,512,128]{2,1,0:T(8,128)S(1)} %constant_dynamic-update-slice_fusion.refs_0_), channel_id=1, source_target_pairs={{0,1},{1,0},{2,3},{3,2},{4,5},{5,4},{6,7},{7,6},{8,9},{9,8},{10,11... | collective-permute-start | bytes 1572872 | tf_op jit(solution)/shard_map/ppermute | solution.py:59
  154.8 0.1 stack.38
  154.9 0.0 collective-permute-done
  154.9 0.1 pad_add_fusion
  155.0 16.1 %all-gather.2.cloned.1.call-done = f32[32,8,128,128]{3,2,1,0:T(8,128)} async-done(((f32[2,8,128,128]{3,2,1,0:T(8,128)}), f32[32,8,128,128]{3,2,1,0:T(8,128)}) %all-gather.2.cloned.1.call-update) | async-done | bytes 16777232 | tf_op jit(solution)/shard_map/all_gather | solution.py:250
  171.1 12.6 %form_and_contract.1 = (f32[32,512,128]{2,1,0:T(8,128)}, f32[8,256]{1,0:T(8,128)S(1)}) custom-call(s32[32]{0:T(128)S(1)} %get-tuple-element.30.occ_index, s32[32]{0:T(128)S(1)} %get-tuple-element.31.vir_index, s32[1]{0:T(128)} %bitcast.12.half, f32[32,2,512,128]{3,2,1,0:T(8,128)} %bitcast.86, f32[16,2,512,128]{3,2,1,0:T(8,128)} %bitcast.85, ...), custom_call_target="tpu_custom_call" | custom-call | flops 35651584 | bytes 27262976 | tf_op jit(solution)/shard_map/form_and_contract/pallas_call | solution.py:190
  183.7 0.0 collective-permute-done.8.refs_1_
  183.7 0.0 collective-permute-done.9.refs_2_
  183.7 0.0 collective-permute-done.10.refs_3_
  183.7 7.6 %contract.1 = f32[8,256]{1,0:T(8,128)S(1)} custom-call(f32[32,512,128]{2,1,0:T(8,128)} %get-tuple-element.8.density_ref, f32[2,512,128]{2,1,0:T(8,128)S(1)} %constant_dynamic-update-slice_fusion.refs_0_, f32[2,512,128]{2,1,0:T(8,128)S(1)} %collective-permute-done.8.refs_1_, f32[2,512,128]{2,1,0:T(8,128)} %collective-permute-done.9.refs_2_, ...), custom_call_target="tpu_custom_call" | custom-call | flops 33554432 | bytes 10485760 | tf_op jit(solution)/shard_map/contract/pallas_call | solution.py:221
  191.4 0.6 copy.90
  192.1 8.8 %all-to-all-start.4 = ((f32[32,2,128]{2,1,0:T(2,128)}), f32[32,2,128]{2,1,0:T(2,128)S(1)}, u32[]{:S(2)}, u32[]{:S(2)}) async-start(f32[32,2,128]{2,1,0:T(2,128)} %copy.90), calls=%async_computation.4 | async-start | bytes 65536 | tf_op jit(solution)/shard_map/all_to_all | solution.py:304
  200.9 0.1 iota_compare_fusion
  201.0 7.2 %all-to-all-done.4 = f32[32,2,128]{2,1,0:T(2,128)S(1)} async-done(((f32[32,2,128]{2,1,0:T(2,128)}), f32[32,2,128]{2,1,0:T(2,128)S(1)}, u32[]{:S(2)}, u32[]{:S(2)}) %all-to-all-start.4) | async-done | bytes 32800 | tf_op jit(solution)/shard_map/all_to_all | solution.py:304
  208.2 0.1 copy.105
  208.3 0.2 fusion.54
  208.5 0.2 copy.92
  208.7 0.2 copy.93
  208.9 0.1 select_reduce_fusion
  209.0 0.7 copy.95
  (26 shorter events, 0.3 us)
Async XLA Ops:
  6.5 164.5 %all-gather.2.cloned.1.call-start = ((), (), s32[]{:S(2)}) async-start(), calls=%async_computation.5 | async-start | bytes 17825792 | tf_op jit(solution)/shard_map/all_gather | solution.py:250
  45.0 15.6 %all-to-all-start.1 = ((f32[16,64,128]{2,1,0:T(8,128)}), f32[16,64,128]{2,1,0:T(8,128)S(1)}, u32[]{:S(2)}, u32[]{:S(2)}) async-start(f32[16,64,128]{2,1,0:T(8,128)} %pick_occ.1), calls=%async_computation.1 | async-start | bytes 1048576 | tf_op jit(solution)/shard_map/all_to_all | solution.py:267
  64.6 25.2 %all-to-all-start.2 = ((f32[8,128,128]{2,0,1:T(8,128)}), f32[8,128,128]{2,0,1:T(8,128)S(1)}, u32[]{:S(2)}, u32[]{:S(2)}) async-start(f32[8,128,128]{2,0,1:T(8,128)} %copy.81), calls=%async_computation.2 | async-start | bytes 1048576 | tf_op jit(solution)/shard_map/all_to_all | solution.py:32
  80.5 32.6 %copy-start = (f32[8,128,128]{2,1,0:T(8,128)S(1)}, f32[8,128,128]{2,1,0:T(8,128)}, u32[]{:S(2)}) copy-start(f32[8,128,128]{2,1,0:T(8,128)} %param.7) | copy-start | bytes 1572868
  80.5 74.5 %collective-permute-start.1 = (f32[16,1,512,128]{3,2,1,0:T(8,128)}, f32[16,1,512,128]{3,2,1,0:T(8,128)}, u32[]{:S(2)}, u32[]{:S(2)}) collective-permute-start(f32[16,1,512,128]{3,2,1,0:T(8,128)} %constant_dynamic-slice_fusion.3), channel_id=1, source_target_pairs={{0,128},{128,0},{1,129},{129,1},{2,130},{130,2},{3,131},{131,3},{4... | collective-permute-start | bytes 12582920 | tf_op jit(solution)/shard_map/ppermute | solution.py:80
  91.7 46.2 %copy-start.1 = (s32[16,2]{0,1:T(2,128)S(1)}, s32[16,2]{0,1:T(2,128)}, u32[]{:S(2)}) copy-start(s32[16,2]{0,1:T(2,128)} %param.8) | copy-start | bytes 388
  92.9 19.3 %all-to-all-start.3 = ((f32[128,8,128]{2,1,0:T(8,128)}), f32[128,8,128]{2,1,0:T(8,128)S(1)}, u32[]{:S(2)}, u32[]{:S(2)}) async-start(f32[128,8,128]{2,1,0:T(8,128)} %copy.87), calls=%async_computation.3 | async-start | bytes 1048576 | tf_op jit(solution)/shard_map/all_to_all | solution.py:44
  114.0 1.6 collective-permute-start.2
  115.6 18.1 %collective-permute-start.3 = (f32[2,512,128]{2,1,0:T(8,128)S(1)}, f32[2,512,128]{2,1,0:T(8,128)S(1)}, u32[]{:S(2)}, u32[]{:S(2)}) collective-permute-start(f32[2,512,128]{2,1,0:T(8,128)S(1)} %pad_maximum_fusion.refs_0_), channel_id=1, source_target_pairs={{0,2},{1,3},{2,4},{3,5},{4,6},{5,7},{6,0},{7,1},{8,10},{9,11},{10,... | collective-permute-start | bytes 1572872 | tf_op jit(solution)/shard_map/ppermute | solution.py:59
  116.3 17.7 %collective-permute-start.4 = (f32[2,512,128]{2,1,0:T(8,128)S(1)}, f32[2,512,128]{2,1,0:T(8,128)S(1)}, u32[]{:S(2)}, u32[]{:S(2)}) collective-permute-start(f32[2,512,128]{2,1,0:T(8,128)S(1)} %pad_maximum_fusion.refs_0_), channel_id=1, source_target_pairs={{0,6},{1,7},{2,0},{3,1},{4,2},{5,3},{6,4},{7,5},{8,14},{9,15},{10,... | collective-permute-start | bytes 1572872 | tf_op jit(solution)/shard_map/ppermute | solution.py:59
  118.9 24.6 %collective-permute-start.5 = (f32[2,512,128]{2,1,0:T(8,128)S(1)}, f32[2,512,128]{2,1,0:T(8,128)S(1)}, u32[]{:S(2)}, u32[]{:S(2)}) collective-permute-start(f32[2,512,128]{2,1,0:T(8,128)S(1)} %pad_maximum_fusion.refs_0_), channel_id=1, source_target_pairs={{0,1},{1,0},{2,3},{3,2},{4,5},{5,4},{6,7},{7,6},{8,9},{9,8},{10,11... | collective-permute-start | bytes 1572872 | tf_op jit(solution)/shard_map/ppermute | solution.py:59
  133.7 11.0 %collective-permute-start.6 = (f32[1,512,128]{2,1,0:T(8,128)S(1)}, f32[1,512,128]{2,1,0:T(8,128)S(1)}, u32[]{:S(2)}, u32[]{:S(2)}) collective-permute-start(f32[1,512,128]{2,1,0:T(8,128)S(1)} %slice.60), channel_id=1, source_target_pairs={{0,2},{1,3},{2,4},{3,5},{4,6},{5,7},{6,0},{7,1},{8,10},{9,11},{10,... | collective-permute-start | bytes 786440 | tf_op jit(solution)/shard_map/ppermute | solution.py:59
  134.7 12.1 %collective-permute-start.7 = (f32[1,512,128]{2,1,0:T(8,128)}, f32[1,512,128]{2,1,0:T(8,128)}, u32[]{:S(2)}, u32[]{:S(2)}) collective-permute-start(f32[1,512,128]{2,1,0:T(8,128)} %slice.61), channel_id=1, source_target_pairs={{0,6},{1,7},{2,0},{3,1},{4,2},{5,3},{6,4},{7,5},{8,14},{9,15},{10,... | collective-permute-start | bytes 786440 | tf_op jit(solution)/shard_map/ppermute | solution.py:59
  137.9 16.9 %collective-permute-start = (s32[16,2]{0,1:T(2,128)S(1)}, s32[16,2]{0,1:T(2,128)S(1)}, u32[]{:S(2)}, u32[]{:S(2)}) collective-permute-start(s32[16,2]{0,1:T(2,128)S(1)} %copy-done.1), channel_id=1, source_target_pairs={{0,128},{128,0},{1,129},{129,1},{2,130},{130,2},{3,131},{131,3},{4... | collective-permute-start | bytes 392 | tf_op jit(solution)/shard_map/ppermute | solution.py:80
  143.5 40.2 %collective-permute-start.8 = (f32[2,512,128]{2,1,0:T(8,128)S(1)}, f32[2,512,128]{2,1,0:T(8,128)S(1)}, u32[]{:S(2)}, u32[]{:S(2)}) collective-permute-start(f32[2,512,128]{2,1,0:T(8,128)S(1)} %collective-permute-done.5.refs_3_), channel_id=1, source_target_pairs={{0,2},{1,3},{2,4},{3,5},{4,6},{5,7},{6,0},{7,1},{8,10},{9,11},{10,... | collective-permute-start | bytes 1572872 | tf_op jit(solution)/shard_map/ppermute | solution.py:59
  144.7 39.0 %collective-permute-start.9 = (f32[2,512,128]{2,1,0:T(8,128)S(1)}, f32[2,512,128]{2,1,0:T(8,128)}, u32[]{:S(2)}, u32[]{:S(2)}) collective-permute-start(f32[2,512,128]{2,1,0:T(8,128)S(1)} %collective-permute-done.5.refs_3_), channel_id=1, source_target_pairs={{0,6},{1,7},{2,0},{3,1},{4,2},{5,3},{6,4},{7,5},{8,14},{9,15},{10,... | collective-permute-start | bytes 1572872 | tf_op jit(solution)/shard_map/ppermute | solution.py:59
  147.8 35.9 %collective-permute-start.10 = (f32[2,512,128]{2,1,0:T(8,128)S(1)}, f32[2,512,128]{2,1,0:T(8,128)}, u32[]{:S(2)}, u32[]{:S(2)}) collective-permute-start(f32[2,512,128]{2,1,0:T(8,128)S(1)} %constant_dynamic-update-slice_fusion.refs_0_), channel_id=1, source_target_pairs={{0,1},{1,0},{2,3},{3,2},{4,5},{5,4},{6,7},{7,6},{8,9},{9,8},{10,11... | collective-permute-start | bytes 1572872 | tf_op jit(solution)/shard_map/ppermute | solution.py:59
  192.1 16.1 %all-to-all-start.4 = ((f32[32,2,128]{2,1,0:T(2,128)}), f32[32,2,128]{2,1,0:T(2,128)S(1)}, u32[]{:S(2)}, u32[]{:S(2)}) async-start(f32[32,2,128]{2,1,0:T(2,128)} %copy.90), calls=%async_computation.4 | async-start | bytes 65536 | tf_op jit(solution)/shard_map/all_to_all | solution.py:304
Sparse Core Ops, SparseCore 0:
  10.1 160.8 all-gather.1

commit v3 on v2

v3 whole, which is shorter than its diff:
```python
import jax
import jax.numpy as jnp
from jax import lax
from jax.experimental import pallas as pl
from jax.experimental.pallas import tpu as pltpu
from jax.sharding import PartitionSpec as P

COULOMB = 0.4
LANES = 128
BLOCK_AXES = ("grp", "col")
VMEM_BYTES = 48 * 1024 * 1024


def cas_table(length):
    indices = jnp.arange(length, dtype=jnp.int32)
    products = indices[:, None] * indices[None, :] % length
    angles = products.astype(jnp.float32) * (2.0 * jnp.pi / length)
    return jnp.cos(angles) + jnp.sin(angles)


def signed_square(frequency, length):
    signed = ((frequency + length // 2) % length - length // 2).astype(jnp.float32)
    return signed * signed


def planes_forward(density):
    cas_rows = cas_table(density.shape[1])
    highest = lax.Precision.HIGHEST
    grid_field = jnp.dot(density, cas_rows, precision=highest)
    return jnp.einsum("xyz,yv->xvz", grid_field, cas_rows, precision=highest)


def filter_columns(columns):
    length, y_width, _ = columns.shape
    cas_rows = cas_table(length)
    highest = lax.Precision.HIGHEST
    columns = jnp.einsum("xyz,xu->uyz", columns, cas_rows, precision=highest)
    frequency = jnp.arange(length, dtype=jnp.int32)
    local_y = lax.axis_index("row") * y_width + jnp.arange(y_width, dtype=jnp.int32)
    squared_sum = (
        signed_square(frequency, length)[:, None, None]
        + signed_square(local_y, length)[None, :, None]
        + signed_square(frequency, length)[None, None, :]
    )
    kernel = jnp.where(squared_sum > 0, COULOMB / jnp.maximum(squared_sum, 1.0), 0.0)
    return jnp.einsum("xyz,xu->uyz", columns * kernel, cas_rows, precision=highest)


def planes_back(grid_field):
    length = grid_field.shape[1]
    cas_rows = cas_table(length)
    highest = lax.Precision.HIGHEST
    grid_field = jnp.einsum("xyz,yv->xvz", grid_field, cas_rows, precision=highest)
    grid_field = jnp.dot(grid_field, cas_rows, precision=highest)
    return grid_field * (1.0 / float(length) ** 3)


RING_Y, RING_X = 4, 2


def shift_col(value, dy, dx):
    pairs = [
        (y * RING_X + x, (y + dy) % RING_Y * RING_X + (x + dx) % RING_X)
        for y in range(RING_Y)
        for x in range(RING_X)
    ]
    return lax.ppermute(value, "col", pairs)


OFFSETS = ((0, 0), (1, 0), (3, 0), (0, 1), (2, 0), (1, 1), (3, 1), (2, 1))


def spread(piece):
    low, high = piece[:1], piece[1:]
    from_side = shift_col(piece, 0, 1)
    below_low, above_high = shift_col(low, 1, 0), shift_col(high, -1, 0)
    below_high, above_low = shift_col(high, 1, 0), shift_col(low, -1, 0)
    far_low, far_high = shift_col(below_low, 1, 0), shift_col(above_high, -1, 0)
    side_below, side_above = shift_col(from_side, 1, 0), shift_col(from_side, -1, 0)
    last_low, last_high = shift_col(far_low, 0, 1), shift_col(far_high, 0, 1)
    near = [piece, below_low, below_high, above_low, above_high, from_side]
    return near, [far_low, far_high, side_below, side_above, last_low, last_high]


def swap_core(value):
    return lax.ppermute(value, "grp", [(0, 1), (1, 0)])


def pick_kernel(place_ref, *refs):
    arrays, out_ref, sems = refs[:-2], refs[-2], refs[-1]
    parts = [array.at[j] for array in arrays for j in range(array.shape[0])]
    for number in range(out_ref.shape[0]):
        for order, part in enumerate(parts):

            @pl.when(place_ref[number] == order)
            def _():
                pltpu.make_async_copy(part, out_ref.at[number], sems.at[number]).start()

    for number in range(out_ref.shape[0]):
        pltpu.make_async_copy(parts[0], out_ref.at[number], sems.at[number]).wait()


def pick(place, arrays):
    count = place.shape[0]
    return pl.pallas_call(
        pick_kernel,
        out_shape=jax.ShapeDtypeStruct((count,) + arrays[0].shape[1:], jnp.float32),
        in_specs=[pl.BlockSpec(memory_space=pltpu.SMEM)]
        + [pl.BlockSpec(memory_space=pl.ANY)] * len(arrays),
        out_specs=pl.BlockSpec(memory_space=pltpu.VMEM),
        scratch_shapes=[pltpu.SemaphoreType.DMA((count,))],
        compiler_params=pltpu.CompilerParams(vmem_limit_bytes=VMEM_BYTES),
        name="pick_occ",
    )(place, *arrays)


PAIR_GROUP = 4


def add_products(total, first, densities, fields, rows):
    sums = [None] * (PAIR_GROUP * 8)
    for tile in range(rows // 8):
        cells = pl.ds(tile * 8, 8)
        right = [field[j, cells, :] for field in fields for j in range(field.shape[0])]
        for k in range(PAIR_GROUP):
            left = densities(k, cells)
            for b in range(8):
                term = left * right[b]
                slot = k * 8 + b
                sums[slot] = term if sums[slot] is None else sums[slot] + term
    for slot, value in enumerate(sums):
        total[first * 8 + slot] += value


def start_total(total):
    @pl.when(pl.program_id(0) == 0)
    def _():
        total[...] = jnp.zeros_like(total)


def finish_total(total, out_ref):
    @pl.when(pl.program_id(0) == pl.num_programs(0) - 1)
    def _():
        lanes = jnp.sum(total[...], axis=1)
        out_ref[...] = lax.dot_general(
            jnp.ones((8, LANES), jnp.float32),
            lanes,
            (((1,), (1,)), ((), ())),
            precision=lax.Precision.HIGHEST,
            preferred_element_type=jnp.float32,
        )


def form_kernel(occ_index, vir_index, half, own_occ, mate_occ, own_vir, mate_vir, *refs):
    fields, (density_ref, out_ref, total) = refs[:-3], refs[-3:]
    held, rows, _ = own_occ.shape
    per_block = own_vir.shape[0]
    start_total(total)
    for block, vir_ref in enumerate((own_vir.at[:, 0], mate_vir.at[:, 0])):

        @pl.loop(0, per_block // PAIR_GROUP)
        def _(group):
            first = block * per_block + group * PAIR_GROUP
            occ = [occ_index[first + k] for k in range(PAIR_GROUP)]
            near = [index < held for index in occ]
            occ = [jnp.where(own, index, index - held) for own, index in zip(near, occ)]
            vir = [vir_index[first + k] for k in range(PAIR_GROUP)]

            def density(k, cells):
                left = jnp.where(near[k], own_occ[occ[k], cells, :], mate_occ[occ[k], cells, :])
                value = left * vir_ref[vir[k], cells, :]
                density_ref[first + k, cells, :] = value
                return value

            add_products(total, first, density, fields, rows)

    finish_total(total, out_ref)


def contract_kernel(density_ref, *refs):
    fields, (out_ref, total) = refs[:-2], refs[-2:]
    start_total(total)

    @pl.loop(0, density_ref.shape[0] // PAIR_GROUP)
    def _(group):
        first = group * PAIR_GROUP
        add_products(
            total,
            first,
            lambda k, cells: density_ref[first + k, cells, :],
            fields,
            density_ref.shape[1],
        )

    finish_total(total, out_ref)


TILE = 128


def form_and_contract(occ_index, vir_index, half, own_occ, mate_occ, own_vir, mate_vir, fields):
    pairs = occ_index.shape[0]
    held, rows, _ = own_occ.shape
    per_block = own_vir.shape[0]
    occ_spec = pl.BlockSpec((held, TILE, LANES), lambda i, o, v, half: (0, i, 0))
    return pl.pallas_call(
        form_kernel,
        grid_spec=pltpu.PrefetchScalarGridSpec(
            num_scalar_prefetch=3,
            grid=(rows // TILE,),
            in_specs=[
                occ_spec,
                occ_spec,
                pl.BlockSpec((per_block, 1, TILE, LANES), lambda i, o, v, half: (0, half[0], i, 0)),
                pl.BlockSpec((per_block, 1, TILE, LANES), lambda i, o, v, half: (0, 0, i, 0)),
            ]
            + [
                pl.BlockSpec((field.shape[0], TILE, LANES), lambda i, o, v, half: (0, i, 0))
                for field in fields
            ],
            out_specs=[
                pl.BlockSpec((pairs, TILE, LANES), lambda i, o, v, half: (0, i, 0)),
                pl.BlockSpec((8, pairs * 8), lambda i, o, v, half: (0, 0)),
            ],
            scratch_shapes=[pltpu.VMEM((pairs * 8, 8, LANES), jnp.float32)],
        ),
        out_shape=[
            jax.ShapeDtypeStruct((pairs, rows, LANES), jnp.float32),
            jax.ShapeDtypeStruct((8, pairs * 8), jnp.float32),
        ],
        compiler_params=pltpu.CompilerParams(vmem_limit_bytes=VMEM_BYTES),
        cost_estimate=pl.CostEstimate(
            flops=17 * pairs * rows * LANES, bytes_accessed=26 * 1024 * 1024, transcendentals=0
        ),
        name="form_and_contract",
    )(occ_index, vir_index, half, own_occ, mate_occ, own_vir, mate_vir, *fields)


def contract(densities, fields):
    pairs, rows, _ = densities.shape
    return pl.pallas_call(
        contract_kernel,
        grid=(rows // TILE,),
        in_specs=[pl.BlockSpec((pairs, TILE, LANES), lambda i: (0, i, 0))]
        + [pl.BlockSpec((field.shape[0], TILE, LANES), lambda i: (0, i, 0)) for field in fields],
        out_specs=pl.BlockSpec((8, pairs * 8), lambda i: (0, 0)),
        out_shape=jax.ShapeDtypeStruct((8, pairs * 8), jnp.float32),
        scratch_shapes=[pltpu.VMEM((pairs * 8, 8, LANES), jnp.float32)],
        compiler_params=pltpu.CompilerParams(vmem_limit_bytes=VMEM_BYTES),
        cost_estimate=pl.CostEstimate(
            flops=16 * pairs * rows * LANES, bytes_accessed=10 * 1024 * 1024, transcendentals=0
        ),
        name="contract",
    )(densities, *fields)


def on_device(occ_orbitals, vir_orbitals, xc_kernel, pairs, batch_slot):
    planes, size_y, size_z = xc_kernel.shape
    cell_count = planes * size_y * size_z
    row_count = lax.axis_size("row")
    scale = 1.0 / float(cell_count * row_count)
    grp = lax.axis_index("grp")
    col = lax.axis_index("col")
    blocks = lax.axis_size(BLOCK_AXES)
    block_index = grp * lax.axis_size("col") + col
    occ_local, vir_local = occ_orbitals.shape[0], vir_orbitals.shape[0]
    half_rows = cell_count // 2 // LANES
    own_y, own_x = col // RING_X, col % RING_X
    mate_block = (1 - grp) * lax.axis_size("col") + col
    places = [
        (own_y + RING_Y - dy) % RING_Y * RING_X + (own_x + RING_X - dx) % RING_X
        for dy, dx in OFFSETS
    ]
    place = jnp.stack(places).astype(jnp.int32)

    def order_of(col_index):
        same = col_index[:, None] == place[None, :]
        return jnp.sum(jnp.where(same, jnp.arange(8, dtype=jnp.int32), 0), axis=1)

    occ_near, occ_far = spread(occ_orbitals.reshape(occ_local, 2 * half_rows, LANES))
    occ_pieces = occ_near + occ_far
    mate_pairs = swap_core(pairs)
    vir_halves = vir_orbitals.reshape(vir_local, 2, half_rows, LANES)
    mate_vir = swap_core(lax.dynamic_index_in_dim(vir_halves, 1 - grp, 1, keepdims=True))

    own_pair = lax.dynamic_index_in_dim(pairs, batch_slot[block_index], 0, keepdims=False)
    mate_pair = lax.dynamic_index_in_dim(mate_pairs, batch_slot[mate_block], 0, keepdims=False)
    wanted = jnp.stack([own_pair[0], mate_pair[0]])
    wanted_place = order_of(wanted // occ_local % 8) * occ_local + wanted % occ_local
    picked = pick(wanted_place, occ_pieces)
    from_mate = swap_core(picked[1])
    own_occ = jnp.where(wanted[0] // occ_local // 8 == grp, picked[0], from_mate)
    own_vir = lax.dynamic_index_in_dim(
        vir_orbitals, own_pair[1] - block_index * vir_local, 0, keepdims=False
    )
    sigma = own_occ.reshape(planes, size_y, size_z) * own_vir
    columns = lax.all_to_all(
        planes_forward(sigma), "row", split_axis=1, concat_axis=0, tiled=True
    )
    field = lax.all_to_all(filter_columns(columns), "row", split_axis=0, concat_axis=1, tiled=True)
    potential = planes_back(field) + xc_kernel * sigma

    halves = potential.reshape(2, half_rows, LANES)
    kept = lax.dynamic_index_in_dim(halves, grp, 0, keepdims=True)
    moved = swap_core(lax.dynamic_index_in_dim(halves, 1 - grp, 0, keepdims=True))
    own_field = jnp.concatenate([kept, moved], axis=0)
    field_near, field_far = spread(own_field)

    def occ_half(half):
        parts = [
            lax.dynamic_slice_in_dim(part, half * half_rows, half_rows, 1) for part in occ_pieces
        ]
        return jnp.concatenate(parts, axis=0)

    own_occs, mate_occs = occ_half(grp), swap_core(occ_half(1 - grp))
    occ_index = jnp.concatenate([pairs[:, 0], mate_pairs[:, 0]])
    source = occ_index // occ_local
    occ_place = jnp.where(source // 8 == grp, 0, 8 * occ_local)
    occ_place = occ_place + order_of(source % 8) * occ_local + occ_index % occ_local
    densities, near = form_and_contract(
        occ_place,
        jnp.concatenate(
            [pairs[:, 1] - block_index * vir_local, mate_pairs[:, 1] - mate_block * vir_local]
        ),
        jnp.full((1,), grp, jnp.int32),
        own_occs,
        mate_occs,
        vir_halves,
        mate_vir,
        field_near,
    )
    far = contract(densities, field_far)

    pair_count = pairs.shape[0]
    sums = jnp.stack([near[0], far[0]]).reshape(2, 2, pair_count * 8)
    sums = sums.transpose(1, 0, 2)
    sums = jnp.where(grp == 0, sums, sums[::-1])
    sent = jnp.broadcast_to(sums[:, None], (2, row_count, 2, pair_count * 8))
    got = lax.all_to_all(
        sent.reshape(2 * row_count, 2, pair_count * 8), ("grp", "row"), 0, 0, tiled=True
    )
    got = jnp.sum(got.reshape(2, row_count, 2, pair_count, 4, 2), axis=1)
    got = got[0] + got[1][..., ::-1]
    got = got.transpose(1, 3, 0, 2).reshape(pair_count, 2, 8)
    chosen = place[:, None] == jnp.arange(8, dtype=jnp.int32)[None, :]
    ordered = jnp.sum(jnp.where(chosen, got[:, :, :, None], 0.0), axis=2)
    return ordered.reshape(pair_count, blocks) * scale


def solution(mesh):
    return jax.shard_map(
        on_device,
        mesh=mesh,
        in_specs=(
            P(BLOCK_AXES, "row", None, None),
            P(BLOCK_AXES, "row", None, None),
            P("row", None, None),
            P(BLOCK_AXES, None),
            P(),
        ),
        out_specs=P(BLOCK_AXES, None),
        check_vma=False,
    )
```

time: 219 us -> 200 us (0.913)
  blocking collectives: 30.7 us -> 0 us
  local copies, waits for them, and re-layouts: 14.7 us -> 30.2 us
  between operations: 15.5 us -> 7.64 us
  starting transfers between devices: 50.3 us -> 53.6 us
    all_to_all x1 -> x0, blocking collectives: 30.7 us -> none  [on_device(): lax.all_to_all(jnp.concatenate([chunks, note], axis=1), BLOCK_AXES, 0, 0,...]
    ppermute x8 -> x22, waiting for transfers between devices: 17 us -> 42.3 us  [shift_col(): return lax.ppermute(value, 'col', pairs)]
    all_gather x1 -> x0, waiting for transfers between devices: 16.1 us -> none  [on_device(): every_occ = lax.all_gather(occ_orbitals, BLOCK_AXES, axis=0, tiled=True)]
    unnamed x6 -> x20, local copies, waits for them, and re-layouts: 0.16 us -> 14.9 us
    ppermute x8 -> x22, starting transfers between devices: 20.4 us -> 31.6 us  [shift_col(): return lax.ppermute(value, 'col', pairs)]
    all_to_all x3 -> x2, waiting for transfers between devices: 34 us -> 23.5 us  [the longest x1 14.8 us: on_device(): lax.all_to_all(filter_columns(columns), 'row', split_axis=0, concat_axis=...]
    all_to_all x3 -> x2, starting transfers between devices: 20.9 us -> 15.8 us  [the longest x1 9.94 us: on_device(): lax.all_to_all(planes_forward(sigma), 'row', split_axis=1, concat_axis=0,...]
    all_to_all x1, starting transfers between devices: 8.83 us -> 5.8 us  [on_device(): lax.all_to_all(sent.reshape(2 * row_count, 2, pair_count * 8), ('grp', 'r...]
  transfers between devices with their start and end apart: 16 -> 30, of which waited for: 8 -> 12; matrix products, arithmetic and copies ran while one was open for 9% -> 19% of each run, Pallas kernels for 7% -> 7%
where the time goes in v3:
time: 200 us; the launch traced here: 198 us
  waiting for transfers between devices  74.5 us (37%)
  starting transfers between devices  53.6 us (27%)
  local copies, waits for them, and re-layouts  30.2 us (15%)
  Pallas kernels  22.3 us (11%)
  between operations  7.64 us (4%)
  matrix products  7.39 us (4%)
  other arithmetic  2.35 us (1%)
    ppermute x22, waiting for transfers between devices, shift_col(): return lax.ppermute(value, 'col', pairs)  42.3 us
    ppermute x22, starting transfers between devices, shift_col(): return lax.ppermute(value, 'col', pairs)  31.6 us
    unnamed x20, local copies, waits for them, and re-layouts  14.9 us
    all_to_all x1, waiting for transfers between devices, on_device(): lax.all_to_all(filter_columns(columns), 'row', split_axis=0, concat_axis=...  14.8 us
    pallas_call x1, Pallas kernels, form_and_contract(): pl.pallas_call(form_kernel, grid_spec=pltpu.PrefetchScalarGridSpec(num_sc...  12.8 us
    all_to_all x1, starting transfers between devices, on_device(): lax.all_to_all(planes_forward(sigma), 'row', split_axis=1, concat_axis=0,...  9.94 us
    all_to_all x1, waiting for transfers between devices, on_device(): lax.all_to_all(planes_forward(sigma), 'row', split_axis=1, concat_axis=0,...  8.74 us
    pallas_call x1, Pallas kernels, contract(): pl.pallas_call(contract_kernel, grid=(rows // TILE,), in_specs=[pl.BlockS...  7.57 us
  transfers between devices with their start and end apart: 30, of which 12 were waited for; matrix products, arithmetic and copies ran while one was open for 19% of the time, Pallas kernels for 7%

profile of v3, /device:TPU:2, one launch (start us, length us, event | category | flops | bytes accessed | tf_op | source)
XLA Modules:
  0.0 198.0 jit_solution(2083083617047781001)
XLA Ops:
  0.0 2.1 %collective-permute-start.5 = (f32[2,1024,128]{2,1,0:T(8,128)}, f32[2,1024,128]{2,1,0:T(8,128)}, u32[]{:S(2)}, u32[]{:S(2)}) collective-permute-start(f32[2,1024,128]{2,1,0:T(8,128)} %bitcast.92), channel_id=1, source_target_pairs={{0,1},{1,0},{2,3},{3,2},{4,5},{5,4},{6,7},{7,6},{8,9},{9,8},{10,11... | collective-permute-start | bytes 3145736 | tf_op jit(solution)/shard_map/ppermute | solution.py:67
  2.1 2.1 %fusion.58 = (f32[1,8,128,128]{3,2,1,0:T(8,128)S(1)}, f32[1,8,128,128]{3,2,1,0:T(8,128)}) fusion(f32[2,8,128,128]{3,2,1,0:T(8,128)} %param.5), kind=kLoop, calls=%fused_computation.144 | loop fusion | bytes 2097152 | tf_op jit(solution)/shard_map/slice | solution.py:74
  4.2 1.6 collective-permute-start.1
  5.8 1.7 collective-permute-start.4
  7.5 0.4 collective-permute-start.2
  7.8 1.4 fusion.61
  11.3 0.8 constant_dynamic-slice_fusion.3
  12.1 2.2 %dynamic-slice_dynamic-update-slice_fusion.3 = (f32[16,512,128]{2,1,0:T(8,128)}, f32[16,512,128]{2,1,0:T(8,128)}) fusion(f32[2,1024,128]{2,1,0:T(8,128)} %bitcast.93, s32[]{:T(128)S(6)} %select_n.264, s32[]{:T(128)S(6)} %select_n.263), kind=kLoop, calls=%fused_computation.20 | loop fusion | bytes 2097160
  14.3 6.2 %collective-permute-done.1.refs_1_ = f32[1,1024,128]{2,1,0:T(8,128)S(1)} collective-permute-done((f32[1,1024,128]{2,1,0:T(8,128)}, f32[1,1024,128]{2,1,0:T(8,128)S(1)}, u32[]{:S(2)}, u32[]{:S(2)}) %collective-permute-start.1) | collective-permute-done | bytes 524320 | tf_op jit(solution)/shard_map/ppermute | solution.py:67
  20.5 0.4 collective-permute-start.6
  20.9 2.9 %collective-permute-start.7 = (f32[1,1024,128]{2,1,0:T(8,128)S(1)}, f32[1,1024,128]{2,1,0:T(8,128)S(1)}, u32[]{:S(2)}, u32[]{:S(2)}) collective-permute-start(f32[1,1024,128]{2,1,0:T(8,128)S(1)} %collective-permute-done.4.refs_4_), channel_id=1, source_target_pairs={{0,6},{1,7},{2,0},{3,1},{4,2},{5,3},{6,4},{7,5},{8,14},{9,15},{10,... | collective-permute-start | bytes 1572872 | tf_op jit(solution)/shard_map/ppermute | solution.py:67
  23.7 3.0 %collective-permute-done.5.refs_5_ = f32[2,1024,128]{2,1,0:T(8,128)} collective-permute-done((f32[2,1024,128]{2,1,0:T(8,128)}, f32[2,1024,128]{2,1,0:T(8,128)}, u32[]{:S(2)}, u32[]{:S(2)}) %collective-permute-start.5) | collective-permute-done | bytes 1048608 | tf_op jit(solution)/shard_map/ppermute | solution.py:67
  26.7 1.6 collective-permute-start.8
  28.3 1.7 collective-permute-start.9
  30.0 0.6 fusion.60
  35.9 4.6 %constant_dynamic-slice_fusion.4 = f32[16,1,512,128]{3,2,1,0:T(8,128)} fusion(f32[16,2,512,128]{3,2,1,0:T(8,128)} %bitcast.90, s32[]{:T(128)S(6)} %select_n.265), kind=kLoop, calls=%fused_computation.74 | loop fusion | bytes 8388612 | tf_op jit(solution)/shard_map/jit(dynamic_index_in_dim)/dynamic_slice | solution.py:284
  40.6 0.6 slice.63
  41.1 1.4 and_select_fusion.3
  42.5 1.9 collective-permute-start.3
  44.4 2.1 %collective-permute-start.10 = (f32[1,1024,128]{2,1,0:T(8,128)S(1)}, f32[1,1024,128]{2,1,0:T(8,128)S(1)}, u32[]{:S(2)}, u32[]{:S(2)}) collective-permute-start(f32[1,1024,128]{2,1,0:T(8,128)S(1)} %collective-permute-done.6.refs_6_), channel_id=1, source_target_pairs={{0,1},{1,0},{2,3},{3,2},{4,5},{5,4},{6,7},{7,6},{8,9},{9,8},{10,11... | collective-permute-start | bytes 1572872 | tf_op jit(solution)/shard_map/ppermute | solution.py:67
  46.6 1.4 collective-permute-start.11
  48.1 0.8 dynamic-slice_dynamic-update-slice_fusion.15
  49.0 0.8 dynamic-slice_dynamic-update-slice_fusion.14
  49.8 16.1 %collective-permute-done.3.refs_3_ = f32[1,1024,128]{2,1,0:T(8,128)S(1)} collective-permute-done((f32[1,1024,128]{2,1,0:T(8,128)}, f32[1,1024,128]{2,1,0:T(8,128)S(1)}, u32[]{:S(2)}, u32[]{:S(2)}) %collective-permute-start.3) | collective-permute-done | bytes 524320 | tf_op jit(solution)/shard_map/ppermute | solution.py:67
  65.9 3.2 %collective-permute-done.11.refs_11_ = f32[1,1024,128]{2,1,0:T(8,128)S(1)} collective-permute-done((f32[1,1024,128]{2,1,0:T(8,128)S(1)}, f32[1,1024,128]{2,1,0:T(8,128)S(1)}, u32[]{:S(2)}, u32[]{:S(2)}) %collective-permute-start.11) | collective-permute-done | bytes 524320 | tf_op jit(solution)/shard_map/ppermute | solution.py:67
  69.1 1.9 pick_occ.1
  71.4 0.8 dynamic-slice_dynamic-update-slice_fusion.13
  72.2 0.8 dynamic-slice_dynamic-update-slice_fusion.12
  73.0 2.2 %dynamic-slice_dynamic-update-slice_fusion.2 = (f32[16,512,128]{2,1,0:T(8,128)}, f32[16,512,128]{2,1,0:T(8,128)}) fusion(f32[16,512,128]{2,1,0:T(8,128)} %get-tuple-element.33, f32[2,1024,128]{2,1,0:T(8,128)} %collective-permute-done.5.refs_5_, s32[]{:T(128)S(6)} %select_n.264, f32[16,512,128]{2,1,0:T(8,128)} %get-tuple-element.34, s32[]{:T(128)S(6)} %select_n.263), kind=kLoop, calls=%fused_computation.19 | loop fusion | bytes 2097160
  75.3 0.8 dynamic-slice_dynamic-update-slice_fusion.11
  76.1 0.8 dynamic-slice_dynamic-update-slice_fusion.10
  77.0 1.9 fusion.6
  78.9 0.9 convolution_bitcast_fusion.1
  79.8 1.1 copy.74
  80.9 9.9 %all-to-all-start = ((f32[8,128,128]{2,0,1:T(8,128)}), f32[8,128,128]{2,0,1:T(8,128)S(1)}, u32[]{:S(2)}, u32[]{:S(2)}) async-start(f32[8,128,128]{2,0,1:T(8,128)} %copy.74), calls=%async_computation | async-start | bytes 1048576 | tf_op jit(solution)/shard_map/all_to_all | solution.py:297
  90.9 2.3 %dynamic-slice_dynamic-update-slice_fusion.1 = (f32[16,512,128]{2,1,0:T(8,128)}, f32[16,512,128]{2,1,0:T(8,128)}) fusion(f32[16,512,128]{2,1,0:T(8,128)} %get-tuple-element.29, f32[2,1024,128]{2,1,0:T(8,128)} %collective-permute-done.8.refs_8_, s32[]{:T(128)S(6)} %select_n.264, f32[16,512,128]{2,1,0:T(8,128)} %get-tuple-element.30, s32[]{:T(128)S(6)} %select_n.263), kind=kLoop, calls=%fused_computation.18 | loop fusion | bytes 2097160
  93.1 2.2 %dynamic-slice_dynamic-update-slice_fusion = (f32[16,512,128]{2,1,0:T(8,128)}, f32[16,512,128]{2,1,0:T(8,128)}) fusion(f32[16,512,128]{2,1,0:T(8,128)} %get-tuple-element.15, f32[2,1024,128]{2,1,0:T(8,128)} %collective-permute-done.9.refs_9_, s32[]{:T(128)S(6)} %select_n.264, f32[16,512,128]{2,1,0:T(8,128)} %get-tuple-element.16, s32[]{:T(128)S(6)} %select_n.263), kind=kLoop, calls=%fused_computation.17 | loop fusion | bytes 2097160
  95.4 0.8 dynamic-slice_dynamic-update-slice_fusion.9
  96.2 0.9 dynamic-slice_dynamic-update-slice_fusion.8
  97.2 8.7 %all-to-all-done = f32[8,128,128]{2,0,1:T(8,128)S(1)} async-done(((f32[8,128,128]{2,0,1:T(8,128)}), f32[8,128,128]{2,0,1:T(8,128)S(1)}, u32[]{:S(2)}, u32[]{:S(2)}) %all-to-all-start) | async-done | bytes 524320 | tf_op jit(solution)/shard_map/all_to_all | solution.py:297
  106.0 0.9 convolution_multiply_fusion.1
  106.9 0.9 fusion.14
  107.8 1.1 copy.80
  109.0 5.9 %all-to-all-start.1 = ((f32[128,8,128]{2,1,0:T(8,128)}), f32[128,8,128]{2,1,0:T(8,128)S(1)}, u32[]{:S(2)}, u32[]{:S(2)}) async-start(f32[128,8,128]{2,1,0:T(8,128)} %copy.80), calls=%async_computation.1 | async-start | bytes 1048576 | tf_op jit(solution)/shard_map/all_to_all | solution.py:300
  114.8 14.8 %all-to-all-done.1 = f32[128,8,128]{2,1,0:T(8,128)S(1)} async-done(((f32[128,8,128]{2,1,0:T(8,128)}), f32[128,8,128]{2,1,0:T(8,128)S(1)}, u32[]{:S(2)}, u32[]{:S(2)}) %all-to-all-start.1) | async-done | bytes 524320 | tf_op jit(solution)/shard_map/all_to_all | solution.py:300
  129.6 0.9 convolution_bitcast_fusion
  130.5 1.9 multiply_add_fusion
  132.7 1.4 collective-permute-done.15
  134.1 2.0 %collective-permute-start.20 = (f32[2,512,128]{2,1,0:T(8,128)S(1)}, f32[2,512,128]{2,1,0:T(8,128)S(1)}, u32[]{:S(2)}, u32[]{:S(2)}) collective-permute-start(f32[2,512,128]{2,1,0:T(8,128)S(1)} %pad_maximum_fusion.refs_0_), channel_id=1, source_target_pairs={{0,1},{1,0},{2,3},{3,2},{4,5},{5,4},{6,7},{7,6},{8,9},{9,8},{10,11... | collective-permute-start | bytes 1572872 | tf_op jit(solution)/shard_map/ppermute | solution.py:67
  136.2 1.8 collective-permute-start.18
  138.0 4.5 %collective-permute-done.16.refs_1_ = f32[1,512,128]{2,1,0:T(8,128)S(1)} collective-permute-done((f32[1,512,128]{2,1,0:T(8,128)S(1)}, f32[1,512,128]{2,1,0:T(8,128)S(1)}, u32[]{:S(2)}, u32[]{:S(2)}) %collective-permute-start.16) | collective-permute-done | bytes 262176 | tf_op jit(solution)/shard_map/ppermute | solution.py:67
  142.5 2.8 %collective-permute-done.18.refs_3_ = f32[1,512,128]{2,1,0:T(8,128)S(1)} collective-permute-done((f32[1,512,128]{2,1,0:T(8,128)S(1)}, f32[1,512,128]{2,1,0:T(8,128)S(1)}, u32[]{:S(2)}, u32[]{:S(2)}) %collective-permute-start.18) | collective-permute-done | bytes 262176 | tf_op jit(solution)/shard_map/ppermute | solution.py:67
  145.6 4.2 %collective-permute-done.19.refs_4_ = f32[1,512,128]{2,1,0:T(8,128)S(1)} collective-permute-done((f32[1,512,128]{2,1,0:T(8,128)S(1)}, f32[1,512,128]{2,1,0:T(8,128)S(1)}, u32[]{:S(2)}, u32[]{:S(2)}) %collective-permute-start.19) | collective-permute-done | bytes 262176 | tf_op jit(solution)/shard_map/ppermute | solution.py:67
  149.9 3.0 %collective-permute-start.22 = (f32[1,512,128]{2,1,0:T(8,128)S(1)}, f32[1,512,128]{2,1,0:T(8,128)S(1)}, u32[]{:S(2)}, u32[]{:S(2)}) collective-permute-start(f32[1,512,128]{2,1,0:T(8,128)S(1)} %collective-permute-done.19.refs_4_), channel_id=1, source_target_pairs={{0,6},{1,7},{2,0},{3,1},{4,2},{5,3},{6,4},{7,5},{8,14},{9,15},{10,... | collective-permute-start | bytes 786440 | tf_op jit(solution)/shard_map/ppermute | solution.py:67
  152.9 3.2 %collective-permute-start.24 = (f32[2,512,128]{2,1,0:T(8,128)S(1)}, f32[2,512,128]{2,1,0:T(8,128)S(1)}, u32[]{:S(2)}, u32[]{:S(2)}) collective-permute-start(f32[2,512,128]{2,1,0:T(8,128)S(1)} %collective-permute-done.20.refs_5_), channel_id=1, source_target_pairs={{0,6},{1,7},{2,0},{3,1},{4,2},{5,3},{6,4},{7,5},{8,14},{9,15},{10,... | collective-permute-start | bytes 1572872 | tf_op jit(solution)/shard_map/ppermute | solution.py:67
  156.3 2.2 %collective-permute-done.21.refs_0_ = f32[1,512,128]{2,1,0:T(8,128)S(1)} collective-permute-done((f32[1,512,128]{2,1,0:T(8,128)S(1)}, f32[1,512,128]{2,1,0:T(8,128)S(1)}, u32[]{:S(2)}, u32[]{:S(2)}) %collective-permute-start.21) | collective-permute-done | bytes 262176 | tf_op jit(solution)/shard_map/ppermute | solution.py:67
  158.5 2.0 collective-permute-start.25
  160.5 1.6 collective-permute-start.26
  162.2 12.8 %form_and_contract.1 = (f32[32,512,128]{2,1,0:T(8,128)}, f32[8,256]{1,0:T(8,128)S(1)}) custom-call(s32[32]{0:T(128)S(1)} %fusion.28.occ_index, s32[32]{0:T(128)S(1)} %pad_add_fusion.1.vir_index, s32[1]{0:T(128)} %bitcast.12.half, f32[16,512,128]{2,1,0:T(8,128)} %get-tuple-element.26.own_occ, f32[16,512,128]{2,1,0:T(8,128)} %collective-permute-done.12.mate_occ, ...), custom_call_target="tpu_custom_call" | custom-call | flops 35651584 | bytes 27262976 | tf_op jit(solution)/shard_map/form_and_contract/pallas_call | solution.py:206
  175.1 7.6 %contract.1 = f32[8,256]{1,0:T(8,128)S(1)} custom-call(f32[32,512,128]{2,1,0:T(8,128)} %get-tuple-element.8.density_ref, f32[1,512,128]{2,1,0:T(8,128)S(1)} %collective-permute-done.21.refs_0_, f32[1,512,128]{2,1,0:T(8,128)S(1)} %collective-permute-done.22.refs_1_, f32[2,512,128]{2,1,0:T(8,128)S(1)} %collective-permute-done.23.refs_2_, ...), custom_call_target="tpu_custom_call" | custom-call | flops 33554432 | bytes 10485760 | tf_op jit(solution)/shard_map/contract/pallas_call | solution.py:241
  182.8 0.6 copy.83
  183.4 5.8 %all-to-all-start.2 = ((f32[32,2,128]{2,1,0:T(2,128)}), f32[32,2,128]{2,1,0:T(2,128)S(1)}, u32[]{:S(2)}, u32[]{:S(2)}) async-start(f32[32,2,128]{2,1,0:T(2,128)} %copy.83), calls=%async_computation.2 | async-start | bytes 65536 | tf_op jit(solution)/shard_map/all_to_all | solution.py:339
  189.3 7.2 %all-to-all-done.2 = f32[32,2,128]{2,1,0:T(2,128)S(1)} async-done(((f32[32,2,128]{2,1,0:T(2,128)}), f32[32,2,128]{2,1,0:T(2,128)S(1)}, u32[]{:S(2)}, u32[]{:S(2)}) %all-to-all-start.2) | async-done | bytes 32800 | tf_op jit(solution)/shard_map/all_to_all | solution.py:339
  197.3 0.7 copy.88
  (71 shorter events, 2.9 us)
Async XLA Ops:
  0.0 26.7 %collective-permute-start.5 = (f32[2,1024,128]{2,1,0:T(8,128)}, f32[2,1024,128]{2,1,0:T(8,128)}, u32[]{:S(2)}, u32[]{:S(2)}) collective-permute-start(f32[2,1024,128]{2,1,0:T(8,128)} %bitcast.92), channel_id=1, source_target_pairs={{0,1},{1,0},{2,3},{3,2},{4,5},{5,4},{6,7},{7,6},{8,9},{9,8},{10,11... | collective-permute-start | bytes 3145736 | tf_op jit(solution)/shard_map/ppermute | solution.py:67
  4.2 16.3 %collective-permute-start.1 = (f32[1,1024,128]{2,1,0:T(8,128)}, f32[1,1024,128]{2,1,0:T(8,128)S(1)}, u32[]{:S(2)}, u32[]{:S(2)}) collective-permute-start(f32[1,1024,128]{2,1,0:T(8,128)} %bitcast.14), channel_id=1, source_target_pairs={{0,2},{1,3},{2,4},{3,5},{4,6},{5,7},{6,0},{7,1},{8,10},{9,11},{10,... | collective-permute-start | bytes 1572872 | tf_op jit(solution)/shard_map/ppermute | solution.py:67
  5.8 15.1 %collective-permute-start.4 = (f32[1,1024,128]{2,1,0:T(8,128)S(1)}, f32[1,1024,128]{2,1,0:T(8,128)S(1)}, u32[]{:S(2)}, u32[]{:S(2)}) collective-permute-start(f32[1,1024,128]{2,1,0:T(8,128)S(1)} %bitcast.102), channel_id=1, source_target_pairs={{0,6},{1,7},{2,0},{3,1},{4,2},{5,3},{6,4},{7,5},{8,14},{9,15},{10,... | collective-permute-start | bytes 1572872 | tf_op jit(solution)/shard_map/ppermute | solution.py:67
  7.5 35.1 %collective-permute-start.2 = (f32[1,1024,128]{2,1,0:T(8,128)S(1)}, f32[1,1024,128]{2,1,0:T(8,128)S(1)}, u32[]{:S(2)}, u32[]{:S(2)}) collective-permute-start(f32[1,1024,128]{2,1,0:T(8,128)S(1)} %bitcast.103), channel_id=1, source_target_pairs={{0,2},{1,3},{2,4},{3,5},{4,6},{5,7},{6,0},{7,1},{8,10},{9,11},{10,... | collective-permute-start | bytes 1572872 | tf_op jit(solution)/shard_map/ppermute | solution.py:67
  7.8 20.5 %collective-permute-start = (s32[16,2]{0,1:T(2,128)}, s32[16,2]{0,1:T(2,128)S(1)}, u32[]{:S(2)}, u32[]{:S(2)}) collective-permute-start(s32[16,2]{0,1:T(2,128)} %param.8), channel_id=1, source_target_pairs={{0,128},{128,0},{1,129},{129,1},{2,130},{130,2},{3,131},{131,3},{4... | collective-permute-start | bytes 392 | tf_op jit(solution)/shard_map/ppermute | solution.py:86
  20.5 23.9 %collective-permute-start.6 = (f32[1,1024,128]{2,1,0:T(8,128)S(1)}, f32[1,1024,128]{2,1,0:T(8,128)S(1)}, u32[]{:S(2)}, u32[]{:S(2)}) collective-permute-start(f32[1,1024,128]{2,1,0:T(8,128)S(1)} %collective-permute-done.1.refs_1_), channel_id=1, source_target_pairs={{0,2},{1,3},{2,4},{3,5},{4,6},{5,7},{6,0},{7,1},{8,10},{9,11},{10,... | collective-permute-start | bytes 1572872 | tf_op jit(solution)/shard_map/ppermute | solution.py:67
  20.9 25.7 %collective-permute-start.7 = (f32[1,1024,128]{2,1,0:T(8,128)S(1)}, f32[1,1024,128]{2,1,0:T(8,128)S(1)}, u32[]{:S(2)}, u32[]{:S(2)}) collective-permute-start(f32[1,1024,128]{2,1,0:T(8,128)S(1)} %collective-permute-done.4.refs_4_), channel_id=1, source_target_pairs={{0,6},{1,7},{2,0},{3,1},{4,2},{5,3},{6,4},{7,5},{8,14},{9,15},{10,... | collective-permute-start | bytes 1572872 | tf_op jit(solution)/shard_map/ppermute | solution.py:67
  26.7 42.4 %collective-permute-start.8 = (f32[2,1024,128]{2,1,0:T(8,128)}, f32[2,1024,128]{2,1,0:T(8,128)}, u32[]{:S(2)}, u32[]{:S(2)}) collective-permute-start(f32[2,1024,128]{2,1,0:T(8,128)} %collective-permute-done.5.refs_5_), channel_id=1, source_target_pairs={{0,2},{1,3},{2,4},{3,5},{4,6},{5,7},{6,0},{7,1},{8,10},{9,11},{10,... | collective-permute-start | bytes 3145736 | tf_op jit(solution)/shard_map/ppermute | solution.py:67
  28.3 40.8 %collective-permute-start.9 = (f32[2,1024,128]{2,1,0:T(8,128)}, f32[2,1024,128]{2,1,0:T(8,128)}, u32[]{:S(2)}, u32[]{:S(2)}) collective-permute-start(f32[2,1024,128]{2,1,0:T(8,128)} %collective-permute-done.5.refs_5_), channel_id=1, source_target_pairs={{0,6},{1,7},{2,0},{3,1},{4,2},{5,3},{6,4},{7,5},{8,14},{9,15},{10,... | collective-permute-start | bytes 3145736 | tf_op jit(solution)/shard_map/ppermute | solution.py:67
  42.5 23.4 %collective-permute-start.3 = (f32[1,1024,128]{2,1,0:T(8,128)}, f32[1,1024,128]{2,1,0:T(8,128)S(1)}, u32[]{:S(2)}, u32[]{:S(2)}) collective-permute-start(f32[1,1024,128]{2,1,0:T(8,128)} %bitcast.14), channel_id=1, source_target_pairs={{0,6},{1,7},{2,0},{3,1},{4,2},{5,3},{6,4},{7,5},{8,14},{9,15},{10,... | collective-permute-start | bytes 1572872 | tf_op jit(solution)/shard_map/ppermute | solution.py:67
  44.4 21.5 %collective-permute-start.10 = (f32[1,1024,128]{2,1,0:T(8,128)S(1)}, f32[1,1024,128]{2,1,0:T(8,128)S(1)}, u32[]{:S(2)}, u32[]{:S(2)}) collective-permute-start(f32[1,1024,128]{2,1,0:T(8,128)S(1)} %collective-permute-done.6.refs_6_), channel_id=1, source_target_pairs={{0,1},{1,0},{2,3},{3,2},{4,5},{5,4},{6,7},{7,6},{8,9},{9,8},{10,11... | collective-permute-start | bytes 1572872 | tf_op jit(solution)/shard_map/ppermute | solution.py:67
  46.6 22.6 %collective-permute-start.11 = (f32[1,1024,128]{2,1,0:T(8,128)S(1)}, f32[1,1024,128]{2,1,0:T(8,128)S(1)}, u32[]{:S(2)}, u32[]{:S(2)}) collective-permute-start(f32[1,1024,128]{2,1,0:T(8,128)S(1)} %collective-permute-done.7.refs_7_), channel_id=1, source_target_pairs={{0,1},{1,0},{2,3},{3,2},{4,5},{5,4},{6,7},{7,6},{8,9},{9,8},{10,11... | collective-permute-start | bytes 1572872 | tf_op jit(solution)/shard_map/ppermute | solution.py:67
  65.9 72.0 %collective-permute-start.13 = (f32[16,1,512,128]{3,2,1,0:T(8,128)}, f32[16,1,512,128]{3,2,1,0:T(8,128)}, u32[]{:S(2)}, u32[]{:S(2)}) collective-permute-start(f32[16,1,512,128]{3,2,1,0:T(8,128)} %constant_dynamic-slice_fusion.4), channel_id=1, source_target_pairs={{0,128},{128,0},{1,129},{129,1},{2,130},{130,2},{3,131},{131,3},{4... | collective-permute-start | bytes 12582920 | tf_op jit(solution)/shard_map/ppermute | solution.py:86
  65.9 5.1 %copy-start = (f32[1,1024,128]{2,1,0:T(8,128)}, f32[1,1024,128]{2,1,0:T(8,128)S(1)}, u32[]{:S(2)}) copy-start(f32[1,1024,128]{2,1,0:T(8,128)S(1)} %collective-permute-done.10.refs_10_) | copy-start | bytes 1572868
  71.1 5.8 %collective-permute-start.14 = (f32[1024,128]{1,0:T(8,128)S(1)}, f32[1024,128]{1,0:T(8,128)S(1)}, u32[]{:S(2)}, u32[]{:S(2)}) collective-permute-start(f32[1024,128]{1,0:T(8,128)S(1)} %slice_bitcast_fusion), channel_id=1, source_target_pairs={{0,128},{128,0},{1,129},{129,1},{2,130},{130,2},{3,131},{131,3},{4... | collective-permute-start | bytes 1572872 | tf_op jit(solution)/shard_map/ppermute | solution.py:86
  77.0 18.4 %copy-start.1 = (f32[1,1024,128]{2,1,0:T(8,128)S(1)}, f32[1,1024,128]{2,1,0:T(8,128)}, u32[]{:S(2)}) copy-start(f32[1,1024,128]{2,1,0:T(8,128)} %copy-done) | copy-start | bytes 1572868
  80.9 25.0 %all-to-all-start = ((f32[8,128,128]{2,0,1:T(8,128)}), f32[8,128,128]{2,0,1:T(8,128)S(1)}, u32[]{:S(2)}, u32[]{:S(2)}) async-start(f32[8,128,128]{2,0,1:T(8,128)} %copy.74), calls=%async_computation | async-start | bytes 1048576 | tf_op jit(solution)/shard_map/all_to_all | solution.py:297
  97.1 33.4 %copy-start.2 = (f32[8,128,128]{2,1,0:T(8,128)S(1)}, f32[8,128,128]{2,1,0:T(8,128)}, u32[]{:S(2)}) copy-start(f32[8,128,128]{2,1,0:T(8,128)} %param.7) | copy-start | bytes 1572868
  97.1 65.2 %collective-permute-start.12 = (f32[16,512,128]{2,1,0:T(8,128)}, f32[16,512,128]{2,1,0:T(8,128)}, u32[]{:S(2)}, u32[]{:S(2)}) collective-permute-start(f32[16,512,128]{2,1,0:T(8,128)} %get-tuple-element.25), channel_id=1, source_target_pairs={{0,128},{128,0},{1,129},{129,1},{2,130},{130,2},{3,131},{131,3},{4... | collective-permute-start | bytes 12582920 | tf_op jit(solution)/shard_map/ppermute | solution.py:86
  107.8 34.7 %copy-start.3 = (s32[16,2]{0,1:T(2,128)S(1)}, s32[16,2]{0,1:T(2,128)}, u32[]{:S(2)}) copy-start(s32[16,2]{0,1:T(2,128)} %param.8) | copy-start | bytes 388
  109.0 20.7 %all-to-all-start.1 = ((f32[128,8,128]{2,1,0:T(8,128)}), f32[128,8,128]{2,1,0:T(8,128)S(1)}, u32[]{:S(2)}, u32[]{:S(2)}) async-start(f32[128,8,128]{2,1,0:T(8,128)} %copy.80), calls=%async_computation.1 | async-start | bytes 1048576 | tf_op jit(solution)/shard_map/all_to_all | solution.py:300
  132.5 1.6 collective-permute-start.15
  132.6 9.9 %collective-permute-start.16 = (f32[1,512,128]{2,1,0:T(8,128)S(1)}, f32[1,512,128]{2,1,0:T(8,128)S(1)}, u32[]{:S(2)}, u32[]{:S(2)}) collective-permute-start(f32[1,512,128]{2,1,0:T(8,128)S(1)} %get-tuple-element.23), channel_id=1, source_target_pairs={{0,2},{1,3},{2,4},{3,5},{4,6},{5,7},{6,0},{7,1},{8,10},{9,11},{10,... | collective-permute-start | bytes 786440 | tf_op jit(solution)/shard_map/ppermute | solution.py:67
  134.1 18.8 %collective-permute-start.20 = (f32[2,512,128]{2,1,0:T(8,128)S(1)}, f32[2,512,128]{2,1,0:T(8,128)S(1)}, u32[]{:S(2)}, u32[]{:S(2)}) collective-permute-start(f32[2,512,128]{2,1,0:T(8,128)S(1)} %pad_maximum_fusion.refs_0_), channel_id=1, source_target_pairs={{0,1},{1,0},{2,3},{3,2},{4,5},{5,4},{6,7},{7,6},{8,9},{9,8},{10,11... | collective-permute-start | bytes 1572872 | tf_op jit(solution)/shard_map/ppermute | solution.py:67
  136.2 9.2 %collective-permute-start.18 = (f32[1,512,128]{2,1,0:T(8,128)S(1)}, f32[1,512,128]{2,1,0:T(8,128)S(1)}, u32[]{:S(2)}, u32[]{:S(2)}) collective-permute-start(f32[1,512,128]{2,1,0:T(8,128)S(1)} %get-tuple-element.23), channel_id=1, source_target_pairs={{0,6},{1,7},{2,0},{3,1},{4,2},{5,3},{6,4},{7,5},{8,14},{9,15},{10,... | collective-permute-start | bytes 786440 | tf_op jit(solution)/shard_map/ppermute | solution.py:67
  138.0 11.9 %collective-permute-start.19 = (f32[1,512,128]{2,1,0:T(8,128)S(1)}, f32[1,512,128]{2,1,0:T(8,128)S(1)}, u32[]{:S(2)}, u32[]{:S(2)}) collective-permute-start(f32[1,512,128]{2,1,0:T(8,128)S(1)} %collective-permute-done.15), channel_id=1, source_target_pairs={{0,6},{1,7},{2,0},{3,1},{4,2},{5,3},{6,4},{7,5},{8,14},{9,15},{10,... | collective-permute-start | bytes 786440 | tf_op jit(solution)/shard_map/ppermute | solution.py:67
  142.5 10.4 %collective-permute-start.17 = (f32[1,512,128]{2,1,0:T(8,128)S(1)}, f32[1,512,128]{2,1,0:T(8,128)S(1)}, u32[]{:S(2)}, u32[]{:S(2)}) collective-permute-start(f32[1,512,128]{2,1,0:T(8,128)S(1)} %collective-permute-done.15), channel_id=1, source_target_pairs={{0,2},{1,3},{2,4},{3,5},{4,6},{5,7},{6,0},{7,1},{8,10},{9,11},{10,... | collective-permute-start | bytes 786440 | tf_op jit(solution)/shard_map/ppermute | solution.py:67
  145.4 13.2 %collective-permute-start.21 = (f32[1,512,128]{2,1,0:T(8,128)S(1)}, f32[1,512,128]{2,1,0:T(8,128)S(1)}, u32[]{:S(2)}, u32[]{:S(2)}) collective-permute-start(f32[1,512,128]{2,1,0:T(8,128)S(1)} %collective-permute-done.16.refs_1_), channel_id=1, source_target_pairs={{0,2},{1,3},{2,4},{3,5},{4,6},{5,7},{6,0},{7,1},{8,10},{9,11},{10,... | collective-permute-start | bytes 786440 | tf_op jit(solution)/shard_map/ppermute | solution.py:67
  149.9 10.7 %collective-permute-start.22 = (f32[1,512,128]{2,1,0:T(8,128)S(1)}, f32[1,512,128]{2,1,0:T(8,128)S(1)}, u32[]{:S(2)}, u32[]{:S(2)}) collective-permute-start(f32[1,512,128]{2,1,0:T(8,128)S(1)} %collective-permute-done.19.refs_4_), channel_id=1, source_target_pairs={{0,6},{1,7},{2,0},{3,1},{4,2},{5,3},{6,4},{7,5},{8,14},{9,15},{10,... | collective-permute-start | bytes 786440 | tf_op jit(solution)/shard_map/ppermute | solution.py:67
  152.9 22.2 %collective-permute-start.23 = (f32[2,512,128]{2,1,0:T(8,128)S(1)}, f32[2,512,128]{2,1,0:T(8,128)S(1)}, u32[]{:S(2)}, u32[]{:S(2)}) collective-permute-start(f32[2,512,128]{2,1,0:T(8,128)S(1)} %collective-permute-done.20.refs_5_), channel_id=1, source_target_pairs={{0,2},{1,3},{2,4},{3,5},{4,6},{5,7},{6,0},{7,1},{8,10},{9,11},{10,... | collective-permute-start | bytes 1572872 | tf_op jit(solution)/shard_map/ppermute | solution.py:67
  152.9 22.2 %collective-permute-start.24 = (f32[2,512,128]{2,1,0:T(8,128)S(1)}, f32[2,512,128]{2,1,0:T(8,128)S(1)}, u32[]{:S(2)}, u32[]{:S(2)}) collective-permute-start(f32[2,512,128]{2,1,0:T(8,128)S(1)} %collective-permute-done.20.refs_5_), channel_id=1, source_target_pairs={{0,6},{1,7},{2,0},{3,1},{4,2},{5,3},{6,4},{7,5},{8,14},{9,15},{10,... | collective-permute-start | bytes 1572872 | tf_op jit(solution)/shard_map/ppermute | solution.py:67
  158.5 16.5 %collective-permute-start.25 = (f32[1,512,128]{2,1,0:T(8,128)S(1)}, f32[1,512,128]{2,1,0:T(8,128)S(1)}, u32[]{:S(2)}, u32[]{:S(2)}) collective-permute-start(f32[1,512,128]{2,1,0:T(8,128)S(1)} %collective-permute-done.21.refs_0_), channel_id=1, source_target_pairs={{0,1},{1,0},{2,3},{3,2},{4,5},{5,4},{6,7},{7,6},{8,9},{9,8},{10,11... | collective-permute-start | bytes 786440 | tf_op jit(solution)/shard_map/ppermute | solution.py:67
  160.5 14.6 %collective-permute-start.26 = (f32[1,512,128]{2,1,0:T(8,128)S(1)}, f32[1,512,128]{2,1,0:T(8,128)S(1)}, u32[]{:S(2)}, u32[]{:S(2)}) collective-permute-start(f32[1,512,128]{2,1,0:T(8,128)S(1)} %collective-permute-done.22.refs_1_), channel_id=1, source_target_pairs={{0,1},{1,0},{2,3},{3,2},{4,5},{5,4},{6,7},{7,6},{8,9},{9,8},{10,11... | collective-permute-start | bytes 786440 | tf_op jit(solution)/shard_map/ppermute | solution.py:67
  183.4 13.1 %all-to-all-start.2 = ((f32[32,2,128]{2,1,0:T(2,128)}), f32[32,2,128]{2,1,0:T(2,128)S(1)}, u32[]{:S(2)}, u32[]{:S(2)}) async-start(f32[32,2,128]{2,1,0:T(2,128)} %copy.83), calls=%async_computation.2 | async-start | bytes 65536 | tf_op jit(solution)/shard_map/all_to_all | solution.py:339

commit v4 on v3

v4 whole, which is shorter than its diff:
```python
import jax
import jax.numpy as jnp
import numpy as np
from jax import lax
from jax.experimental import pallas as pl
from jax.experimental.pallas import tpu as pltpu
from jax.sharding import PartitionSpec as P

COULOMB = 0.4
LANES = 128
BLOCK_AXES = ("grp", "col")
VMEM_BYTES = 48 * 1024 * 1024


def cas_table(length):
    indices = np.arange(length)
    angles = indices[:, None] * indices[None, :] % length * (2.0 * np.pi / length)
    return jnp.asarray((np.cos(angles) + np.sin(angles)).astype(np.float32))


def dot_exact(left, right):
    return jnp.dot(left, right, precision=lax.Precision.HIGHEST, preferred_element_type=jnp.float32)


def forward_kernel(flag_ref, vir_place, own_occ, mate_occ, vir_ref, cas_ref, sigma_ref, out_ref):
    planes, length, _ = sigma_ref.shape
    cas = cas_ref[...]
    left = jnp.where(flag_ref[0] != 0, own_occ[...], mate_occ[...])
    sigma = left.reshape(sigma_ref.shape) * vir_ref[0]
    sigma_ref[...] = sigma
    field = dot_exact(sigma.reshape(planes * length, length), cas).reshape(sigma.shape)
    field = jnp.stack([dot_exact(cas, field[x]) for x in range(planes)])
    out_ref[...] = jnp.swapaxes(field, 0, 1)


def forward(flag, vir_place, own_occ, mate_occ, vir, cas):
    _, planes, length, _ = vir.shape
    whole = pl.BlockSpec(memory_space=pltpu.VMEM)
    return pl.pallas_call(
        forward_kernel,
        grid_spec=pltpu.PrefetchScalarGridSpec(
            num_scalar_prefetch=2,
            grid=(1,),
            in_specs=[
                whole,
                whole,
                pl.BlockSpec((1, planes, length, length), lambda i, f, v: (v[0], 0, 0, 0)),
                whole,
            ],
            out_specs=[whole, whole],
        ),
        out_shape=[
            jax.ShapeDtypeStruct((planes, length, length), jnp.float32),
            jax.ShapeDtypeStruct((length, planes, length), jnp.float32),
        ],
        compiler_params=pltpu.CompilerParams(vmem_limit_bytes=VMEM_BYTES),
        name="forward",
    )(flag, vir_place, own_occ, mate_occ, vir, cas)


def filter_kernel(first_ref, in_ref, cas_ref, out_ref):
    blocks, width, part, length = in_ref.shape
    cas = cas_ref[...]

    def square(index):
        signed = jnp.where(index >= length // 2, index - length, index)
        return (signed * signed).astype(jnp.float32)

    side = square(lax.broadcasted_iota(jnp.int32, (length, length), 0))
    side = side + square(lax.broadcasted_iota(jnp.int32, (length, length), 1))
    for v in range(width):
        column = dot_exact(cas, in_ref[:, v].reshape(length, length))
        squared_sum = side + square(first_ref[0] + v + jnp.zeros((1, length), jnp.int32))
        factor = jnp.where(squared_sum > 0, COULOMB / jnp.maximum(squared_sum, 1.0), 0.0)
        out_ref[:, v] = dot_exact(cas, column * factor).reshape(blocks, part, length)


def filter_columns(first, columns, cas):
    return pl.pallas_call(
        filter_kernel,
        out_shape=jax.ShapeDtypeStruct(columns.shape, jnp.float32),
        in_specs=[pl.BlockSpec(memory_space=pltpu.SMEM)]
        + [pl.BlockSpec(memory_space=pltpu.VMEM)] * 2,
        out_specs=pl.BlockSpec(memory_space=pltpu.VMEM),
        compiler_params=pltpu.CompilerParams(vmem_limit_bytes=VMEM_BYTES),
        name="filter_columns",
    )(first, columns, cas)


def back_kernel(half_ref, in_ref, sigma_ref, xc_ref, cas_ref, kept_ref, given_ref, held):
    length, planes, _ = in_ref.shape
    cas = cas_ref[...]
    field = dot_exact(in_ref[...].reshape(length * planes, length), cas)
    held[...] = jnp.swapaxes(field.reshape(length, planes, length), 0, 1)
    scale = 1.0 / float(length) ** 3
    for half, out_ref in ((half_ref[0], kept_ref), (1 - half_ref[0], given_ref)):
        for number in range(planes // 2):
            x = half * (planes // 2) + number
            value = dot_exact(cas, held[x]) * scale + xc_ref[x] * sigma_ref[x]
            out_ref[0, number * length : (number + 1) * length, :] = value


def back(half, field, sigma, xc_kernel, cas):
    length, planes, _ = field.shape
    shape = jax.ShapeDtypeStruct((1, planes // 2 * length, length), jnp.float32)
    return pl.pallas_call(
        back_kernel,
        out_shape=[shape, shape],
        in_specs=[pl.BlockSpec(memory_space=pltpu.SMEM)]
        + [pl.BlockSpec(memory_space=pltpu.VMEM)] * 4,
        out_specs=[pl.BlockSpec(memory_space=pltpu.VMEM)] * 2,
        scratch_shapes=[pltpu.VMEM((planes, length, length), jnp.float32)],
        compiler_params=pltpu.CompilerParams(vmem_limit_bytes=VMEM_BYTES),
        name="back",
    )(half, field, sigma, xc_kernel, cas)


RING_Y, RING_X = 4, 2


def shift_col(value, dy, dx):
    pairs = [
        (y * RING_X + x, (y + dy) % RING_Y * RING_X + (x + dx) % RING_X)
        for y in range(RING_Y)
        for x in range(RING_X)
    ]
    return lax.ppermute(value, "col", pairs)


OFFSETS = ((0, 0), (1, 0), (3, 0), (0, 1), (2, 0), (1, 1), (3, 1), (2, 1))


def spread(piece, *others):
    from_below, from_above = shift_col(piece, 1, 0), shift_col(piece, -1, 0)
    from_side = shift_col(piece, 0, 1)
    from_side, from_below, from_above, others = lax.optimization_barrier(
        (from_side, from_below, from_above, others)
    )
    far = [shift_col(from_below[:1], 1, 0), shift_col(from_above[1:], -1, 0)]
    far = jnp.concatenate(far, axis=0)
    side_below, side_above = shift_col(from_side, 1, 0), shift_col(from_side, -1, 0)
    near = [piece, from_below, from_above, from_side]
    return near, [far, side_below, side_above, shift_col(far, 0, 1)], others


def swap_core(value):
    return lax.ppermute(value, "grp", [(0, 1), (1, 0)])


def pick_kernel(place_ref, *refs):
    arrays, out_ref, sems = refs[:-2], refs[-2], refs[-1]
    parts = [array.at[j] for array in arrays for j in range(array.shape[0])]
    for number in range(out_ref.shape[0]):
        for order, part in enumerate(parts):

            @pl.when(place_ref[number] == order)
            def _():
                pltpu.make_async_copy(part, out_ref.at[number], sems.at[number]).start()

    for number in range(out_ref.shape[0]):
        pltpu.make_async_copy(parts[0], out_ref.at[number], sems.at[number]).wait()


def pick(place, arrays):
    count = place.shape[0]
    return pl.pallas_call(
        pick_kernel,
        out_shape=jax.ShapeDtypeStruct((count,) + arrays[0].shape[1:], jnp.float32),
        in_specs=[pl.BlockSpec(memory_space=pltpu.SMEM)]
        + [pl.BlockSpec(memory_space=pl.ANY)] * len(arrays),
        out_specs=pl.BlockSpec(memory_space=pltpu.VMEM),
        scratch_shapes=[pltpu.SemaphoreType.DMA((count,))],
        compiler_params=pltpu.CompilerParams(vmem_limit_bytes=VMEM_BYTES),
        name="pick_occ",
    )(place, *arrays)


PAIR_GROUP = 4


def add_products(total, first, densities, fields, rows):
    count = sum(field.shape[0] for field in fields)
    sums = [None] * (PAIR_GROUP * count)
    for tile in range(rows // 8):
        cells = pl.ds(tile * 8, 8)
        right = [field[j, cells, :] for field in fields for j in range(field.shape[0])]
        for k in range(PAIR_GROUP):
            left = densities(k, cells)
            for b in range(count):
                term = left * right[b]
                slot = k * count + b
                sums[slot] = term if sums[slot] is None else sums[slot] + term
    for slot, value in enumerate(sums):
        total[first * count + slot] += value


def start_total(total):
    @pl.when(pl.program_id(0) == 0)
    def _():
        total[...] = jnp.zeros_like(total)


def finish_total(total, out_ref):
    @pl.when(pl.program_id(0) == pl.num_programs(0) - 1)
    def _():
        lanes = jnp.sum(total[...], axis=1)
        out_ref[...] = lax.dot_general(
            jnp.ones((8, LANES), jnp.float32),
            lanes,
            (((1,), (1,)), ((), ())),
            precision=lax.Precision.HIGHEST,
            preferred_element_type=jnp.float32,
        )


def form_kernel(occ_index, vir_index, half, own_occ, mate_occ, own_vir, mate_vir, density_ref):
    held, rows, _ = own_occ.shape
    per_block = own_vir.shape[0]
    for block, vir_ref in enumerate((own_vir.at[:, 0], mate_vir.at[:, 0])):

        @pl.loop(block * per_block, (block + 1) * per_block)
        def _(pair):
            index, vir = occ_index[pair], vir_index[pair]

            @pl.when(index < held)
            def _():
                density_ref[0, pair] = own_occ[index] * vir_ref[vir]

            @pl.when(index >= held)
            def _():
                density_ref[0, pair] = mate_occ[index - held] * vir_ref[vir]


def contract_kernel(density_ref, *refs):
    fields, (out_ref, total) = refs[:-2], refs[-2:]
    start_total(total)

    @pl.loop(0, density_ref.shape[1] // PAIR_GROUP)
    def _(group):
        first = group * PAIR_GROUP
        add_products(
            total,
            first,
            lambda k, cells: density_ref[0, first + k, cells, :],
            fields,
            density_ref.shape[2],
        )

    finish_total(total, out_ref)


TILE = 128


def form_densities(occ_index, vir_index, half, own_occ, mate_occ, own_vir, mate_vir):
    pairs = occ_index.shape[0]
    held, rows, _ = own_occ.shape
    per_block = own_vir.shape[0]
    occ_spec = pl.BlockSpec((held, TILE, LANES), lambda i, o, v, half: (0, i, 0))
    return pl.pallas_call(
        form_kernel,
        grid_spec=pltpu.PrefetchScalarGridSpec(
            num_scalar_prefetch=3,
            grid=(rows // TILE,),
            in_specs=[
                occ_spec,
                occ_spec,
                pl.BlockSpec((per_block, 1, TILE, LANES), lambda i, o, v, half: (0, half[0], i, 0)),
                pl.BlockSpec((per_block, 1, TILE, LANES), lambda i, o, v, half: (0, half[0], i, 0)),
            ],
            out_specs=pl.BlockSpec((1, pairs, TILE, LANES), lambda i, o, v, half: (i, 0, 0, 0)),
        ),
        out_shape=jax.ShapeDtypeStruct((rows // TILE, pairs, TILE, LANES), jnp.float32),
        compiler_params=pltpu.CompilerParams(vmem_limit_bytes=VMEM_BYTES),
        cost_estimate=pl.CostEstimate(
            flops=pairs * rows * LANES, bytes_accessed=24 * 1024 * 1024, transcendentals=0
        ),
        name="form_densities",
    )(occ_index, vir_index, half, own_occ, mate_occ, own_vir, mate_vir)


def contract(densities, fields):
    tiles, pairs, rows, _ = densities.shape
    count = sum(field.shape[0] for field in fields)
    return pl.pallas_call(
        contract_kernel,
        grid=(tiles,),
        in_specs=[pl.BlockSpec((1, pairs, rows, LANES), lambda i: (i, 0, 0, 0))]
        + [pl.BlockSpec((field.shape[0], rows, LANES), lambda i: (0, i, 0)) for field in fields],
        out_specs=pl.BlockSpec((8, pairs * count), lambda i: (0, 0)),
        out_shape=jax.ShapeDtypeStruct((8, pairs * count), jnp.float32),
        scratch_shapes=[pltpu.VMEM((pairs * count, 8, LANES), jnp.float32)],
        compiler_params=pltpu.CompilerParams(vmem_limit_bytes=VMEM_BYTES),
        cost_estimate=pl.CostEstimate(
            flops=2 * count * tiles * pairs * rows * LANES, bytes_accessed=10 * 1024 * 1024, transcendentals=0
        ),
        name="contract",
    )(densities, *fields)


def on_device(occ_orbitals, vir_orbitals, xc_kernel, pairs, batch_slot):
    planes, size_y, size_z = xc_kernel.shape
    cell_count = planes * size_y * size_z
    row_count = lax.axis_size("row")
    scale = 1.0 / float(cell_count * row_count)
    grp = lax.axis_index("grp")
    col = lax.axis_index("col")
    blocks = lax.axis_size(BLOCK_AXES)
    block_index = grp * lax.axis_size("col") + col
    occ_local, vir_local = occ_orbitals.shape[0], vir_orbitals.shape[0]
    half_rows = cell_count // 2 // LANES
    own_y, own_x = col // RING_X, col % RING_X
    mate_block = (1 - grp) * lax.axis_size("col") + col
    places = [
        (own_y + RING_Y - dy) % RING_Y * RING_X + (own_x + RING_X - dx) % RING_X
        for dy, dx in OFFSETS
    ]
    place = jnp.stack(places).astype(jnp.int32)

    def order_of(col_index):
        same = col_index[:, None] == place[None, :]
        return jnp.sum(jnp.where(same, jnp.arange(8, dtype=jnp.int32), 0), axis=1)

    mate_pairs = swap_core(pairs)
    vir_halves = vir_orbitals.reshape(vir_local, 2, half_rows, LANES)
    mate_vir = swap_core(vir_halves)

    own_pair = lax.dynamic_index_in_dim(pairs, batch_slot[block_index], 0, keepdims=False)
    mate_pair = lax.dynamic_index_in_dim(mate_pairs, batch_slot[mate_block], 0, keepdims=False)
    wanted = jnp.stack([own_pair[0], mate_pair[0]])
    wanted_place = order_of(wanted // occ_local % 8) * occ_local + wanted % occ_local
    own_vir_place = (own_pair[1] - block_index * vir_local).reshape(1)
    occ_index = jnp.concatenate([pairs[:, 0], mate_pairs[:, 0]])
    source = occ_index // occ_local
    occ_place = jnp.where(source // 8 == grp, 0, 8 * occ_local)
    occ_place = occ_place + order_of(source % 8) * occ_local + occ_index % occ_local
    vir_place = jnp.concatenate(
        [pairs[:, 1] - block_index * vir_local, mate_pairs[:, 1] - mate_block * vir_local]
    )

    occ_near, occ_far, (wanted_place, occ_place, vir_place) = spread(
        occ_orbitals.reshape(occ_local, 2 * half_rows, LANES), wanted_place, occ_place, vir_place
    )
    occ_pieces = occ_near + occ_far
    picked = pick(wanted_place, occ_pieces)
    from_mate = swap_core(picked[1])
    cas = cas_table(size_z)
    as_flag = jnp.where(wanted[0] // occ_local // 8 == grp, 1, 0).reshape(1)
    sigma, field = forward(as_flag, own_vir_place, picked[0], from_mate, vir_orbitals, cas)
    columns = lax.all_to_all(field, "row", split_axis=0, concat_axis=0, tiled=True)
    columns = columns.reshape(row_count, -1, planes, size_z)
    first = (lax.axis_index("row") * (size_y // row_count)).reshape(1)
    columns = filter_columns(first, columns, cas)
    columns, *occ_pieces[7:] = lax.optimization_barrier((columns, *occ_pieces[7:]))

    def occ_half(half):
        parts = [
            lax.dynamic_slice_in_dim(part, half * half_rows, half_rows, 1) for part in occ_pieces
        ]
        return jnp.concatenate(parts, axis=0)

    mate_occs, own_occs = swap_core(occ_half(1 - grp)), occ_half(grp)
    densities = form_densities(
        occ_place, vir_place, jnp.full((1,), grp, jnp.int32), own_occs, mate_occs, vir_halves, mate_vir
    )
    field = lax.all_to_all(columns, "row", split_axis=0, concat_axis=0, tiled=True)
    half = jnp.full((1,), grp, jnp.int32)
    kept, given = back(half, field.reshape(size_y, planes, size_z), sigma, xc_kernel, cas)
    own_field = jnp.concatenate([kept, swap_core(given)], axis=0)
    field_near, field_far, (densities,) = spread(own_field, densities)

    near = contract(densities, field_near + field_far[:1])
    far = contract(densities, field_far[1:])

    pair_count = pairs.shape[0]
    sums = [part[0].reshape(2, pair_count, -1) for part in (near, far)]
    sums = jnp.concatenate(sums, axis=2)
    sums = jnp.where(grp == 0, sums, sums[::-1])
    sent = jnp.broadcast_to(sums[:, None], (2, row_count, pair_count, blocks))
    got = lax.all_to_all(
        sent.reshape(2 * row_count, 2, pair_count * blocks // 2), ("grp", "row"), 0, 0, tiled=True
    )
    got = jnp.sum(got.reshape(2, row_count, pair_count, 8, 2), axis=1)
    got = got[0] + got[1][..., ::-1]
    got = got.transpose(0, 2, 1)
    chosen = place[:, None] == jnp.arange(8, dtype=jnp.int32)[None, :]
    ordered = jnp.sum(jnp.where(chosen, got[:, :, :, None], 0.0), axis=2)
    return ordered.reshape(pair_count, blocks) * scale


def solution(mesh):
    return jax.shard_map(
        on_device,
        mesh=mesh,
        in_specs=(
            P(BLOCK_AXES, "row", None, None),
            P(BLOCK_AXES, "row", None, None),
            P("row", None, None),
            P(BLOCK_AXES, None),
            P(),
        ),
        out_specs=P(BLOCK_AXES, None),
        check_vma=False,
    )
```

time: 200 us -> 198 us (0.990)
  blocking collectives: 0 us -> 20.7 us
  Pallas kernels: 22.3 us -> 33.7 us
  waiting for transfers between devices: 74.5 us -> 64.1 us
  starting transfers between devices: 53.6 us -> 44.2 us
  matrix products: 7.39 us -> 0 us
  local copies, waits for them, and re-layouts: 30.2 us -> 23.4 us
    all_to_all x0 -> x1, blocking collectives: none -> 20.7 us  [on_device(): lax.all_to_all(columns, 'row', split_axis=0, concat_axis=0, tiled=True)]
    all_to_all x3 -> x2, waiting for transfers between devices: 30.7 us -> 13.9 us  [the longest x1 7.18 us: on_device(): lax.all_to_all(sent.reshape(2 * row_count, 2, pair_count * blocks // 2),...]
    pallas_call x2 -> x6, Pallas kernels: 20.4 us -> 32.9 us  [the longest x2 15.2 us: contract(): pl.pallas_call(contract_kernel, grid=(tiles,), in_specs=[pl.BlockSpec((1,...]
    dot_general x6 -> x0, matrix products: 7.39 us -> none  [the longest x1 1.93 us: planes_forward(): grid_field = jnp.dot(density, cas_rows, precision=highest)]
    ppermute x22 -> x16, waiting for transfers between devices: 42.3 us -> 48.7 us  [shift_col(): return lax.ppermute(value, 'col', pairs)]
    all_to_all x3 -> x2, starting transfers between devices: 21.6 us -> 16 us  [the longest x1 9.94 us: on_device(): lax.all_to_all(field, 'row', split_axis=0, concat_axis=0, tiled=True)]
    dynamic_slice x3 -> x1, local copies, waits for them, and re-layouts: 6 us -> 1.39 us  [on_device(): batch_slot[mate_block]]
    ppermute x22 -> x16, starting transfers between devices: 31.6 us -> 27.6 us  [shift_col(): return lax.ppermute(value, 'col', pairs)]
  transfers between devices with their start and end apart: 30 -> 23, of which waited for: 12 -> 11; matrix products, arithmetic and copies ran while one was open for 19% -> 9% of each run, Pallas kernels for 7% -> 14%
where the time goes in v4:
time: 198 us; the launch traced here: 196 us
  waiting for transfers between devices  64.1 us (32%)
  starting transfers between devices  44.2 us (22%)
  Pallas kernels  33.7 us (17%)
  local copies, waits for them, and re-layouts  23.4 us (12%)
  blocking collectives  20.7 us (10%)
  between operations  7.2 us (4%)
  other arithmetic  2.74 us (1%)
    ppermute x16, waiting for transfers between devices, shift_col(): return lax.ppermute(value, 'col', pairs)  48.7 us
    ppermute x16, starting transfers between devices, shift_col(): return lax.ppermute(value, 'col', pairs)  27.6 us
    all_to_all x1, blocking collectives, on_device(): lax.all_to_all(columns, 'row', split_axis=0, concat_axis=0, tiled=True)  20.7 us
    pallas_call x2, Pallas kernels, contract(): pl.pallas_call(contract_kernel, grid=(tiles,), in_specs=[pl.BlockSpec((1,...  15.2 us
    unnamed x41, local copies, waits for them, and re-layouts  14.3 us
    pallas_call x1, Pallas kernels, form_densities(): pl.pallas_call(form_kernel, grid_spec=pltpu.PrefetchScalarGridSpec(num_sc...  10.6 us
    all_to_all x1, starting transfers between devices, on_device(): lax.all_to_all(field, 'row', split_axis=0, concat_axis=0, tiled=True)  9.94 us
    all_to_all x1, waiting for transfers between devices, on_device(): lax.all_to_all(sent.reshape(2 * row_count, 2, pair_count * blocks // 2),...  7.18 us
  transfers between devices with their start and end apart: 23, of which 11 were waited for; matrix products, arithmetic and copies ran while one was open for 9% of the time, Pallas kernels for 14%

profile of v4, /device:TPU:2, one launch (start us, length us, event | category | flops | bytes accessed | tf_op | source)
XLA Modules:
  0.0 196.0 jit_solution(3277871353692249895)
XLA Ops:
  0.0 2.1 %collective-permute-start = (f32[2,1024,128]{2,1,0:T(8,128)}, f32[2,1024,128]{2,1,0:T(8,128)}, u32[]{:S(2)}, u32[]{:S(2)}) collective-permute-start(f32[2,1024,128]{2,1,0:T(8,128)} %bitcast.48), channel_id=1, source_target_pairs={{0,1},{1,0},{2,3},{3,2},{4,5},{5,4},{6,7},{7,6},{8,9},{9,8},{10,11... | collective-permute-start | bytes 3145736 | tf_op jit(solution)/shard_map/ppermute | solution.py:127
  2.1 1.6 collective-permute-start.1
  3.7 1.7 collective-permute-start.2
  5.4 0.5 collective-permute-start.15
  5.9 1.4 fusion.8
  9.8 0.8 subtract_bitcast_fusion.1
  11.1 0.8 constant_dynamic-slice_fusion.1
  11.9 0.5 fusion.7
  13.3 0.5 slice.56
  13.9 1.3 and_select_fusion.5
  15.2 0.2 fusion.1
  15.5 11.2 %collective-permute-done.refs_3_ = f32[2,1024,128]{2,1,0:T(8,128)} collective-permute-done((f32[2,1024,128]{2,1,0:T(8,128)}, f32[2,1024,128]{2,1,0:T(8,128)}, u32[]{:S(2)}, u32[]{:S(2)}) %collective-permute-start) | collective-permute-done | bytes 1048608 | tf_op jit(solution)/shard_map/ppermute | solution.py:127
  26.7 1.5 collective-permute-done.1.refs_1_
  28.3 1.6 collective-permute-start.4
  30.0 1.7 collective-permute-start.5
  31.7 0.4 collective-permute-start.6
  32.1 2.9 %collective-permute-start.7 = (f32[2,1024,128]{2,1,0:T(8,128)}, f32[2,1024,128]{2,1,0:T(8,128)S(1)}, u32[]{:S(2)}, u32[]{:S(2)}) collective-permute-start(f32[2,1024,128]{2,1,0:T(8,128)} %collective-permute-done.refs_3_), channel_id=1, source_target_pairs={{0,6},{1,7},{2,0},{3,1},{4,2},{5,3},{6,4},{7,5},{8,14},{9,15},{10,... | collective-permute-start | bytes 3145736 | tf_op jit(solution)/shard_map/ppermute | solution.py:127
  35.0 9.5 %collective-permute-done.4 = f32[1,1024,128]{2,1,0:T(8,128)S(1)} collective-permute-done((f32[1,1024,128]{2,1,0:T(8,128)S(1)}, f32[1,1024,128]{2,1,0:T(8,128)S(1)}, u32[]{:S(2)}, u32[]{:S(2)}) %collective-permute-start.4) | collective-permute-done | bytes 524320 | tf_op jit(solution)/shard_map/ppermute | solution.py:127
  44.5 0.4 collective-permute-done.5
  45.0 1.5 collective-permute-start.8
  46.5 18.2 %collective-permute-done.6.refs_5_ = f32[2,1024,128]{2,1,0:T(8,128)S(1)} collective-permute-done((f32[2,1024,128]{2,1,0:T(8,128)}, f32[2,1024,128]{2,1,0:T(8,128)S(1)}, u32[]{:S(2)}, u32[]{:S(2)}) %collective-permute-start.6) | collective-permute-done | bytes 1048608 | tf_op jit(solution)/shard_map/ppermute | solution.py:127
  64.6 2.1 %collective-permute-done.8.refs_7_ = f32[2,1024,128]{2,1,0:T(8,128)S(1)} collective-permute-done((f32[2,1024,128]{2,1,0:T(8,128)S(1)}, f32[2,1024,128]{2,1,0:T(8,128)S(1)}, u32[]{:S(2)}, u32[]{:S(2)}) %collective-permute-start.8) | collective-permute-done | bytes 1048608 | tf_op jit(solution)/shard_map/ppermute | solution.py:127
  66.8 1.0 copy-done.11
  67.8 0.7 pick_occ.1
  68.5 1.0 slice_bitcast_fusion
  72.7 1.0 copy-done.1
  73.7 2.9 %forward.1 = (f32[8,128,128]{2,1,0:T(8,128)S(1)}, f32[128,8,128]{2,1,0:T(8,128)S(1)}) custom-call(s32[1]{0:T(128)} %bitcast.12.flag_ref, s32[1]{0:T(128)} %bitcast.14.vir_place, f32[1024,128]{1,0:T(8,128)S(1)} %copy-done.1, f32[1024,128]{1,0:T(8,128)} %collective-permute-done.9.mate_occ, f32[16,8,128,128]{3,2,1,0:T(8,128)} %vir_ref.1, f32[128,128]{1,0:T(8,128)S(1)} %copy-done.2), custom_call_target="tpu_custom_call" | custom-call | tf_op jit(solution)/shard_map/forward/pallas_call | solution.py:39
  76.7 0.8 copy-done.4
  77.5 0.8 copy-done.6
  78.3 9.9 %all-to-all-start = ((f32[128,8,128]{2,1,0:T(8,128)}), f32[128,8,128]{2,1,0:T(8,128)}, u32[]{:S(2)}, u32[]{:S(2)}) async-start(f32[128,8,128]{2,1,0:T(8,128)} %copy-done.6), calls=%async_computation | async-start | bytes 1048576 | tf_op jit(solution)/shard_map/all_to_all | solution.py:350
  88.2 1.0 dynamic-slice_dynamic-update-slice_fusion.7
  89.3 1.0 dynamic-slice_dynamic-update-slice_fusion.6
  90.3 1.0 dynamic-slice_dynamic-update-slice_fusion.5
  91.3 2.2 %dynamic-slice_dynamic-update-slice_fusion.4 = (f32[16,512,128]{2,1,0:T(8,128)}, f32[16,512,128]{2,1,0:T(8,128)}) fusion(f32[16,512,128]{2,1,0:T(8,128)} %get-tuple-element.51, f32[2,1024,128]{2,1,0:T(8,128)} %collective-permute-done.refs_3_, s32[]{:T(128)S(6)} %select_n.198, f32[16,512,128]{2,1,0:T(8,128)} %get-tuple-element.52, s32[]{:T(128)S(6)} %select_n.197), kind=kLoop, calls=%fused_computation.6 | loop fusion | bytes 2097160
  93.6 1.0 dynamic-slice_dynamic-update-slice_fusion.3
  94.6 1.0 dynamic-slice_dynamic-update-slice_fusion.2
  95.7 1.0 dynamic-slice_dynamic-update-slice_fusion.1
  96.7 6.7 %all-to-all-done = f32[128,8,128]{2,1,0:T(8,128)} async-done(((f32[128,8,128]{2,1,0:T(8,128)}), f32[128,8,128]{2,1,0:T(8,128)}, u32[]{:S(2)}, u32[]{:S(2)}) %all-to-all-start) | async-done | bytes 524320 | tf_op jit(solution)/shard_map/all_to_all | solution.py:350
  103.4 2.2 %filter_columns.1 = f32[16,8,8,128]{3,2,1,0:T(8,128)S(1)} custom-call(s32[1]{0:T(128)} %bitcast.9.first_ref, f32[16,8,8,128]{3,2,1,0:T(8,128)} %bitcast.25.in_ref, f32[128,128]{1,0:T(8,128)S(1)} %copy-done.2), custom_call_target="tpu_custom_call" | custom-call | tf_op jit(solution)/shard_map/filter_columns/pallas_call | solution.py:79
  105.6 2.2 %dynamic-slice_dynamic-update-slice_fusion = (f32[16,512,128]{2,1,0:T(8,128)}, f32[16,512,128]{2,1,0:T(8,128)}) fusion(f32[16,512,128]{2,1,0:T(8,128)} %get-tuple-element.43, f32[2,1024,128]{2,1,0:T(8,128)} %copy-done.11, s32[]{:T(128)S(6)} %select_n.198, f32[16,512,128]{2,1,0:T(8,128)} %get-tuple-element.44, s32[]{:T(128)S(6)} %select_n.197), kind=kLoop, calls=%fused_computation.2 | loop fusion | bytes 2097160 | tf_op jit(solution)/shard_map/concatenate | solution.py:360
  107.9 20.7 %all_to_all.15 = f32[16,8,8,128]{3,2,1,0:T(8,128)S(1)} all-to-all(f32[16,8,8,128]{3,2,1,0:T(8,128)S(1)} %filter_columns.1), channel_id=1, replica_groups=mesh['grp'=2,'row'=16,'col'=8] {'row'}, dimensions={0} | all-to-all | bytes 1048576 | tf_op jit(solution)/shard_map/all_to_all | solution.py:366
  128.6 1.9 back.1
  130.6 1.5 collective-permute-done.10
  132.1 2.7 %collective-permute-start.11 = (f32[2,512,128]{2,1,0:T(8,128)S(1)}, f32[2,512,128]{2,1,0:T(8,128)S(1)}, u32[]{:S(2)}, u32[]{:S(2)}) collective-permute-start(f32[2,512,128]{2,1,0:T(8,128)S(1)} %constant_dynamic-update-slice_fusion.2.refs_0_), channel_id=1, source_target_pairs={{0,1},{1,0},{2,3},{3,2},{4,5},{5,4},{6,7},{7,6},{8,9},{9,8},{10,11... | collective-permute-start | bytes 1572872 | tf_op jit(solution)/shard_map/ppermute | solution.py:127
  134.8 0.4 collective-permute-start.12
  135.2 2.8 %collective-permute-start.13 = (f32[2,512,128]{2,1,0:T(8,128)S(1)}, f32[2,512,128]{2,1,0:T(8,128)S(1)}, u32[]{:S(2)}, u32[]{:S(2)}) collective-permute-start(f32[2,512,128]{2,1,0:T(8,128)S(1)} %constant_dynamic-update-slice_fusion.2.refs_0_), channel_id=1, source_target_pairs={{0,6},{1,7},{2,0},{3,1},{4,2},{5,3},{6,4},{7,5},{8,14},{9,15},{10,... | collective-permute-start | bytes 1572872 | tf_op jit(solution)/shard_map/ppermute | solution.py:127
  138.1 2.0 %copy-done.14 = f32[16,512,128]{2,1,0:T(8,128)} copy-done((f32[16,512,128]{2,1,0:T(8,128)}, f32[16,512,128]{2,1,0:T(8,128)S(1)}, u32[]{:S(2)}) %copy-start.14) | copy-done | bytes 4194328
  140.1 10.6 %form_densities.1.density_ref = f32[4,32,128,128]{3,2,1,0:T(8,128)} custom-call(s32[32]{0:T(128)S(1)} %get-tuple-element.30.occ_index, s32[32]{0:T(128)S(1)} %get-tuple-element.31.vir_index, s32[1]{0:T(128)} %bitcast.8.half_ref.half, f32[16,512,128]{2,1,0:T(8,128)} %get-tuple-element.42.own_occ, f32[16,512,128]{2,1,0:T(8,128)} %copy-done.14, ...), custom_call_target="tpu_custom_call" | custom-call | flops 2097152 | bytes 25165824 | tf_op jit(solution)/shard_map/form_densities/pallas_call | solution.py:260
  150.9 3.3 %collective-permute-start.17 = (f32[1,512,128]{2,1,0:T(8,128)S(1)}, f32[1,512,128]{2,1,0:T(8,128)S(1)}, u32[]{:S(2)}, u32[]{:S(2)}) collective-permute-start(f32[1,512,128]{2,1,0:T(8,128)S(1)} %slice.66), channel_id=1, source_target_pairs={{0,6},{1,7},{2,0},{3,1},{4,2},{5,3},{6,4},{7,5},{8,14},{9,15},{10,... | collective-permute-start | bytes 786440 | tf_op jit(solution)/shard_map/ppermute | solution.py:127
  154.2 3.2 %collective-permute-start.19 = (f32[2,512,128]{2,1,0:T(8,128)S(1)}, f32[2,512,128]{2,1,0:T(8,128)}, u32[]{:S(2)}, u32[]{:S(2)}) collective-permute-start(f32[2,512,128]{2,1,0:T(8,128)S(1)} %collective-permute-done.11.refs_3_), channel_id=1, source_target_pairs={{0,6},{1,7},{2,0},{3,1},{4,2},{5,3},{6,4},{7,5},{8,14},{9,15},{10,... | collective-permute-start | bytes 1572872 | tf_op jit(solution)/shard_map/ppermute | solution.py:127
  157.4 3.9 %collective-permute-done.16 = f32[1,512,128]{2,1,0:T(8,128)S(1)} collective-permute-done((f32[1,512,128]{2,1,0:T(8,128)S(1)}, f32[1,512,128]{2,1,0:T(8,128)S(1)}, u32[]{:S(2)}, u32[]{:S(2)}) %collective-permute-start.16) | collective-permute-done | bytes 262176 | tf_op jit(solution)/shard_map/ppermute | solution.py:127
  161.4 1.6 collective-permute-start.20
  162.9 8.6 %contract.2 = f32[8,320]{1,0:T(8,128)S(1)} custom-call(f32[4,32,128,128]{3,2,1,0:T(8,128)} %form_densities.1.density_ref, f32[2,512,128]{2,1,0:T(8,128)S(1)} %constant_dynamic-update-slice_fusion.2.refs_0_, f32[2,512,128]{2,1,0:T(8,128)S(1)} %collective-permute-done.12.refs_1_, f32[2,512,128]{2,1,0:T(8,128)S(1)} %collective-permute-done.13.refs_2_, ...), custom_call_target="tpu_custom_call" | custom-call | flops 41943040 | bytes 10485760 | tf_op jit(solution)/shard_map/contract/pallas_call | solution.py:285
  171.6 0.1 reshape_squeeze.6
  171.7 1.8 collective-permute-done.20.refs_2_
  173.5 6.7 %contract.3 = f32[8,192]{1,0:T(8,128)S(1)} custom-call(f32[4,32,128,128]{3,2,1,0:T(8,128)} %form_densities.1.density_ref, f32[2,512,128]{2,1,0:T(8,128)S(1)} %collective-permute-done.18.refs_0_, f32[2,512,128]{2,1,0:T(8,128)} %collective-permute-done.19.refs_1_, f32[2,512,128]{2,1,0:T(8,128)} %collective-permute-done.20.refs_2_), custom_call_target="tpu_custom_call" | custom-call | flops 25165824 | bytes 10485760 | tf_op jit(solution)/shard_map/contract/pallas_call | solution.py:285
  180.5 0.7 reshape.190
  181.2 6.0 %all-to-all-start.2 = ((f32[32,2,128]{2,1,0:T(2,128)}), f32[32,2,128]{2,1,0:T(2,128)S(1)}, u32[]{:S(2)}, u32[]{:S(2)}) async-start(f32[32,2,128]{2,1,0:T(2,128)} %reshape.190), calls=%async_computation.2 | async-start | bytes 65536 | tf_op jit(solution)/shard_map/all_to_all | solution.py:380
  187.3 7.2 %all-to-all-done.2 = f32[32,2,128]{2,1,0:T(2,128)S(1)} async-done(((f32[32,2,128]{2,1,0:T(2,128)}), f32[32,2,128]{2,1,0:T(2,128)S(1)}, u32[]{:S(2)}, u32[]{:S(2)}) %all-to-all-start.2) | async-done | bytes 32800 | tf_op jit(solution)/shard_map/all_to_all | solution.py:380
  194.5 0.1 copy.29
  194.7 0.2 fusion.6
  194.9 0.2 copy.27
  195.0 0.2 copy.26
  195.3 0.7 copy.28
  (71 shorter events, 1.5 us)
Async XLA Ops:
  0.0 67.8 %copy-start = (f32[2,8,128,128]{3,2,1,0:T(8,128)S(1)}, f32[2,8,128,128]{3,2,1,0:T(8,128)}, u32[]{:S(2)}) copy-start(f32[2,8,128,128]{3,2,1,0:T(8,128)} %param.6) | copy-start | bytes 3145732
  0.0 26.7 %collective-permute-start = (f32[2,1024,128]{2,1,0:T(8,128)}, f32[2,1024,128]{2,1,0:T(8,128)}, u32[]{:S(2)}, u32[]{:S(2)}) collective-permute-start(f32[2,1024,128]{2,1,0:T(8,128)} %bitcast.48), channel_id=1, source_target_pairs={{0,1},{1,0},{2,3},{3,2},{4,5},{5,4},{6,7},{7,6},{8,9},{9,8},{10,11... | collective-permute-start | bytes 3145736 | tf_op jit(solution)/shard_map/ppermute | solution.py:127
  2.1 26.1 %collective-permute-start.1 = (f32[2,1024,128]{2,1,0:T(8,128)}, f32[2,1024,128]{2,1,0:T(8,128)S(1)}, u32[]{:S(2)}, u32[]{:S(2)}) collective-permute-start(f32[2,1024,128]{2,1,0:T(8,128)} %bitcast.49), channel_id=1, source_target_pairs={{0,2},{1,3},{2,4},{3,5},{4,6},{5,7},{6,0},{7,1},{8,10},{9,11},{10,... | collective-permute-start | bytes 3145736 | tf_op jit(solution)/shard_map/ppermute | solution.py:127
  3.7 24.6 %collective-permute-start.2 = (f32[2,1024,128]{2,1,0:T(8,128)}, f32[2,1024,128]{2,1,0:T(8,128)S(1)}, u32[]{:S(2)}, u32[]{:S(2)}) collective-permute-start(f32[2,1024,128]{2,1,0:T(8,128)} %bitcast.50), channel_id=1, source_target_pairs={{0,6},{1,7},{2,0},{3,1},{4,2},{5,3},{6,4},{7,5},{8,14},{9,15},{10,... | collective-permute-start | bytes 3145736 | tf_op jit(solution)/shard_map/ppermute | solution.py:127
  5.4 7.8 %collective-permute-start.3 = (s32[16,2]{0,1:T(2,128)}, s32[16,2]{0,1:T(2,128)S(1)}, u32[]{:S(2)}, u32[]{:S(2)}) collective-permute-start(s32[16,2]{0,1:T(2,128)} %param.9), channel_id=1, source_target_pairs={{0,128},{128,0},{1,129},{129,1},{2,130},{130,2},{3,131},{131,3},{4... | collective-permute-start | bytes 392 | tf_op jit(solution)/shard_map/ppermute | solution.py:147
  5.4 132.7 %collective-permute-start.15 = (f32[16,2,512,128]{3,2,1,0:T(8,128)}, f32[16,2,512,128]{3,2,1,0:T(8,128)}, u32[]{:S(2)}, u32[]{:S(2)}) collective-permute-start(f32[16,2,512,128]{3,2,1,0:T(8,128)} %bitcast.54), channel_id=1, source_target_pairs={{0,128},{128,0},{1,129},{129,1},{2,130},{130,2},{3,131},{131,3},{4... | collective-permute-start | bytes 25165832 | tf_op jit(solution)/shard_map/ppermute | solution.py:147
  28.3 16.1 %collective-permute-start.4 = (f32[1,1024,128]{2,1,0:T(8,128)S(1)}, f32[1,1024,128]{2,1,0:T(8,128)S(1)}, u32[]{:S(2)}, u32[]{:S(2)}) collective-permute-start(f32[1,1024,128]{2,1,0:T(8,128)S(1)} %slice.61), channel_id=1, source_target_pairs={{0,2},{1,3},{2,4},{3,5},{4,6},{5,7},{6,0},{7,1},{8,10},{9,11},{10,... | collective-permute-start | bytes 1572872 | tf_op jit(solution)/shard_map/ppermute | solution.py:127
  30.0 14.9 %collective-permute-start.5 = (f32[1,1024,128]{2,1,0:T(8,128)S(1)}, f32[1,1024,128]{2,1,0:T(8,128)S(1)}, u32[]{:S(2)}, u32[]{:S(2)}) collective-permute-start(f32[1,1024,128]{2,1,0:T(8,128)S(1)} %slice.62), channel_id=1, source_target_pairs={{0,6},{1,7},{2,0},{3,1},{4,2},{5,3},{6,4},{7,5},{8,14},{9,15},{10,... | collective-permute-start | bytes 1572872 | tf_op jit(solution)/shard_map/ppermute | solution.py:127
  31.7 32.9 %collective-permute-start.6 = (f32[2,1024,128]{2,1,0:T(8,128)}, f32[2,1024,128]{2,1,0:T(8,128)S(1)}, u32[]{:S(2)}, u32[]{:S(2)}) collective-permute-start(f32[2,1024,128]{2,1,0:T(8,128)} %collective-permute-done.refs_3_), channel_id=1, source_target_pairs={{0,2},{1,3},{2,4},{3,5},{4,6},{5,7},{6,0},{7,1},{8,10},{9,11},{10,... | collective-permute-start | bytes 3145736 | tf_op jit(solution)/shard_map/ppermute | solution.py:127
  32.1 32.6 %collective-permute-start.7 = (f32[2,1024,128]{2,1,0:T(8,128)}, f32[2,1024,128]{2,1,0:T(8,128)S(1)}, u32[]{:S(2)}, u32[]{:S(2)}) collective-permute-start(f32[2,1024,128]{2,1,0:T(8,128)} %collective-permute-done.refs_3_), channel_id=1, source_target_pairs={{0,6},{1,7},{2,0},{3,1},{4,2},{5,3},{6,4},{7,5},{8,14},{9,15},{10,... | collective-permute-start | bytes 3145736 | tf_op jit(solution)/shard_map/ppermute | solution.py:127
  45.0 21.8 %copy-start.7 = (f32[2,1024,128]{2,1,0:T(8,128)}, f32[2,1024,128]{2,1,0:T(8,128)S(1)}, u32[]{:S(2)}) copy-start(f32[2,1024,128]{2,1,0:T(8,128)S(1)} %constant_dynamic-update-slice_fusion.refs_4_) | copy-start | bytes 3145732
  45.0 27.7 %copy-start.2 = (f32[128,128]{1,0:T(8,128)S(1)}, f32[128,128]{1,0:T(8,128)}, u32[]{:S(2)}) copy-start(f32[128,128]{1,0:T(8,128)} %constant.191.clone.cas_ref) | copy-start | bytes 196612
  45.0 21.8 %collective-permute-start.8 = (f32[2,1024,128]{2,1,0:T(8,128)S(1)}, f32[2,1024,128]{2,1,0:T(8,128)S(1)}, u32[]{:S(2)}, u32[]{:S(2)}) collective-permute-start(f32[2,1024,128]{2,1,0:T(8,128)S(1)} %constant_dynamic-update-slice_fusion.refs_4_), channel_id=1, source_target_pairs={{0,1},{1,0},{2,3},{3,2},{4,5},{5,4},{6,7},{7,6},{8,9},{9,8},{10,11... | collective-permute-start | bytes 3145736 | tf_op jit(solution)/shard_map/ppermute | solution.py:127
  64.6 2.1 %copy-start.12 = (f32[2,1024,128]{2,1,0:T(8,128)}, f32[2,1024,128]{2,1,0:T(8,128)S(1)}, u32[]{:S(2)}) copy-start(f32[2,1024,128]{2,1,0:T(8,128)S(1)} %collective-permute-done.6.refs_5_) | copy-start | bytes 3145732
  64.6 2.1 %copy-start.9 = (f32[2,1024,128]{2,1,0:T(8,128)}, f32[2,1024,128]{2,1,0:T(8,128)S(1)}, u32[]{:S(2)}) copy-start(f32[2,1024,128]{2,1,0:T(8,128)S(1)} %collective-permute-done.7.refs_6_) | copy-start | bytes 3145732
  66.8 1.0 copy-start.11
  69.6 3.1 %collective-permute-start.9 = (f32[1024,128]{1,0:T(8,128)}, f32[1024,128]{1,0:T(8,128)}, u32[]{:S(2)}, u32[]{:S(2)}) collective-permute-start(f32[1024,128]{1,0:T(8,128)} %get-tuple-element.57), channel_id=1, source_target_pairs={{0,128},{128,0},{1,129},{129,1},{2,130},{130,2},{3,131},{131,3},{4... | collective-permute-start | bytes 1572872 | tf_op jit(solution)/shard_map/ppermute | solution.py:147
  72.7 1.0 copy-start.1
  76.7 0.8 copy-start.4
  77.5 0.8 copy-start.6
  78.3 25.1 %all-to-all-start = ((f32[128,8,128]{2,1,0:T(8,128)}), f32[128,8,128]{2,1,0:T(8,128)}, u32[]{:S(2)}, u32[]{:S(2)}) async-start(f32[128,8,128]{2,1,0:T(8,128)} %copy-done.6), calls=%async_computation | async-start | bytes 1048576 | tf_op jit(solution)/shard_map/all_to_all | solution.py:350
  88.2 5.3 %copy-start.8 = (f32[2,1024,128]{2,1,0:T(8,128)S(1)}, f32[2,1024,128]{2,1,0:T(8,128)}, u32[]{:S(2)}) copy-start(f32[2,1024,128]{2,1,0:T(8,128)} %copy-done.7) | copy-start | bytes 3145732
  89.3 5.4 %copy-start.13 = (f32[2,1024,128]{2,1,0:T(8,128)S(1)}, f32[2,1024,128]{2,1,0:T(8,128)}, u32[]{:S(2)}) copy-start(f32[2,1024,128]{2,1,0:T(8,128)} %copy-done.12) | copy-start | bytes 3145732
  90.3 5.3 %copy-start.10 = (f32[2,1024,128]{2,1,0:T(8,128)S(1)}, f32[2,1024,128]{2,1,0:T(8,128)}, u32[]{:S(2)}) copy-start(f32[2,1024,128]{2,1,0:T(8,128)} %copy-done.9) | copy-start | bytes 3145732
  94.6 33.9 %copy-start.3 = (f32[8,128,128]{2,1,0:T(8,128)S(1)}, f32[8,128,128]{2,1,0:T(8,128)}, u32[]{:S(2)}) copy-start(f32[8,128,128]{2,1,0:T(8,128)} %xc_ref.1) | copy-start | bytes 1572868
  94.6 33.9 %copy-start.5 = (f32[8,128,128]{2,1,0:T(8,128)S(1)}, f32[8,128,128]{2,1,0:T(8,128)}, u32[]{:S(2)}) copy-start(f32[8,128,128]{2,1,0:T(8,128)} %copy-done.4) | copy-start | bytes 1572868
  107.9 30.2 %collective-permute-start.14 = (f32[16,512,128]{2,1,0:T(8,128)}, f32[16,512,128]{2,1,0:T(8,128)S(1)}, u32[]{:S(2)}, u32[]{:S(2)}) collective-permute-start(f32[16,512,128]{2,1,0:T(8,128)} %get-tuple-element.41), channel_id=1, source_target_pairs={{0,128},{128,0},{1,129},{129,1},{2,130},{130,2},{3,131},{131,3},{4... | collective-permute-start | bytes 12582920 | tf_op jit(solution)/shard_map/ppermute | solution.py:147
  130.5 1.6 collective-permute-start.10
  132.1 18.6 %collective-permute-start.11 = (f32[2,512,128]{2,1,0:T(8,128)S(1)}, f32[2,512,128]{2,1,0:T(8,128)S(1)}, u32[]{:S(2)}, u32[]{:S(2)}) collective-permute-start(f32[2,512,128]{2,1,0:T(8,128)S(1)} %constant_dynamic-update-slice_fusion.2.refs_0_), channel_id=1, source_target_pairs={{0,1},{1,0},{2,3},{3,2},{4,5},{5,4},{6,7},{7,6},{8,9},{9,8},{10,11... | collective-permute-start | bytes 1572872 | tf_op jit(solution)/shard_map/ppermute | solution.py:127
  134.8 15.9 %collective-permute-start.12 = (f32[2,512,128]{2,1,0:T(8,128)S(1)}, f32[2,512,128]{2,1,0:T(8,128)S(1)}, u32[]{:S(2)}, u32[]{:S(2)}) collective-permute-start(f32[2,512,128]{2,1,0:T(8,128)S(1)} %constant_dynamic-update-slice_fusion.2.refs_0_), channel_id=1, source_target_pairs={{0,2},{1,3},{2,4},{3,5},{4,6},{5,7},{6,0},{7,1},{8,10},{9,11},{10,... | collective-permute-start | bytes 1572872 | tf_op jit(solution)/shard_map/ppermute | solution.py:127
  135.2 15.5 %collective-permute-start.13 = (f32[2,512,128]{2,1,0:T(8,128)S(1)}, f32[2,512,128]{2,1,0:T(8,128)S(1)}, u32[]{:S(2)}, u32[]{:S(2)}) collective-permute-start(f32[2,512,128]{2,1,0:T(8,128)S(1)} %constant_dynamic-update-slice_fusion.2.refs_0_), channel_id=1, source_target_pairs={{0,6},{1,7},{2,0},{3,1},{4,2},{5,3},{6,4},{7,5},{8,14},{9,15},{10,... | collective-permute-start | bytes 1572872 | tf_op jit(solution)/shard_map/ppermute | solution.py:127
  138.1 2.0 %copy-start.14 = (f32[16,512,128]{2,1,0:T(8,128)}, f32[16,512,128]{2,1,0:T(8,128)S(1)}, u32[]{:S(2)}) copy-start(f32[16,512,128]{2,1,0:T(8,128)S(1)} %collective-permute-done.14.mate_occ) | copy-start | bytes 12582916
  150.8 10.5 %collective-permute-start.16 = (f32[1,512,128]{2,1,0:T(8,128)S(1)}, f32[1,512,128]{2,1,0:T(8,128)S(1)}, u32[]{:S(2)}, u32[]{:S(2)}) collective-permute-start(f32[1,512,128]{2,1,0:T(8,128)S(1)} %slice.65), channel_id=1, source_target_pairs={{0,2},{1,3},{2,4},{3,5},{4,6},{5,7},{6,0},{7,1},{8,10},{9,11},{10,... | collective-permute-start | bytes 786440 | tf_op jit(solution)/shard_map/ppermute | solution.py:127
  150.9 10.4 %collective-permute-start.17 = (f32[1,512,128]{2,1,0:T(8,128)S(1)}, f32[1,512,128]{2,1,0:T(8,128)S(1)}, u32[]{:S(2)}, u32[]{:S(2)}) collective-permute-start(f32[1,512,128]{2,1,0:T(8,128)S(1)} %slice.66), channel_id=1, source_target_pairs={{0,6},{1,7},{2,0},{3,1},{4,2},{5,3},{6,4},{7,5},{8,14},{9,15},{10,... | collective-permute-start | bytes 786440 | tf_op jit(solution)/shard_map/ppermute | solution.py:127
  154.2 17.5 %collective-permute-start.18 = (f32[2,512,128]{2,1,0:T(8,128)S(1)}, f32[2,512,128]{2,1,0:T(8,128)S(1)}, u32[]{:S(2)}, u32[]{:S(2)}) collective-permute-start(f32[2,512,128]{2,1,0:T(8,128)S(1)} %collective-permute-done.11.refs_3_), channel_id=1, source_target_pairs={{0,2},{1,3},{2,4},{3,5},{4,6},{5,7},{6,0},{7,1},{8,10},{9,11},{10,... | collective-permute-start | bytes 1572872 | tf_op jit(solution)/shard_map/ppermute | solution.py:127
  154.2 17.5 %collective-permute-start.19 = (f32[2,512,128]{2,1,0:T(8,128)S(1)}, f32[2,512,128]{2,1,0:T(8,128)}, u32[]{:S(2)}, u32[]{:S(2)}) collective-permute-start(f32[2,512,128]{2,1,0:T(8,128)S(1)} %collective-permute-done.11.refs_3_), channel_id=1, source_target_pairs={{0,6},{1,7},{2,0},{3,1},{4,2},{5,3},{6,4},{7,5},{8,14},{9,15},{10,... | collective-permute-start | bytes 1572872 | tf_op jit(solution)/shard_map/ppermute | solution.py:127
  161.4 12.2 %collective-permute-start.20 = (f32[2,512,128]{2,1,0:T(8,128)S(1)}, f32[2,512,128]{2,1,0:T(8,128)}, u32[]{:S(2)}, u32[]{:S(2)}) collective-permute-start(f32[2,512,128]{2,1,0:T(8,128)S(1)} %constant_dynamic-update-slice_fusion.4.refs_4_), channel_id=1, source_target_pairs={{0,1},{1,0},{2,3},{3,2},{4,5},{5,4},{6,7},{7,6},{8,9},{9,8},{10,11... | collective-permute-start | bytes 1572872 | tf_op jit(solution)/shard_map/ppermute | solution.py:127
  181.2 13.3 %all-to-all-start.2 = ((f32[32,2,128]{2,1,0:T(2,128)}), f32[32,2,128]{2,1,0:T(2,128)S(1)}, u32[]{:S(2)}, u32[]{:S(2)}) async-start(f32[32,2,128]{2,1,0:T(2,128)} %reshape.190), calls=%async_computation.2 | async-start | bytes 65536 | tf_op jit(solution)/shard_map/all_to_all | solution.py:380

commit v5 on v4

--- a/solution.py
+++ b/solution.py
@@ -148,28 +148,28 @@
 
 
 def pick_kernel(place_ref, *refs):
-    arrays, out_ref, sems = refs[:-2], refs[-2], refs[-1]
+    arrays, outs, sems = refs[:-3], refs[-3:-1], refs[-1]
     parts = [array.at[j] for array in arrays for j in range(array.shape[0])]
-    for number in range(out_ref.shape[0]):
+    for number, out_ref in enumerate(outs):
         for order, part in enumerate(parts):
 
             @pl.when(place_ref[number] == order)
             def _():
-                pltpu.make_async_copy(part, out_ref.at[number], sems.at[number]).start()
-
-    for number in range(out_ref.shape[0]):
-        pltpu.make_async_copy(parts[0], out_ref.at[number], sems.at[number]).wait()
+                pltpu.make_async_copy(part, out_ref, sems.at[number]).start()
+
+    for number, out_ref in enumerate(outs):
+        pltpu.make_async_copy(parts[0], out_ref, sems.at[number]).wait()
 
 
 def pick(place, arrays):
-    count = place.shape[0]
+    shape = jax.ShapeDtypeStruct(arrays[0].shape[1:], jnp.float32)
     return pl.pallas_call(
         pick_kernel,
-        out_shape=jax.ShapeDtypeStruct((count,) + arrays[0].shape[1:], jnp.float32),
+        out_shape=[shape, shape],
         in_specs=[pl.BlockSpec(memory_space=pltpu.SMEM)]
         + [pl.BlockSpec(memory_space=pl.ANY)] * len(arrays),
-        out_specs=pl.BlockSpec(memory_space=pltpu.VMEM),
-        scratch_shapes=[pltpu.SemaphoreType.DMA((count,))],
+        out_specs=[pl.BlockSpec(memory_space=pltpu.VMEM)] * 2,
+        scratch_shapes=[pltpu.SemaphoreType.DMA((2,))],
         compiler_params=pltpu.CompilerParams(vmem_limit_bytes=VMEM_BYTES),
         name="pick_occ",
     )(place, *arrays)

time: 198 us -> 199 us (level)
    unnamed x41 -> x43, local copies, waits for them, and re-layouts: 14.3 us -> 15.2 us
  transfers between devices with their start and end apart: 23 -> 23, of which waited for: 11 -> 11; matrix products, arithmetic and copies ran while one was open for 9% -> 9% of each run, Pallas kernels for 14% -> 15%
where the time goes in v5:
time: 199 us; the launch traced here: 196 us
  waiting for transfers between devices  63.8 us (32%)
  starting transfers between devices  43.6 us (22%)
  Pallas kernels  35.5 us (18%)
  local copies, waits for them, and re-layouts  23.3 us (12%)
  blocking collectives  20.7 us (10%)
  between operations  6.59 us (3%)
  other arithmetic  2.75 us (1%)
    ppermute x16, waiting for transfers between devices, shift_col(): return lax.ppermute(value, 'col', pairs)  48.5 us
    ppermute x16, starting transfers between devices, shift_col(): return lax.ppermute(value, 'col', pairs)  27 us
    all_to_all x1, blocking collectives, on_device(): lax.all_to_all(columns, 'row', split_axis=0, concat_axis=0, tiled=True)  20.7 us
    pallas_call x2, Pallas kernels, contract(): pl.pallas_call(contract_kernel, grid=(tiles,), in_specs=[pl.BlockSpec((1,...  15.2 us
    unnamed x43, local copies, waits for them, and re-layouts  15.2 us
    pallas_call x1, Pallas kernels, form_densities(): pl.pallas_call(form_kernel, grid_spec=pltpu.PrefetchScalarGridSpec(num_sc...  10.6 us
    all_to_all x1, starting transfers between devices, on_device(): lax.all_to_all(field, 'row', split_axis=0, concat_axis=0, tiled=True)  9.94 us
    all_to_all x1, waiting for transfers between devices, on_device(): lax.all_to_all(sent.reshape(2 * row_count, 2, pair_count * blocks // 2),...  7.12 us
  transfers between devices with their start and end apart: 23, of which 11 were waited for; matrix products, arithmetic and copies ran while one was open for 9% of the time, Pallas kernels for 15%

profile of v5, /device:TPU:2, one launch (start us, length us, event | category | flops | bytes accessed | tf_op | source)
XLA Modules:
  0.0 196.2 jit_solution(74179988856391924)
XLA Ops:
  0.0 2.1 %collective-permute-start = (f32[2,1024,128]{2,1,0:T(8,128)}, f32[2,1024,128]{2,1,0:T(8,128)}, u32[]{:S(2)}, u32[]{:S(2)}) collective-permute-start(f32[2,1024,128]{2,1,0:T(8,128)} %bitcast.44), channel_id=1, source_target_pairs={{0,1},{1,0},{2,3},{3,2},{4,5},{5,4},{6,7},{7,6},{8,9},{9,8},{10,11... | collective-permute-start | bytes 3145736 | tf_op jit(solution)/shard_map/ppermute | solution.py:127
  2.1 1.6 collective-permute-start.1
  3.7 1.7 collective-permute-start.2
  5.4 0.5 collective-permute-start.15
  5.9 1.3 fusion.8
  9.5 0.8 subtract_bitcast_fusion.1
  10.8 0.8 constant_dynamic-slice_fusion.1
  11.6 0.5 fusion.7
  12.8 0.6 slice.50
  13.5 1.3 and_select_fusion.5
  14.9 0.2 fusion.1
  15.1 11.6 %collective-permute-done.refs_3_ = f32[2,1024,128]{2,1,0:T(8,128)} collective-permute-done((f32[2,1024,128]{2,1,0:T(8,128)}, f32[2,1024,128]{2,1,0:T(8,128)}, u32[]{:S(2)}, u32[]{:S(2)}) %collective-permute-start) | collective-permute-done | bytes 1048608 | tf_op jit(solution)/shard_map/ppermute | solution.py:127
  26.7 1.5 collective-permute-done.1.refs_1_
  28.3 1.6 collective-permute-start.4
  30.0 1.7 collective-permute-start.5
  31.7 0.4 collective-permute-start.6
  32.1 2.9 %collective-permute-start.7 = (f32[2,1024,128]{2,1,0:T(8,128)}, f32[2,1024,128]{2,1,0:T(8,128)S(1)}, u32[]{:S(2)}, u32[]{:S(2)}) collective-permute-start(f32[2,1024,128]{2,1,0:T(8,128)} %collective-permute-done.refs_3_), channel_id=1, source_target_pairs={{0,6},{1,7},{2,0},{3,1},{4,2},{5,3},{6,4},{7,5},{8,14},{9,15},{10,... | collective-permute-start | bytes 3145736 | tf_op jit(solution)/shard_map/ppermute | solution.py:127
  35.0 9.5 %collective-permute-done.4 = f32[1,1024,128]{2,1,0:T(8,128)S(1)} collective-permute-done((f32[1,1024,128]{2,1,0:T(8,128)S(1)}, f32[1,1024,128]{2,1,0:T(8,128)S(1)}, u32[]{:S(2)}, u32[]{:S(2)}) %collective-permute-start.4) | collective-permute-done | bytes 524320 | tf_op jit(solution)/shard_map/ppermute | solution.py:127
  44.5 0.4 collective-permute-done.5
  45.0 1.5 collective-permute-start.8
  46.5 18.2 %collective-permute-done.6.refs_5_ = f32[2,1024,128]{2,1,0:T(8,128)S(1)} collective-permute-done((f32[2,1024,128]{2,1,0:T(8,128)}, f32[2,1024,128]{2,1,0:T(8,128)S(1)}, u32[]{:S(2)}, u32[]{:S(2)}) %collective-permute-start.6) | collective-permute-done | bytes 1048608 | tf_op jit(solution)/shard_map/ppermute | solution.py:127
  64.6 2.1 %collective-permute-done.8.refs_7_ = f32[2,1024,128]{2,1,0:T(8,128)S(1)} collective-permute-done((f32[2,1024,128]{2,1,0:T(8,128)S(1)}, f32[2,1024,128]{2,1,0:T(8,128)S(1)}, u32[]{:S(2)}, u32[]{:S(2)}) %collective-permute-start.8) | collective-permute-done | bytes 1048608 | tf_op jit(solution)/shard_map/ppermute | solution.py:127
  66.8 1.0 copy-done.12
  67.8 2.6 %pick_occ.1 = (f32[1024,128]{1,0:T(8,128)S(1)}, f32[1024,128]{1,0:T(8,128)}) custom-call(s32[2]{0:T(128)S(1)} %fusion.2.place_ref, f32[2,1024,128]{2,1,0:T(8,128)S(1)} %bitcast.47, f32[2,1024,128]{2,1,0:T(8,128)S(1)} %collective-permute-done.1.refs_1_, f32[2,1024,128]{2,1,0:T(8,128)S(1)} %collective-permute-done.2.refs_2_, ...), custom_call_target="tpu_custom_call" | custom-call | tf_op jit(solution)/shard_map/pick_occ/pallas_call | solution.py:166
  70.4 0.8 copy-done.2
  74.1 1.0 copy-done.3
  75.1 2.9 %forward.1 = (f32[8,128,128]{2,1,0:T(8,128)S(1)}, f32[128,8,128]{2,1,0:T(8,128)S(1)}) custom-call(s32[1]{0:T(128)} %bitcast.12.flag_ref, s32[1]{0:T(128)} %bitcast.14.vir_place, f32[1024,128]{1,0:T(8,128)S(1)} %copy-done.3, f32[1024,128]{1,0:T(8,128)} %collective-permute-done.9.mate_occ, f32[16,8,128,128]{3,2,1,0:T(8,128)} %vir_ref.1, f32[128,128]{1,0:T(8,128)S(1)} %copy-done.1), custom_call_target="tpu_custom_call" | custom-call | tf_op jit(solution)/shard_map/forward/pallas_call | solution.py:39
  78.1 0.8 copy-done.5
  78.8 0.8 copy-done.7
  79.6 9.9 %all-to-all-start = ((f32[128,8,128]{2,1,0:T(8,128)}), f32[128,8,128]{2,1,0:T(8,128)}, u32[]{:S(2)}, u32[]{:S(2)}) async-start(f32[128,8,128]{2,1,0:T(8,128)} %copy-done.7), calls=%async_computation | async-start | bytes 1048576 | tf_op jit(solution)/shard_map/all_to_all | solution.py:350
  89.6 1.0 dynamic-slice_dynamic-update-slice_fusion.7
  90.6 1.1 dynamic-slice_dynamic-update-slice_fusion.6
  91.7 1.0 dynamic-slice_dynamic-update-slice_fusion.5
  92.7 2.2 %dynamic-slice_dynamic-update-slice_fusion.4 = (f32[16,512,128]{2,1,0:T(8,128)}, f32[16,512,128]{2,1,0:T(8,128)}) fusion(f32[16,512,128]{2,1,0:T(8,128)} %get-tuple-element.55, f32[2,1024,128]{2,1,0:T(8,128)} %collective-permute-done.refs_3_, s32[]{:T(128)S(6)} %select_n.198, f32[16,512,128]{2,1,0:T(8,128)} %get-tuple-element.56, s32[]{:T(128)S(6)} %select_n.197), kind=kLoop, calls=%fused_computation.4 | loop fusion | bytes 2097160
  95.0 1.1 dynamic-slice_dynamic-update-slice_fusion.3
  96.0 1.0 dynamic-slice_dynamic-update-slice_fusion.2
  97.0 1.0 dynamic-slice_dynamic-update-slice_fusion.1
  98.1 6.7 %all-to-all-done = f32[128,8,128]{2,1,0:T(8,128)} async-done(((f32[128,8,128]{2,1,0:T(8,128)}), f32[128,8,128]{2,1,0:T(8,128)}, u32[]{:S(2)}, u32[]{:S(2)}) %all-to-all-start) | async-done | bytes 524320 | tf_op jit(solution)/shard_map/all_to_all | solution.py:350
  104.7 2.2 %filter_columns.1 = f32[16,8,8,128]{3,2,1,0:T(8,128)S(1)} custom-call(s32[1]{0:T(128)} %bitcast.9.first_ref, f32[16,8,8,128]{3,2,1,0:T(8,128)} %bitcast.23.in_ref, f32[128,128]{1,0:T(8,128)S(1)} %copy-done.1), custom_call_target="tpu_custom_call" | custom-call | tf_op jit(solution)/shard_map/filter_columns/pallas_call | solution.py:79
  107.0 2.3 %dynamic-slice_dynamic-update-slice_fusion = (f32[16,512,128]{2,1,0:T(8,128)}, f32[16,512,128]{2,1,0:T(8,128)}) fusion(f32[16,512,128]{2,1,0:T(8,128)} %get-tuple-element.47, f32[2,1024,128]{2,1,0:T(8,128)} %copy-done.12, s32[]{:T(128)S(6)} %select_n.198, f32[16,512,128]{2,1,0:T(8,128)} %get-tuple-element.48, s32[]{:T(128)S(6)} %select_n.197), kind=kLoop, calls=%fused_computation | loop fusion | bytes 2097160 | tf_op jit(solution)/shard_map/concatenate | solution.py:360
  109.2 20.7 %all_to_all.15 = f32[16,8,8,128]{3,2,1,0:T(8,128)S(1)} all-to-all(f32[16,8,8,128]{3,2,1,0:T(8,128)S(1)} %filter_columns.1), channel_id=1, replica_groups=mesh['grp'=2,'row'=16,'col'=8] {'row'}, dimensions={0} | all-to-all | bytes 1048576 | tf_op jit(solution)/shard_map/all_to_all | solution.py:366
  129.9 1.9 back.1
  132.0 1.5 collective-permute-done.10
  133.5 1.6 collective-permute-start.11
  135.1 0.3 collective-permute-start.12
  135.4 2.9 %collective-permute-start.13 = (f32[2,512,128]{2,1,0:T(8,128)S(1)}, f32[2,512,128]{2,1,0:T(8,128)S(1)}, u32[]{:S(2)}, u32[]{:S(2)}) collective-permute-start(f32[2,512,128]{2,1,0:T(8,128)S(1)} %constant_dynamic-update-slice_fusion.2.refs_0_), channel_id=1, source_target_pairs={{0,6},{1,7},{2,0},{3,1},{4,2},{5,3},{6,4},{7,5},{8,14},{9,15},{10,... | collective-permute-start | bytes 1572872 | tf_op jit(solution)/shard_map/ppermute | solution.py:127
  138.3 2.0 %copy-done.15 = f32[16,512,128]{2,1,0:T(8,128)} copy-done((f32[16,512,128]{2,1,0:T(8,128)}, f32[16,512,128]{2,1,0:T(8,128)S(1)}, u32[]{:S(2)}) %copy-start.15) | copy-done | bytes 4194328
  140.4 10.6 %form_densities.1.density_ref = f32[4,32,128,128]{3,2,1,0:T(8,128)} custom-call(s32[32]{0:T(128)S(1)} %get-tuple-element.34.occ_index, s32[32]{0:T(128)S(1)} %get-tuple-element.35.vir_index, s32[1]{0:T(128)} %bitcast.8.half_ref.half, f32[16,512,128]{2,1,0:T(8,128)} %get-tuple-element.46.own_occ, f32[16,512,128]{2,1,0:T(8,128)} %copy-done.15, ...), custom_call_target="tpu_custom_call" | custom-call | flops 2097152 | bytes 25165824 | tf_op jit(solution)/shard_map/form_densities/pallas_call | solution.py:260
  151.1 3.3 %collective-permute-start.17 = (f32[1,512,128]{2,1,0:T(8,128)S(1)}, f32[1,512,128]{2,1,0:T(8,128)S(1)}, u32[]{:S(2)}, u32[]{:S(2)}) collective-permute-start(f32[1,512,128]{2,1,0:T(8,128)S(1)} %slice.58), channel_id=1, source_target_pairs={{0,6},{1,7},{2,0},{3,1},{4,2},{5,3},{6,4},{7,5},{8,14},{9,15},{10,... | collective-permute-start | bytes 786440 | tf_op jit(solution)/shard_map/ppermute | solution.py:127
  154.4 3.2 %collective-permute-start.19 = (f32[2,512,128]{2,1,0:T(8,128)S(1)}, f32[2,512,128]{2,1,0:T(8,128)}, u32[]{:S(2)}, u32[]{:S(2)}) collective-permute-start(f32[2,512,128]{2,1,0:T(8,128)S(1)} %collective-permute-done.11.refs_3_), channel_id=1, source_target_pairs={{0,6},{1,7},{2,0},{3,1},{4,2},{5,3},{6,4},{7,5},{8,14},{9,15},{10,... | collective-permute-start | bytes 1572872 | tf_op jit(solution)/shard_map/ppermute | solution.py:127
  157.7 3.9 %collective-permute-done.16 = f32[1,512,128]{2,1,0:T(8,128)S(1)} collective-permute-done((f32[1,512,128]{2,1,0:T(8,128)S(1)}, f32[1,512,128]{2,1,0:T(8,128)S(1)}, u32[]{:S(2)}, u32[]{:S(2)}) %collective-permute-start.16) | collective-permute-done | bytes 262176 | tf_op jit(solution)/shard_map/ppermute | solution.py:127
  161.6 2.1 %collective-permute-start.20 = (f32[2,512,128]{2,1,0:T(8,128)S(1)}, f32[2,512,128]{2,1,0:T(8,128)}, u32[]{:S(2)}, u32[]{:S(2)}) collective-permute-start(f32[2,512,128]{2,1,0:T(8,128)S(1)} %constant_dynamic-update-slice_fusion.4.refs_4_), channel_id=1, source_target_pairs={{0,1},{1,0},{2,3},{3,2},{4,5},{5,4},{6,7},{7,6},{8,9},{9,8},{10,11... | collective-permute-start | bytes 1572872 | tf_op jit(solution)/shard_map/ppermute | solution.py:127
  163.7 8.6 %contract.2 = f32[8,320]{1,0:T(8,128)S(1)} custom-call(f32[4,32,128,128]{3,2,1,0:T(8,128)} %form_densities.1.density_ref, f32[2,512,128]{2,1,0:T(8,128)S(1)} %constant_dynamic-update-slice_fusion.2.refs_0_, f32[2,512,128]{2,1,0:T(8,128)S(1)} %collective-permute-done.12.refs_1_, f32[2,512,128]{2,1,0:T(8,128)S(1)} %collective-permute-done.13.refs_2_, ...), custom_call_target="tpu_custom_call" | custom-call | flops 41943040 | bytes 10485760 | tf_op jit(solution)/shard_map/contract/pallas_call | solution.py:285
  172.3 0.1 reshape_squeeze.6
  172.5 1.3 collective-permute-done.20.refs_2_
  173.8 6.7 %contract.3 = f32[8,192]{1,0:T(8,128)S(1)} custom-call(f32[4,32,128,128]{3,2,1,0:T(8,128)} %form_densities.1.density_ref, f32[2,512,128]{2,1,0:T(8,128)S(1)} %collective-permute-done.18.refs_0_, f32[2,512,128]{2,1,0:T(8,128)} %collective-permute-done.19.refs_1_, f32[2,512,128]{2,1,0:T(8,128)} %collective-permute-done.20.refs_2_), custom_call_target="tpu_custom_call" | custom-call | flops 25165824 | bytes 10485760 | tf_op jit(solution)/shard_map/contract/pallas_call | solution.py:285
  180.7 0.7 reshape.190
  181.5 6.0 %all-to-all-start.2 = ((f32[32,2,128]{2,1,0:T(2,128)}), f32[32,2,128]{2,1,0:T(2,128)S(1)}, u32[]{:S(2)}, u32[]{:S(2)}) async-start(f32[32,2,128]{2,1,0:T(2,128)} %reshape.190), calls=%async_computation.2 | async-start | bytes 65536 | tf_op jit(solution)/shard_map/all_to_all | solution.py:380
  187.6 7.1 %all-to-all-done.2 = f32[32,2,128]{2,1,0:T(2,128)S(1)} async-done(((f32[32,2,128]{2,1,0:T(2,128)}), f32[32,2,128]{2,1,0:T(2,128)S(1)}, u32[]{:S(2)}, u32[]{:S(2)}) %all-to-all-start.2) | async-done | bytes 32800 | tf_op jit(solution)/shard_map/all_to_all | solution.py:380
  194.7 0.1 copy.29
  194.9 0.2 fusion.6
  195.1 0.2 copy.27
  195.3 0.2 copy.26
  195.5 0.7 copy.28
  (72 shorter events, 1.5 us)
Async XLA Ops:
  0.0 67.8 %copy-start = (f32[2,8,128,128]{3,2,1,0:T(8,128)S(1)}, f32[2,8,128,128]{3,2,1,0:T(8,128)}, u32[]{:S(2)}) copy-start(f32[2,8,128,128]{3,2,1,0:T(8,128)} %param.6) | copy-start | bytes 3145732
  0.0 26.7 %collective-permute-start = (f32[2,1024,128]{2,1,0:T(8,128)}, f32[2,1024,128]{2,1,0:T(8,128)}, u32[]{:S(2)}, u32[]{:S(2)}) collective-permute-start(f32[2,1024,128]{2,1,0:T(8,128)} %bitcast.44), channel_id=1, source_target_pairs={{0,1},{1,0},{2,3},{3,2},{4,5},{5,4},{6,7},{7,6},{8,9},{9,8},{10,11... | collective-permute-start | bytes 3145736 | tf_op jit(solution)/shard_map/ppermute | solution.py:127
  2.1 26.1 %collective-permute-start.1 = (f32[2,1024,128]{2,1,0:T(8,128)}, f32[2,1024,128]{2,1,0:T(8,128)S(1)}, u32[]{:S(2)}, u32[]{:S(2)}) collective-permute-start(f32[2,1024,128]{2,1,0:T(8,128)} %bitcast.45), channel_id=1, source_target_pairs={{0,2},{1,3},{2,4},{3,5},{4,6},{5,7},{6,0},{7,1},{8,10},{9,11},{10,... | collective-permute-start | bytes 3145736 | tf_op jit(solution)/shard_map/ppermute | solution.py:127
  3.7 24.6 %collective-permute-start.2 = (f32[2,1024,128]{2,1,0:T(8,128)}, f32[2,1024,128]{2,1,0:T(8,128)S(1)}, u32[]{:S(2)}, u32[]{:S(2)}) collective-permute-start(f32[2,1024,128]{2,1,0:T(8,128)} %bitcast.46), channel_id=1, source_target_pairs={{0,6},{1,7},{2,0},{3,1},{4,2},{5,3},{6,4},{7,5},{8,14},{9,15},{10,... | collective-permute-start | bytes 3145736 | tf_op jit(solution)/shard_map/ppermute | solution.py:127
  5.4 7.4 %collective-permute-start.3 = (s32[16,2]{0,1:T(2,128)}, s32[16,2]{0,1:T(2,128)S(1)}, u32[]{:S(2)}, u32[]{:S(2)}) collective-permute-start(s32[16,2]{0,1:T(2,128)} %param.9), channel_id=1, source_target_pairs={{0,128},{128,0},{1,129},{129,1},{2,130},{130,2},{3,131},{131,3},{4... | collective-permute-start | bytes 392 | tf_op jit(solution)/shard_map/ppermute | solution.py:147
  5.4 133.0 %collective-permute-start.15 = (f32[16,2,512,128]{3,2,1,0:T(8,128)}, f32[16,2,512,128]{3,2,1,0:T(8,128)}, u32[]{:S(2)}, u32[]{:S(2)}) collective-permute-start(f32[16,2,512,128]{3,2,1,0:T(8,128)} %bitcast.50), channel_id=1, source_target_pairs={{0,128},{128,0},{1,129},{129,1},{2,130},{130,2},{3,131},{131,3},{4... | collective-permute-start | bytes 25165832 | tf_op jit(solution)/shard_map/ppermute | solution.py:147
  28.3 16.1 %collective-permute-start.4 = (f32[1,1024,128]{2,1,0:T(8,128)S(1)}, f32[1,1024,128]{2,1,0:T(8,128)S(1)}, u32[]{:S(2)}, u32[]{:S(2)}) collective-permute-start(f32[1,1024,128]{2,1,0:T(8,128)S(1)} %slice.55), channel_id=1, source_target_pairs={{0,2},{1,3},{2,4},{3,5},{4,6},{5,7},{6,0},{7,1},{8,10},{9,11},{10,... | collective-permute-start | bytes 1572872 | tf_op jit(solution)/shard_map/ppermute | solution.py:127
  30.0 14.9 %collective-permute-start.5 = (f32[1,1024,128]{2,1,0:T(8,128)S(1)}, f32[1,1024,128]{2,1,0:T(8,128)S(1)}, u32[]{:S(2)}, u32[]{:S(2)}) collective-permute-start(f32[1,1024,128]{2,1,0:T(8,128)S(1)} %slice.56), channel_id=1, source_target_pairs={{0,6},{1,7},{2,0},{3,1},{4,2},{5,3},{6,4},{7,5},{8,14},{9,15},{10,... | collective-permute-start | bytes 1572872 | tf_op jit(solution)/shard_map/ppermute | solution.py:127
  31.7 32.9 %collective-permute-start.6 = (f32[2,1024,128]{2,1,0:T(8,128)}, f32[2,1024,128]{2,1,0:T(8,128)S(1)}, u32[]{:S(2)}, u32[]{:S(2)}) collective-permute-start(f32[2,1024,128]{2,1,0:T(8,128)} %collective-permute-done.refs_3_), channel_id=1, source_target_pairs={{0,2},{1,3},{2,4},{3,5},{4,6},{5,7},{6,0},{7,1},{8,10},{9,11},{10,... | collective-permute-start | bytes 3145736 | tf_op jit(solution)/shard_map/ppermute | solution.py:127
  32.1 32.6 %collective-permute-start.7 = (f32[2,1024,128]{2,1,0:T(8,128)}, f32[2,1024,128]{2,1,0:T(8,128)S(1)}, u32[]{:S(2)}, u32[]{:S(2)}) collective-permute-start(f32[2,1024,128]{2,1,0:T(8,128)} %collective-permute-done.refs_3_), channel_id=1, source_target_pairs={{0,6},{1,7},{2,0},{3,1},{4,2},{5,3},{6,4},{7,5},{8,14},{9,15},{10,... | collective-permute-start | bytes 3145736 | tf_op jit(solution)/shard_map/ppermute | solution.py:127
  45.0 21.8 %copy-start.8 = (f32[2,1024,128]{2,1,0:T(8,128)}, f32[2,1024,128]{2,1,0:T(8,128)S(1)}, u32[]{:S(2)}) copy-start(f32[2,1024,128]{2,1,0:T(8,128)S(1)} %constant_dynamic-update-slice_fusion.refs_4_) | copy-start | bytes 3145732
  45.0 29.1 %copy-start.1 = (f32[128,128]{1,0:T(8,128)S(1)}, f32[128,128]{1,0:T(8,128)}, u32[]{:S(2)}) copy-start(f32[128,128]{1,0:T(8,128)} %constant.191.clone.cas_ref) | copy-start | bytes 196612
  45.0 21.8 %collective-permute-start.8 = (f32[2,1024,128]{2,1,0:T(8,128)S(1)}, f32[2,1024,128]{2,1,0:T(8,128)S(1)}, u32[]{:S(2)}, u32[]{:S(2)}) collective-permute-start(f32[2,1024,128]{2,1,0:T(8,128)S(1)} %constant_dynamic-update-slice_fusion.refs_4_), channel_id=1, source_target_pairs={{0,1},{1,0},{2,3},{3,2},{4,5},{5,4},{6,7},{7,6},{8,9},{9,8},{10,11... | collective-permute-start | bytes 3145736 | tf_op jit(solution)/shard_map/ppermute | solution.py:127
  64.6 2.1 %copy-start.13 = (f32[2,1024,128]{2,1,0:T(8,128)}, f32[2,1024,128]{2,1,0:T(8,128)S(1)}, u32[]{:S(2)}) copy-start(f32[2,1024,128]{2,1,0:T(8,128)S(1)} %collective-permute-done.6.refs_5_) | copy-start | bytes 3145732
  64.6 2.1 %copy-start.10 = (f32[2,1024,128]{2,1,0:T(8,128)}, f32[2,1024,128]{2,1,0:T(8,128)S(1)}, u32[]{:S(2)}) copy-start(f32[2,1024,128]{2,1,0:T(8,128)S(1)} %collective-permute-done.7.refs_6_) | copy-start | bytes 3145732
  66.8 1.0 copy-start.12
  70.4 0.8 copy-start.2
  71.2 2.9 %collective-permute-start.9 = (f32[1024,128]{1,0:T(8,128)}, f32[1024,128]{1,0:T(8,128)}, u32[]{:S(2)}, u32[]{:S(2)}) collective-permute-start(f32[1024,128]{1,0:T(8,128)} %get-tuple-element.28), channel_id=1, source_target_pairs={{0,128},{128,0},{1,129},{129,1},{2,130},{130,2},{3,131},{131,3},{4... | collective-permute-start | bytes 1572872 | tf_op jit(solution)/shard_map/ppermute | solution.py:147
  74.1 1.0 copy-start.3
  78.0 0.8 copy-start.5
  78.8 0.8 copy-start.7
  79.6 25.1 %all-to-all-start = ((f32[128,8,128]{2,1,0:T(8,128)}), f32[128,8,128]{2,1,0:T(8,128)}, u32[]{:S(2)}, u32[]{:S(2)}) async-start(f32[128,8,128]{2,1,0:T(8,128)} %copy-done.7), calls=%async_computation | async-start | bytes 1048576 | tf_op jit(solution)/shard_map/all_to_all | solution.py:350
  89.6 5.4 %copy-start.9 = (f32[2,1024,128]{2,1,0:T(8,128)S(1)}, f32[2,1024,128]{2,1,0:T(8,128)}, u32[]{:S(2)}) copy-start(f32[2,1024,128]{2,1,0:T(8,128)} %copy-done.8) | copy-start | bytes 3145732
  90.6 5.4 %copy-start.14 = (f32[2,1024,128]{2,1,0:T(8,128)S(1)}, f32[2,1024,128]{2,1,0:T(8,128)}, u32[]{:S(2)}) copy-start(f32[2,1024,128]{2,1,0:T(8,128)} %copy-done.13) | copy-start | bytes 3145732
  91.7 5.4 %copy-start.11 = (f32[2,1024,128]{2,1,0:T(8,128)S(1)}, f32[2,1024,128]{2,1,0:T(8,128)}, u32[]{:S(2)}) copy-start(f32[2,1024,128]{2,1,0:T(8,128)} %copy-done.10) | copy-start | bytes 3145732
  96.0 33.9 %copy-start.4 = (f32[8,128,128]{2,1,0:T(8,128)S(1)}, f32[8,128,128]{2,1,0:T(8,128)}, u32[]{:S(2)}) copy-start(f32[8,128,128]{2,1,0:T(8,128)} %xc_ref.1) | copy-start | bytes 1572868
  96.0 33.9 %copy-start.6 = (f32[8,128,128]{2,1,0:T(8,128)S(1)}, f32[8,128,128]{2,1,0:T(8,128)}, u32[]{:S(2)}) copy-start(f32[8,128,128]{2,1,0:T(8,128)} %copy-done.5) | copy-start | bytes 1572868
  109.2 29.1 %collective-permute-start.14 = (f32[16,512,128]{2,1,0:T(8,128)}, f32[16,512,128]{2,1,0:T(8,128)S(1)}, u32[]{:S(2)}, u32[]{:S(2)}) collective-permute-start(f32[16,512,128]{2,1,0:T(8,128)} %get-tuple-element.45), channel_id=1, source_target_pairs={{0,128},{128,0},{1,129},{129,1},{2,130},{130,2},{3,131},{131,3},{4... | collective-permute-start | bytes 12582920 | tf_op jit(solution)/shard_map/ppermute | solution.py:147
  131.8 1.6 collective-permute-start.10
  133.5 17.5 %collective-permute-start.11 = (f32[2,512,128]{2,1,0:T(8,128)S(1)}, f32[2,512,128]{2,1,0:T(8,128)S(1)}, u32[]{:S(2)}, u32[]{:S(2)}) collective-permute-start(f32[2,512,128]{2,1,0:T(8,128)S(1)} %constant_dynamic-update-slice_fusion.2.refs_0_), channel_id=1, source_target_pairs={{0,1},{1,0},{2,3},{3,2},{4,5},{5,4},{6,7},{7,6},{8,9},{9,8},{10,11... | collective-permute-start | bytes 1572872 | tf_op jit(solution)/shard_map/ppermute | solution.py:127
  135.1 15.9 %collective-permute-start.12 = (f32[2,512,128]{2,1,0:T(8,128)S(1)}, f32[2,512,128]{2,1,0:T(8,128)S(1)}, u32[]{:S(2)}, u32[]{:S(2)}) collective-permute-start(f32[2,512,128]{2,1,0:T(8,128)S(1)} %constant_dynamic-update-slice_fusion.2.refs_0_), channel_id=1, source_target_pairs={{0,2},{1,3},{2,4},{3,5},{4,6},{5,7},{6,0},{7,1},{8,10},{9,11},{10,... | collective-permute-start | bytes 1572872 | tf_op jit(solution)/shard_map/ppermute | solution.py:127
  135.4 15.6 %collective-permute-start.13 = (f32[2,512,128]{2,1,0:T(8,128)S(1)}, f32[2,512,128]{2,1,0:T(8,128)S(1)}, u32[]{:S(2)}, u32[]{:S(2)}) collective-permute-start(f32[2,512,128]{2,1,0:T(8,128)S(1)} %constant_dynamic-update-slice_fusion.2.refs_0_), channel_id=1, source_target_pairs={{0,6},{1,7},{2,0},{3,1},{4,2},{5,3},{6,4},{7,5},{8,14},{9,15},{10,... | collective-permute-start | bytes 1572872 | tf_op jit(solution)/shard_map/ppermute | solution.py:127
  138.3 2.0 %copy-start.15 = (f32[16,512,128]{2,1,0:T(8,128)}, f32[16,512,128]{2,1,0:T(8,128)S(1)}, u32[]{:S(2)}) copy-start(f32[16,512,128]{2,1,0:T(8,128)S(1)} %collective-permute-done.14.mate_occ) | copy-start | bytes 12582916
  151.0 10.5 %collective-permute-start.16 = (f32[1,512,128]{2,1,0:T(8,128)S(1)}, f32[1,512,128]{2,1,0:T(8,128)S(1)}, u32[]{:S(2)}, u32[]{:S(2)}) collective-permute-start(f32[1,512,128]{2,1,0:T(8,128)S(1)} %slice.57), channel_id=1, source_target_pairs={{0,2},{1,3},{2,4},{3,5},{4,6},{5,7},{6,0},{7,1},{8,10},{9,11},{10,... | collective-permute-start | bytes 786440 | tf_op jit(solution)/shard_map/ppermute | solution.py:127
  151.1 10.4 %collective-permute-start.17 = (f32[1,512,128]{2,1,0:T(8,128)S(1)}, f32[1,512,128]{2,1,0:T(8,128)S(1)}, u32[]{:S(2)}, u32[]{:S(2)}) collective-permute-start(f32[1,512,128]{2,1,0:T(8,128)S(1)} %slice.58), channel_id=1, source_target_pairs={{0,6},{1,7},{2,0},{3,1},{4,2},{5,3},{6,4},{7,5},{8,14},{9,15},{10,... | collective-permute-start | bytes 786440 | tf_op jit(solution)/shard_map/ppermute | solution.py:127
  154.4 18.0 %collective-permute-start.18 = (f32[2,512,128]{2,1,0:T(8,128)S(1)}, f32[2,512,128]{2,1,0:T(8,128)S(1)}, u32[]{:S(2)}, u32[]{:S(2)}) collective-permute-start(f32[2,512,128]{2,1,0:T(8,128)S(1)} %collective-permute-done.11.refs_3_), channel_id=1, source_target_pairs={{0,2},{1,3},{2,4},{3,5},{4,6},{5,7},{6,0},{7,1},{8,10},{9,11},{10,... | collective-permute-start | bytes 1572872 | tf_op jit(solution)/shard_map/ppermute | solution.py:127
  154.4 18.0 %collective-permute-start.19 = (f32[2,512,128]{2,1,0:T(8,128)S(1)}, f32[2,512,128]{2,1,0:T(8,128)}, u32[]{:S(2)}, u32[]{:S(2)}) collective-permute-start(f32[2,512,128]{2,1,0:T(8,128)S(1)} %collective-permute-done.11.refs_3_), channel_id=1, source_target_pairs={{0,6},{1,7},{2,0},{3,1},{4,2},{5,3},{6,4},{7,5},{8,14},{9,15},{10,... | collective-permute-start | bytes 1572872 | tf_op jit(solution)/shard_map/ppermute | solution.py:127
  161.6 12.2 %collective-permute-start.20 = (f32[2,512,128]{2,1,0:T(8,128)S(1)}, f32[2,512,128]{2,1,0:T(8,128)}, u32[]{:S(2)}, u32[]{:S(2)}) collective-permute-start(f32[2,512,128]{2,1,0:T(8,128)S(1)} %constant_dynamic-update-slice_fusion.4.refs_4_), channel_id=1, source_target_pairs={{0,1},{1,0},{2,3},{3,2},{4,5},{5,4},{6,7},{7,6},{8,9},{9,8},{10,11... | collective-permute-start | bytes 1572872 | tf_op jit(solution)/shard_map/ppermute | solution.py:127
  181.5 13.2 %all-to-all-start.2 = ((f32[32,2,128]{2,1,0:T(2,128)}), f32[32,2,128]{2,1,0:T(2,128)S(1)}, u32[]{:S(2)}, u32[]{:S(2)}) async-start(f32[32,2,128]{2,1,0:T(2,128)} %reshape.190), calls=%async_computation.2 | async-start | bytes 65536 | tf_op jit(solution)/shard_map/all_to_all | solution.py:380
